TPU v7x, 768 devices: a whole 4x8x12 slice. The times are simulated.
768 devices in a mesh: lat: 128 (over x, z_hi, y, core), section: 6 (over z_lo).
Axes of the slice: x: 4, y: 8, z: 12 (z_hi: 2, z_lo: 6; z = z_hi * 6 + z_lo), core: 2. Of those that a mesh axis runs over, the one named last changes fastest.
Arguments:
- trajectory: bfloat16 [6, 2, 1024, 8, 768], P('section', None, 'lat'), may hold values from -8 to 8
- observed: bfloat16 [6, 2, 1024, 8, 768], P('section', None, 'lat'), may hold values from -6 to 6
- obs_mask: int32 [6, 1024, 8], P('section', 'lat'), may hold values 0 or 1
- shift_rows: int32 [6], P('section'), may hold values from 0 to 7
- final_adjoint: float32 [2, 1024, 8, 768], P(None, 'lat'), may hold values from -6 to 6
- w_query: bfloat16 [6, 768, 384], P('section'), may hold values from -0.21875 to 0.21875
- w_key: bfloat16 [6, 768, 384], P('section'), may hold values from -0.21875 to 0.21875
- w_value: bfloat16 [6, 768, 384], P('section'), may hold values from -0.21875 to 0.21875
- w_out: bfloat16 [6, 384, 768], P('section'), may hold values from -0.3125 to 0.3125
Outputs:
- adjoint_field: float32 [6, 2, 1024, 8, 768], P('section', None, 'lat')
All inputs are finite; a program needn't handle non-finite values. No bound on the sum of `obs_mask` on one device may be relied on, other than what follows from the above.
Results may differ from a plain program's by a relative error of at most 0.015.
Values may be sent and summed in bfloat16 or wider, within the bound.
No kernel may reach another device: no remote copies, remote signals or barrier semaphores. Data moves between devices by JAX's collectives and lax.ppermute only.
A program may use at most 64 MiB of HBM per device.

v0:
```python
import jax
import jax.numpy as jnp
from jax import lax
from jax.sharding import PartitionSpec as P

HD = 32
WIN = 8


def passed_along(shard, axis, by):
    size = lax.axis_size(axis)
    pairs = [(i, i + by) for i in range(size) if 0 <= i + by < size]
    return lax.ppermute(shard, axis, pairs)


def extended(block, sides, width):
    for axis, dim in sides:
        count = lax.axis_size(axis)
        forward = [(i, i + 1) for i in range(count - 1)]
        backward = [(target, source) for source, target in forward]
        low = lax.ppermute(
            lax.slice_in_dim(block, block.shape[dim] - width, None, axis=dim), axis, forward
        )
        high = lax.ppermute(lax.slice_in_dim(block, 0, width, axis=dim), axis, backward)
        block = jnp.concatenate([low, block, high], axis=dim)
    return block


def to_windows(field):
    count, across, width = field.shape
    split = field.reshape(count // WIN, WIN, across // WIN, WIN, width)
    return split.transpose(0, 2, 1, 3, 4).reshape(-1, WIN * WIN, width)


def from_windows(tiles, count, across):
    width = tiles.shape[-1]
    split = tiles.reshape(count // WIN, across // WIN, WIN, WIN, width)
    return split.transpose(0, 2, 1, 3, 4).reshape(count, across, width)


def window_adjoint(tiles, grad_tiles, key_valid, w_query, w_key, w_value, w_out):
    flt = jnp.float32
    count, tokens, width = tiles.shape
    hidden = w_query.shape[1]
    head_count = hidden // HD
    scale = HD ** (-0.5)
    queries = (
        jnp.einsum("wtd,de->wte", tiles, w_query, preferred_element_type=flt) * scale
    ).astype(jnp.bfloat16)
    key_rows = jnp.einsum("wtd,de->wte", tiles, w_key, preferred_element_type=flt).astype(
        jnp.bfloat16
    )
    value_rows = jnp.einsum("wtd,de->wte", tiles, w_value, preferred_element_type=flt).astype(
        jnp.bfloat16
    )
    heads_q = queries.reshape(count, tokens, head_count, HD)
    heads_k = key_rows.reshape(count, tokens, head_count, HD)
    heads_v = value_rows.reshape(count, tokens, head_count, HD)
    scores = jnp.einsum("wihe,wjhe->whij", heads_q, heads_k, preferred_element_type=flt)
    scores = jnp.where(key_valid[:, None, None, :], scores, -1000000000.0)
    scores = scores - jnp.max(scores, axis=-1, keepdims=True)
    expon = jnp.exp(scores)
    attend = expon / jnp.sum(expon, axis=-1, keepdims=True)
    attend_b = attend.astype(jnp.bfloat16)
    grad_out = jnp.einsum("wid,ed->wie", grad_tiles, w_out, preferred_element_type=flt).astype(
        jnp.bfloat16
    )
    heads_g = grad_out.reshape(count, tokens, head_count, HD)
    grad_probs = jnp.einsum("wihe,wjhe->whij", heads_g, heads_v, preferred_element_type=flt)
    grad_scores = attend * (grad_probs - jnp.sum(attend * grad_probs, axis=-1, keepdims=True))
    grad_scores = grad_scores.astype(jnp.bfloat16)
    grad_query = (
        jnp.einsum("whij,wjhe->wihe", grad_scores, heads_k, preferred_element_type=flt) * scale
    ).astype(jnp.bfloat16)
    grad_key = jnp.einsum("whij,wihe->wjhe", grad_scores, heads_q, preferred_element_type=flt)
    grad_value = jnp.einsum("whij,wihe->wjhe", attend_b, heads_g, preferred_element_type=flt)
    change_q = jnp.einsum(
        "wie,de->wid",
        grad_query.reshape(count, tokens, hidden),
        w_query,
        preferred_element_type=flt,
    )
    grad_both = jnp.concatenate(
        [grad_key.reshape(count, tokens, hidden), grad_value.reshape(count, tokens, hidden)],
        axis=-1,
    )
    w_both = jnp.concatenate([w_key, w_value], axis=1).astype(flt)
    change_kv = jnp.einsum("wje,de->wjd", grad_both, w_both, precision=lax.Precision.HIGHEST)
    return change_q + change_kv


def band_adjoint(banded, grad_band, valid_rows, offset, w_query, w_key, w_value, w_out):
    total_rows, across, width = banded.shape
    span = 2 * (total_rows // 3)
    x_span = lax.dynamic_slice_in_dim(banded, offset, span, 0)
    g_span = lax.dynamic_slice_in_dim(grad_band, offset, span, 0)
    v_span = lax.dynamic_slice_in_dim(valid_rows, offset, span, 0)
    valid_grid = jnp.broadcast_to(v_span[:, None, None], (span, across, 1))
    key_valid = to_windows(valid_grid)[:, :, 0]
    tiles = window_adjoint(
        to_windows(x_span), to_windows(g_span), key_valid, w_query, w_key, w_value, w_out
    )
    change_span = from_windows(tiles, span, across)
    return lax.dynamic_update_slice_in_dim(
        jnp.zeros((total_rows, across, width), jnp.float32), change_span, offset, 0
    )


def chain_body(
    trajectory, observed, obs_mask, shift_rows, final_adjoint, w_query, w_key, w_value, w_out
):
    sections = lax.axis_size("section")
    section_at = lax.axis_index("section")
    band_at = lax.axis_index("lat")
    bands_all = lax.axis_size("lat")
    members = trajectory.shape[1]
    rows_here = trajectory.shape[2]
    across = trajectory.shape[3]
    width = trajectory.shape[4]
    states = trajectory[0]
    targets = observed[0]
    obs_weight = obs_mask[0].astype(jnp.float32)[:, :, None]
    offset = shift_rows[0]
    query_w = w_query[0]
    key_w = w_key[0]
    value_w = w_value[0]
    out_w = w_out[0]
    global_rows = band_at * rows_here + jnp.arange(3 * rows_here, dtype=jnp.int32) - rows_here
    valid_rows = (global_rows >= 0) & (global_rows < bands_all * rows_here)
    ticks = members + sections - 1

    def advance(step_at, carry):
        passed, result = carry
        member = step_at - (sections - 1 - section_at)
        active = (member >= 0) & (member < members)
        member_at = jnp.clip(member, 0, members - 1)
        incoming = passed_along(passed, "section", -1)
        final_here = lax.dynamic_index_in_dim(final_adjoint, member_at, 0, keepdims=False)
        adjoint = incoming + jnp.where(
            section_at == sections - 1, final_here, jnp.zeros_like(final_here)
        )
        own_band = lax.dynamic_index_in_dim(states, member_at, 0, keepdims=False)
        banded = extended(own_band, (("lat", 0),), rows_here)
        grad_here = adjoint.astype(jnp.bfloat16)
        blank = jnp.zeros_like(grad_here)
        grad_band = jnp.concatenate([blank, grad_here, blank], axis=0)
        change = lax.cond(
            active,
            lambda: band_adjoint(
                banded, grad_band, valid_rows, offset, query_w, key_w, value_w, out_w
            ),
            lambda: jnp.zeros((3 * rows_here, across, width), jnp.float32),
        )
        packed = jnp.concatenate([change[:rows_here], change[2 * rows_here :]], axis=0)
        received = extended(packed, (("lat", 0),), rows_here)
        own_change = (
            change[rows_here : 2 * rows_here] + received[:rows_here] + received[3 * rows_here :]
        )
        target_here = lax.dynamic_index_in_dim(targets, member_at, 0, keepdims=False)
        forcing = obs_weight * (own_band.astype(jnp.float32) - target_here.astype(jnp.float32))
        updated = adjoint + own_change + forcing
        stored = lax.dynamic_update_index_in_dim(result, updated, member_at, 0)
        result = jnp.where(active, stored, result)
        return (updated, result)

    start = (
        jnp.zeros((rows_here, across, width), jnp.float32),
        jnp.zeros((members, rows_here, across, width), jnp.float32),
    )
    final_carry = lax.fori_loop(0, ticks, advance, start)
    return final_carry[1][None]


def on_device(
    trajectory, observed, obs_mask, shift_rows, final_adjoint, w_query, w_key, w_value, w_out
):
    outcome = chain_body(
        trajectory, observed, obs_mask, shift_rows, final_adjoint, w_query, w_key, w_value, w_out
    )
    return outcome


def solution(mesh):
    placed = (
        P("section", None, "lat", None, None),
        P("section", None, "lat", None, None),
        P("section", "lat", None),
        P("section"),
        P(None, "lat", None, None),
        P("section", None, None),
        P("section", None, None),
        P("section", None, None),
        P("section", None, None),
    )
    return jax.shard_map(
        on_device,
        mesh=mesh,
        in_specs=placed,
        out_specs=P("section", None, "lat", None, None),
        check_vma=False,
    )
```

profile of v0, /device:TPU:6, one launch (start us, length us, event | category | flops | bytes accessed | tf_op | source)
XLA Modules:
  0.0 442.6 jit_solution(1584617229439441100)
XLA Ops:
  2.1 440.5 %while.18 = (s32[]{:T(128)}, f32[8,8,768]{2,1,0:T(8,128)}, f32[2,8,8,768]{3,2,1,0:T(8,128)}, pred[]{:T(512)}, s32[]{:T(128)}, /*index=5*/f32[2,8,8,768]{3,2,1,0:...) while((s32[]{:T(128)}, f32[8,8,768]{2,1,0:T(8,128)}, ...), condition=%wide.region_6.7_spmd.clone, body=%wide.region_0.6_spmd.clone.sunk | while | flops 1326809344 | bytes 36806780 | solution.py:170
  3.0 17.7 %collective-permute-start = (bf16[8,8,768]{2,1,0:T(8,128)(2,1)S(1)}, bf16[8,8,768]{2,1,0:T(8,128)(2,1)S(1)}, u32[]{:S(2)}, u32[]{:S(2)}) collective-permute-start(bf16[8,8,768]{2,1,0:T(8,128)(2,1)S(1)} %dynamic-slice_bitcast_fusion.2), channel_id=1, source_target_pairs={{6,0},{12,6},{18,12},{24,18},{30,24},{36,30},{42,36},{48,42},{54,4... | collective-permute-start | bytes 294920 | tf_op jit(solution)/shard_map/while/body/eval_jaxpr/ppermute | solution.py:24
  20.7 1.9 collective-permute-start.1
  24.2 12.0 %collective-permute-done.1 = bf16[8,8,768]{2,1,0:T(8,128)(2,1)S(1)} collective-permute-done((bf16[8,8,768]{2,1,0:T(8,128)(2,1)S(1)}, bf16[8,8,768]{2,1,0:T(8,128)(2,1)S(1)}, u32[]{:S(2)}, u32[]{:S(2)}) %collective-permute-start.1) | collective-permute-done | bytes 98336 | tf_op jit(solution)/shard_map/while/body/eval_jaxpr/ppermute | solution.py:21
  38.4 8.1 %collective-permute-start.3 = (f32[8,8,768]{2,1,0:T(8,128)S(1)}, f32[8,8,768]{2,1,0:T(8,128)S(1)}, u32[]{:S(2)}, u32[]{:S(2)}) collective-permute-start(f32[8,8,768]{2,1,0:T(8,128)S(1)} %get-tuple-element.575), channel_id=1, source_target_pairs={{6,0},{12,6},{18,12},{24,18},{30,24},{36,30},{42,36},{48,42},{54,4... | collective-permute-start | bytes 589832 | tf_op jit(solution)/shard_map/while/body/eval_jaxpr/ppermute | solution.py:24
  46.5 1.9 collective-permute-start.4
  49.7 13.3 %collective-permute-done.4 = f32[8,8,768]{2,1,0:T(8,128)S(1)} collective-permute-done((f32[8,8,768]{2,1,0:T(8,128)S(1)}, f32[8,8,768]{2,1,0:T(8,128)S(1)}, u32[]{:S(2)}, u32[]{:S(2)}) %collective-permute-start.4) | collective-permute-done | bytes 196640 | tf_op jit(solution)/shard_map/while/body/eval_jaxpr/ppermute | solution.py:21
  65.8 1.9 collective-permute-start
  67.7 2.4 collective-permute-start.1
  72.5 10.5 %collective-permute-done.1 = bf16[8,8,768]{2,1,0:T(8,128)(2,1)S(1)} collective-permute-done((bf16[8,8,768]{2,1,0:T(8,128)(2,1)S(1)}, bf16[8,8,768]{2,1,0:T(8,128)(2,1)S(1)}, u32[]{:S(2)}, u32[]{:S(2)}) %collective-permute-start.1) | collective-permute-done | bytes 98336 | tf_op jit(solution)/shard_map/while/body/eval_jaxpr/ppermute | solution.py:21
  85.1 9.0 %collective-permute-start.3 = (f32[8,8,768]{2,1,0:T(8,128)S(1)}, f32[8,8,768]{2,1,0:T(8,128)S(1)}, u32[]{:S(2)}, u32[]{:S(2)}) collective-permute-start(f32[8,8,768]{2,1,0:T(8,128)S(1)} %get-tuple-element.575), channel_id=1, source_target_pairs={{6,0},{12,6},{18,12},{24,18},{30,24},{36,30},{42,36},{48,42},{54,4... | collective-permute-start | bytes 589832 | tf_op jit(solution)/shard_map/while/body/eval_jaxpr/ppermute | solution.py:24
  94.2 1.9 collective-permute-start.4
  97.3 13.2 %collective-permute-done.4 = f32[8,8,768]{2,1,0:T(8,128)S(1)} collective-permute-done((f32[8,8,768]{2,1,0:T(8,128)S(1)}, f32[8,8,768]{2,1,0:T(8,128)S(1)}, u32[]{:S(2)}, u32[]{:S(2)}) %collective-permute-start.4) | collective-permute-done | bytes 196640 | tf_op jit(solution)/shard_map/while/body/eval_jaxpr/ppermute | solution.py:21
  113.4 1.9 collective-permute-start
  115.3 2.4 collective-permute-start.1
  120.1 10.5 %collective-permute-done.1 = bf16[8,8,768]{2,1,0:T(8,128)(2,1)S(1)} collective-permute-done((bf16[8,8,768]{2,1,0:T(8,128)(2,1)S(1)}, bf16[8,8,768]{2,1,0:T(8,128)(2,1)S(1)}, u32[]{:S(2)}, u32[]{:S(2)}) %collective-permute-start.1) | collective-permute-done | bytes 98336 | tf_op jit(solution)/shard_map/while/body/eval_jaxpr/ppermute | solution.py:21
  133.4 11.1 %collective-permute-start.3 = (f32[8,8,768]{2,1,0:T(8,128)S(1)}, f32[8,8,768]{2,1,0:T(8,128)S(1)}, u32[]{:S(2)}, u32[]{:S(2)}) collective-permute-start(f32[8,8,768]{2,1,0:T(8,128)S(1)} %get-tuple-element.575), channel_id=1, source_target_pairs={{6,0},{12,6},{18,12},{24,18},{30,24},{36,30},{42,36},{48,42},{54,4... | collective-permute-start | bytes 589832 | tf_op jit(solution)/shard_map/while/body/eval_jaxpr/ppermute | solution.py:24
  144.5 1.9 collective-permute-start.4
  147.7 13.2 %collective-permute-done.4 = f32[8,8,768]{2,1,0:T(8,128)S(1)} collective-permute-done((f32[8,8,768]{2,1,0:T(8,128)S(1)}, f32[8,8,768]{2,1,0:T(8,128)S(1)}, u32[]{:S(2)}, u32[]{:S(2)}) %collective-permute-start.4) | collective-permute-done | bytes 196640 | tf_op jit(solution)/shard_map/while/body/eval_jaxpr/ppermute | solution.py:21
  163.7 1.9 collective-permute-start
  165.7 2.4 collective-permute-start.1
  170.5 10.5 %collective-permute-done.1 = bf16[8,8,768]{2,1,0:T(8,128)(2,1)S(1)} collective-permute-done((bf16[8,8,768]{2,1,0:T(8,128)(2,1)S(1)}, bf16[8,8,768]{2,1,0:T(8,128)(2,1)S(1)}, u32[]{:S(2)}, u32[]{:S(2)}) %collective-permute-start.1) | collective-permute-done | bytes 98336 | tf_op jit(solution)/shard_map/while/body/eval_jaxpr/ppermute | solution.py:21
  183.2 8.2 %collective-permute-start.3 = (f32[8,8,768]{2,1,0:T(8,128)S(1)}, f32[8,8,768]{2,1,0:T(8,128)S(1)}, u32[]{:S(2)}, u32[]{:S(2)}) collective-permute-start(f32[8,8,768]{2,1,0:T(8,128)S(1)} %get-tuple-element.575), channel_id=1, source_target_pairs={{6,0},{12,6},{18,12},{24,18},{30,24},{36,30},{42,36},{48,42},{54,4... | collective-permute-start | bytes 589832 | tf_op jit(solution)/shard_map/while/body/eval_jaxpr/ppermute | solution.py:24
  191.4 1.9 collective-permute-start.4
  193.3 2.3 collective-permute-done.3
  195.6 12.9 %collective-permute-done.4 = f32[8,8,768]{2,1,0:T(8,128)S(1)} collective-permute-done((f32[8,8,768]{2,1,0:T(8,128)S(1)}, f32[8,8,768]{2,1,0:T(8,128)S(1)}, u32[]{:S(2)}, u32[]{:S(2)}) %collective-permute-start.4) | collective-permute-done | bytes 196640 | tf_op jit(solution)/shard_map/while/body/eval_jaxpr/ppermute | solution.py:21
  211.4 1.9 collective-permute-start
  213.3 2.4 collective-permute-start.1
  218.1 10.5 %collective-permute-done.1 = bf16[8,8,768]{2,1,0:T(8,128)(2,1)S(1)} collective-permute-done((bf16[8,8,768]{2,1,0:T(8,128)(2,1)S(1)}, bf16[8,8,768]{2,1,0:T(8,128)(2,1)S(1)}, u32[]{:S(2)}, u32[]{:S(2)}) %collective-permute-start.1) | collective-permute-done | bytes 98336 | tf_op jit(solution)/shard_map/while/body/eval_jaxpr/ppermute | solution.py:21
  230.7 7.3 %collective-permute-start.3 = (f32[8,8,768]{2,1,0:T(8,128)S(1)}, f32[8,8,768]{2,1,0:T(8,128)S(1)}, u32[]{:S(2)}, u32[]{:S(2)}) collective-permute-start(f32[8,8,768]{2,1,0:T(8,128)S(1)} %get-tuple-element.575), channel_id=1, source_target_pairs={{6,0},{12,6},{18,12},{24,18},{30,24},{36,30},{42,36},{48,42},{54,4... | collective-permute-start | bytes 589832 | tf_op jit(solution)/shard_map/while/body/eval_jaxpr/ppermute | solution.py:24
  238.0 1.9 collective-permute-start.4
  241.2 13.1 %collective-permute-done.4 = f32[8,8,768]{2,1,0:T(8,128)S(1)} collective-permute-done((f32[8,8,768]{2,1,0:T(8,128)S(1)}, f32[8,8,768]{2,1,0:T(8,128)S(1)}, u32[]{:S(2)}, u32[]{:S(2)}) %collective-permute-start.4) | collective-permute-done | bytes 196640 | tf_op jit(solution)/shard_map/while/body/eval_jaxpr/ppermute | solution.py:21
  257.2 1.9 collective-permute-start
  259.1 2.4 collective-permute-start.1
  263.9 10.5 %collective-permute-done.1 = bf16[8,8,768]{2,1,0:T(8,128)(2,1)S(1)} collective-permute-done((bf16[8,8,768]{2,1,0:T(8,128)(2,1)S(1)}, bf16[8,8,768]{2,1,0:T(8,128)(2,1)S(1)}, u32[]{:S(2)}, u32[]{:S(2)}) %collective-permute-start.1) | collective-permute-done | bytes 98336 | tf_op jit(solution)/shard_map/while/body/eval_jaxpr/ppermute | solution.py:21
  274.4 60.2 %collective-permute-done.2 = f32[8,8,768]{2,1,0:T(8,128)S(1)} collective-permute-done((f32[8,8,768]{2,1,0:T(8,128)S(1)}, f32[8,8,768]{2,1,0:T(8,128)S(1)}, u32[]{:S(2)}, u32[]{:S(2)}) %collective-permute-start.2) | collective-permute-done | bytes 196640 | tf_op jit(solution)/shard_map/while/body/eval_jaxpr/ppermute | solution.py:13
  334.7 15.9 %conditional.3 = (f32[24,8,768]{2,1,0:T(8,128)}) conditional(s32[]{:T(128)} %convert_element_type.106, () %tuple.60, (s32[]{:T(128)}, bf16[24,8,768]{2,1,0:T(8,128)(2,1)S(1)}, bf16[768,384]{1,0:T(8,128)(2,1)S(1)}, s32[24]{0:T(128)S(1)}, bf16[768,384]{1,0:T(8,128)(2,1)S(1)}, /*index=5*/bf16[24,8,768]{2,1,0:T(8,128)(2,1)S(1)}, ...), branch_computations={%region_1.1_spmd, %region_2.5_spmd.clone} | conditional | flops 1325482240 | bytes 17045022 | solution.py:147
  339.5 2.0 convolution_convert_fusion
  351.7 10.8 %collective-permute-start.3 = (f32[8,8,768]{2,1,0:T(8,128)S(1)}, f32[8,8,768]{2,1,0:T(8,128)S(1)}, u32[]{:S(2)}, u32[]{:S(2)}) collective-permute-start(f32[8,8,768]{2,1,0:T(8,128)S(1)} %get-tuple-element.575), channel_id=1, source_target_pairs={{6,0},{12,6},{18,12},{24,18},{30,24},{36,30},{42,36},{48,42},{54,4... | collective-permute-start | bytes 589832 | tf_op jit(solution)/shard_map/while/body/eval_jaxpr/ppermute | solution.py:24
  362.5 1.9 collective-permute-start.4
  365.7 13.1 %collective-permute-done.4 = f32[8,8,768]{2,1,0:T(8,128)S(1)} collective-permute-done((f32[8,8,768]{2,1,0:T(8,128)S(1)}, f32[8,8,768]{2,1,0:T(8,128)S(1)}, u32[]{:S(2)}, u32[]{:S(2)}) %collective-permute-start.4) | collective-permute-done | bytes 196640 | tf_op jit(solution)/shard_map/while/body/eval_jaxpr/ppermute | solution.py:21
  383.6 2.4 collective-permute-start.1
  388.4 10.5 %collective-permute-done.1 = bf16[8,8,768]{2,1,0:T(8,128)(2,1)S(1)} collective-permute-done((bf16[8,8,768]{2,1,0:T(8,128)(2,1)S(1)}, bf16[8,8,768]{2,1,0:T(8,128)(2,1)S(1)}, u32[]{:S(2)}, u32[]{:S(2)}) %collective-permute-start.1) | collective-permute-done | bytes 98336 | tf_op jit(solution)/shard_map/while/body/eval_jaxpr/ppermute | solution.py:21
  399.0 15.9 %conditional.3 = (f32[24,8,768]{2,1,0:T(8,128)}) conditional(s32[]{:T(128)} %convert_element_type.106, () %tuple.60, (s32[]{:T(128)}, bf16[24,8,768]{2,1,0:T(8,128)(2,1)S(1)}, bf16[768,384]{1,0:T(8,128)(2,1)S(1)}, s32[24]{0:T(128)S(1)}, bf16[768,384]{1,0:T(8,128)(2,1)S(1)}, /*index=5*/bf16[24,8,768]{2,1,0:T(8,128)(2,1)S(1)}, ...), branch_computations={%region_1.1_spmd, %region_2.5_spmd.clone} | conditional | flops 1325482240 | bytes 17045022 | solution.py:147
  403.8 2.0 convolution_convert_fusion
  416.0 8.3 %collective-permute-start.3 = (f32[8,8,768]{2,1,0:T(8,128)S(1)}, f32[8,8,768]{2,1,0:T(8,128)S(1)}, u32[]{:S(2)}, u32[]{:S(2)}) collective-permute-start(f32[8,8,768]{2,1,0:T(8,128)S(1)} %get-tuple-element.575), channel_id=1, source_target_pairs={{6,0},{12,6},{18,12},{24,18},{30,24},{36,30},{42,36},{48,42},{54,4... | collective-permute-start | bytes 589832 | tf_op jit(solution)/shard_map/while/body/eval_jaxpr/ppermute | solution.py:24
  424.4 1.9 collective-permute-start.4
  427.5 13.1 %collective-permute-done.4 = f32[8,8,768]{2,1,0:T(8,128)S(1)} collective-permute-done((f32[8,8,768]{2,1,0:T(8,128)S(1)}, f32[8,8,768]{2,1,0:T(8,128)S(1)}, u32[]{:S(2)}, u32[]{:S(2)}) %collective-permute-start.4) | collective-permute-done | bytes 196640 | tf_op jit(solution)/shard_map/while/body/eval_jaxpr/ppermute | solution.py:21
  (273 shorter events, 88.1 us)
Async XLA Ops:
  2.1 34.2 %copy-start.4 = (f32[2,8,8,768]{3,2,1,0:T(8,128)S(1)}, f32[2,8,8,768]{3,2,1,0:T(8,128)}, u32[]{:S(2)}) copy-start(f32[2,8,8,768]{3,2,1,0:T(8,128)} %get-tuple-element.622) | copy-start | bytes 1179652 | tf_op jit(solution)/shard_map/while
  3.0 21.2 %collective-permute-start = (bf16[8,8,768]{2,1,0:T(8,128)(2,1)S(1)}, bf16[8,8,768]{2,1,0:T(8,128)(2,1)S(1)}, u32[]{:S(2)}, u32[]{:S(2)}) collective-permute-start(bf16[8,8,768]{2,1,0:T(8,128)(2,1)S(1)} %dynamic-slice_bitcast_fusion.2), channel_id=1, source_target_pairs={{6,0},{12,6},{18,12},{24,18},{30,24},{36,30},{42,36},{48,42},{54,4... | collective-permute-start | bytes 294920 | tf_op jit(solution)/shard_map/while/body/eval_jaxpr/ppermute | solution.py:24
  20.7 15.5 %collective-permute-start.1 = (bf16[8,8,768]{2,1,0:T(8,128)(2,1)S(1)}, bf16[8,8,768]{2,1,0:T(8,128)(2,1)S(1)}, u32[]{:S(2)}, u32[]{:S(2)}) collective-permute-start(bf16[8,8,768]{2,1,0:T(8,128)(2,1)S(1)} %dynamic-slice_bitcast_fusion.2), channel_id=1, source_target_pairs={{0,6},{6,12},{12,18},{18,24},{24,30},{30,36},{36,42},{42,48},{48,5... | collective-permute-start | bytes 294920 | tf_op jit(solution)/shard_map/while/body/eval_jaxpr/ppermute | solution.py:21
  22.7 13.5 %collective-permute-start.2 = (f32[8,8,768]{2,1,0:T(8,128)S(1)}, f32[8,8,768]{2,1,0:T(8,128)S(1)}, u32[]{:S(2)}, u32[]{:S(2)}) collective-permute-start(f32[8,8,768]{2,1,0:T(8,128)S(1)} %broadcast_select_fusion.2), channel_id=1, source_target_pairs={{1,0},{2,1},{3,2},{4,3},{5,4},{7,6},{8,7},{9,8},{10,9},{11,10},{13... | collective-permute-start | bytes 589832 | tf_op jit(solution)/shard_map/while/body/eval_jaxpr/ppermute | solution.py:13
  38.4 11.3 %collective-permute-start.3 = (f32[8,8,768]{2,1,0:T(8,128)S(1)}, f32[8,8,768]{2,1,0:T(8,128)S(1)}, u32[]{:S(2)}, u32[]{:S(2)}) collective-permute-start(f32[8,8,768]{2,1,0:T(8,128)S(1)} %get-tuple-element.575), channel_id=1, source_target_pairs={{6,0},{12,6},{18,12},{24,18},{30,24},{36,30},{42,36},{48,42},{54,4... | collective-permute-start | bytes 589832 | tf_op jit(solution)/shard_map/while/body/eval_jaxpr/ppermute | solution.py:24
  46.5 16.4 %collective-permute-start.4 = (f32[8,8,768]{2,1,0:T(8,128)S(1)}, f32[8,8,768]{2,1,0:T(8,128)S(1)}, u32[]{:S(2)}, u32[]{:S(2)}) collective-permute-start(f32[8,8,768]{2,1,0:T(8,128)S(1)} %get-tuple-element.576), channel_id=1, source_target_pairs={{0,6},{6,12},{12,18},{18,24},{24,30},{30,36},{36,42},{42,48},{48,5... | collective-permute-start | bytes 589832 | tf_op jit(solution)/shard_map/while/body/eval_jaxpr/ppermute | solution.py:21
  65.8 6.7 %collective-permute-start = (bf16[8,8,768]{2,1,0:T(8,128)(2,1)S(1)}, bf16[8,8,768]{2,1,0:T(8,128)(2,1)S(1)}, u32[]{:S(2)}, u32[]{:S(2)}) collective-permute-start(bf16[8,8,768]{2,1,0:T(8,128)(2,1)S(1)} %dynamic-slice_bitcast_fusion.2), channel_id=1, source_target_pairs={{6,0},{12,6},{18,12},{24,18},{30,24},{36,30},{42,36},{48,42},{54,4... | collective-permute-start | bytes 294920 | tf_op jit(solution)/shard_map/while/body/eval_jaxpr/ppermute | solution.py:24
  67.7 15.3 %collective-permute-start.1 = (bf16[8,8,768]{2,1,0:T(8,128)(2,1)S(1)}, bf16[8,8,768]{2,1,0:T(8,128)(2,1)S(1)}, u32[]{:S(2)}, u32[]{:S(2)}) collective-permute-start(bf16[8,8,768]{2,1,0:T(8,128)(2,1)S(1)} %dynamic-slice_bitcast_fusion.2), channel_id=1, source_target_pairs={{0,6},{6,12},{12,18},{18,24},{24,30},{30,36},{36,42},{42,48},{48,5... | collective-permute-start | bytes 294920 | tf_op jit(solution)/shard_map/while/body/eval_jaxpr/ppermute | solution.py:21
  71.2 11.9 %collective-permute-start.2 = (f32[8,8,768]{2,1,0:T(8,128)S(1)}, f32[8,8,768]{2,1,0:T(8,128)S(1)}, u32[]{:S(2)}, u32[]{:S(2)}) collective-permute-start(f32[8,8,768]{2,1,0:T(8,128)S(1)} %broadcast_select_fusion.2), channel_id=1, source_target_pairs={{1,0},{2,1},{3,2},{4,3},{5,4},{7,6},{8,7},{9,8},{10,9},{11,10},{13... | collective-permute-start | bytes 589832 | tf_op jit(solution)/shard_map/while/body/eval_jaxpr/ppermute | solution.py:13
  85.1 12.2 %collective-permute-start.3 = (f32[8,8,768]{2,1,0:T(8,128)S(1)}, f32[8,8,768]{2,1,0:T(8,128)S(1)}, u32[]{:S(2)}, u32[]{:S(2)}) collective-permute-start(f32[8,8,768]{2,1,0:T(8,128)S(1)} %get-tuple-element.575), channel_id=1, source_target_pairs={{6,0},{12,6},{18,12},{24,18},{30,24},{36,30},{42,36},{48,42},{54,4... | collective-permute-start | bytes 589832 | tf_op jit(solution)/shard_map/while/body/eval_jaxpr/ppermute | solution.py:24
  94.2 16.4 %collective-permute-start.4 = (f32[8,8,768]{2,1,0:T(8,128)S(1)}, f32[8,8,768]{2,1,0:T(8,128)S(1)}, u32[]{:S(2)}, u32[]{:S(2)}) collective-permute-start(f32[8,8,768]{2,1,0:T(8,128)S(1)} %get-tuple-element.576), channel_id=1, source_target_pairs={{0,6},{6,12},{12,18},{18,24},{24,30},{30,36},{36,42},{42,48},{48,5... | collective-permute-start | bytes 589832 | tf_op jit(solution)/shard_map/while/body/eval_jaxpr/ppermute | solution.py:21
  113.4 6.7 %collective-permute-start = (bf16[8,8,768]{2,1,0:T(8,128)(2,1)S(1)}, bf16[8,8,768]{2,1,0:T(8,128)(2,1)S(1)}, u32[]{:S(2)}, u32[]{:S(2)}) collective-permute-start(bf16[8,8,768]{2,1,0:T(8,128)(2,1)S(1)} %dynamic-slice_bitcast_fusion.2), channel_id=1, source_target_pairs={{6,0},{12,6},{18,12},{24,18},{30,24},{36,30},{42,36},{48,42},{54,4... | collective-permute-start | bytes 294920 | tf_op jit(solution)/shard_map/while/body/eval_jaxpr/ppermute | solution.py:24
  115.3 15.3 %collective-permute-start.1 = (bf16[8,8,768]{2,1,0:T(8,128)(2,1)S(1)}, bf16[8,8,768]{2,1,0:T(8,128)(2,1)S(1)}, u32[]{:S(2)}, u32[]{:S(2)}) collective-permute-start(bf16[8,8,768]{2,1,0:T(8,128)(2,1)S(1)} %dynamic-slice_bitcast_fusion.2), channel_id=1, source_target_pairs={{0,6},{6,12},{12,18},{18,24},{24,30},{30,36},{36,42},{42,48},{48,5... | collective-permute-start | bytes 294920 | tf_op jit(solution)/shard_map/while/body/eval_jaxpr/ppermute | solution.py:21
  118.8 12.5 %collective-permute-start.2 = (f32[8,8,768]{2,1,0:T(8,128)S(1)}, f32[8,8,768]{2,1,0:T(8,128)S(1)}, u32[]{:S(2)}, u32[]{:S(2)}) collective-permute-start(f32[8,8,768]{2,1,0:T(8,128)S(1)} %broadcast_select_fusion.2), channel_id=1, source_target_pairs={{1,0},{2,1},{3,2},{4,3},{5,4},{7,6},{8,7},{9,8},{10,9},{11,10},{13... | collective-permute-start | bytes 589832 | tf_op jit(solution)/shard_map/while/body/eval_jaxpr/ppermute | solution.py:13
  132.2 28.7 %copy-start.5 = (f32[2,8,8,768]{3,2,1,0:T(8,128)S(1)}, f32[2,8,8,768]{3,2,1,0:T(8,128)}, u32[]{:S(2)}) copy-start(f32[2,8,8,768]{3,2,1,0:T(8,128)} %get-tuple-element.622) | copy-start | bytes 1179652 | tf_op jit(solution)/shard_map/while
  132.2 28.7 %copy-start.6 = (bf16[2,8,8,768]{3,2,1,0:T(8,128)(2,1)S(1)}, bf16[2,8,8,768]{3,2,1,0:T(8,128)(2,1)}, u32[]{:S(2)}) copy-start(bf16[2,8,8,768]{3,2,1,0:T(8,128)(2,1)} %get-tuple-element.623) | copy-start | bytes 589828 | tf_op jit(solution)/shard_map/while
  132.2 28.7 %copy-start.7 = (bf16[2,8,8,768]{3,2,1,0:T(8,128)(2,1)S(1)}, bf16[2,8,8,768]{3,2,1,0:T(8,128)(2,1)}, u32[]{:S(2)}) copy-start(bf16[2,8,8,768]{3,2,1,0:T(8,128)(2,1)} %get-tuple-element.630) | copy-start | bytes 589828 | tf_op jit(solution)/shard_map/while
  132.2 28.7 %copy-start.8 = (f32[8,8,1]{1,0,2:T(8,128)S(1)}, f32[8,8,1]{1,0,2:T(8,128)}, u32[]{:S(2)}) copy-start(f32[8,8,1]{1,0,2:T(8,128)} %get-tuple-element.629) | copy-start | bytes 772 | tf_op jit(solution)/shard_map/while
  133.4 14.3 %collective-permute-start.3 = (f32[8,8,768]{2,1,0:T(8,128)S(1)}, f32[8,8,768]{2,1,0:T(8,128)S(1)}, u32[]{:S(2)}, u32[]{:S(2)}) collective-permute-start(f32[8,8,768]{2,1,0:T(8,128)S(1)} %get-tuple-element.575), channel_id=1, source_target_pairs={{6,0},{12,6},{18,12},{24,18},{30,24},{36,30},{42,36},{48,42},{54,4... | collective-permute-start | bytes 589832 | tf_op jit(solution)/shard_map/while/body/eval_jaxpr/ppermute | solution.py:24
  144.5 16.4 %collective-permute-start.4 = (f32[8,8,768]{2,1,0:T(8,128)S(1)}, f32[8,8,768]{2,1,0:T(8,128)S(1)}, u32[]{:S(2)}, u32[]{:S(2)}) collective-permute-start(f32[8,8,768]{2,1,0:T(8,128)S(1)} %get-tuple-element.576), channel_id=1, source_target_pairs={{0,6},{6,12},{12,18},{18,24},{24,30},{30,36},{36,42},{42,48},{48,5... | collective-permute-start | bytes 589832 | tf_op jit(solution)/shard_map/while/body/eval_jaxpr/ppermute | solution.py:21
  163.7 6.7 %collective-permute-start = (bf16[8,8,768]{2,1,0:T(8,128)(2,1)S(1)}, bf16[8,8,768]{2,1,0:T(8,128)(2,1)S(1)}, u32[]{:S(2)}, u32[]{:S(2)}) collective-permute-start(bf16[8,8,768]{2,1,0:T(8,128)(2,1)S(1)} %dynamic-slice_bitcast_fusion.2), channel_id=1, source_target_pairs={{6,0},{12,6},{18,12},{24,18},{30,24},{36,30},{42,36},{48,42},{54,4... | collective-permute-start | bytes 294920 | tf_op jit(solution)/shard_map/while/body/eval_jaxpr/ppermute | solution.py:24
  165.7 15.3 %collective-permute-start.1 = (bf16[8,8,768]{2,1,0:T(8,128)(2,1)S(1)}, bf16[8,8,768]{2,1,0:T(8,128)(2,1)S(1)}, u32[]{:S(2)}, u32[]{:S(2)}) collective-permute-start(bf16[8,8,768]{2,1,0:T(8,128)(2,1)S(1)} %dynamic-slice_bitcast_fusion.2), channel_id=1, source_target_pairs={{0,6},{6,12},{12,18},{18,24},{24,30},{30,36},{36,42},{42,48},{48,5... | collective-permute-start | bytes 294920 | tf_op jit(solution)/shard_map/while/body/eval_jaxpr/ppermute | solution.py:21
  169.1 11.9 %collective-permute-start.2 = (f32[8,8,768]{2,1,0:T(8,128)S(1)}, f32[8,8,768]{2,1,0:T(8,128)S(1)}, u32[]{:S(2)}, u32[]{:S(2)}) collective-permute-start(f32[8,8,768]{2,1,0:T(8,128)S(1)} %broadcast_select_fusion.2), channel_id=1, source_target_pairs={{1,0},{2,1},{3,2},{4,3},{5,4},{7,6},{8,7},{9,8},{10,9},{11,10},{13... | collective-permute-start | bytes 589832 | tf_op jit(solution)/shard_map/while/body/eval_jaxpr/ppermute | solution.py:13
  183.2 12.5 %collective-permute-start.3 = (f32[8,8,768]{2,1,0:T(8,128)S(1)}, f32[8,8,768]{2,1,0:T(8,128)S(1)}, u32[]{:S(2)}, u32[]{:S(2)}) collective-permute-start(f32[8,8,768]{2,1,0:T(8,128)S(1)} %get-tuple-element.575), channel_id=1, source_target_pairs={{6,0},{12,6},{18,12},{24,18},{30,24},{36,30},{42,36},{48,42},{54,4... | collective-permute-start | bytes 589832 | tf_op jit(solution)/shard_map/while/body/eval_jaxpr/ppermute | solution.py:24
  191.4 17.1 %collective-permute-start.4 = (f32[8,8,768]{2,1,0:T(8,128)S(1)}, f32[8,8,768]{2,1,0:T(8,128)S(1)}, u32[]{:S(2)}, u32[]{:S(2)}) collective-permute-start(f32[8,8,768]{2,1,0:T(8,128)S(1)} %get-tuple-element.576), channel_id=1, source_target_pairs={{0,6},{6,12},{12,18},{18,24},{24,30},{30,36},{36,42},{42,48},{48,5... | collective-permute-start | bytes 589832 | tf_op jit(solution)/shard_map/while/body/eval_jaxpr/ppermute | solution.py:21
  211.4 6.7 %collective-permute-start = (bf16[8,8,768]{2,1,0:T(8,128)(2,1)S(1)}, bf16[8,8,768]{2,1,0:T(8,128)(2,1)S(1)}, u32[]{:S(2)}, u32[]{:S(2)}) collective-permute-start(bf16[8,8,768]{2,1,0:T(8,128)(2,1)S(1)} %dynamic-slice_bitcast_fusion.2), channel_id=1, source_target_pairs={{6,0},{12,6},{18,12},{24,18},{30,24},{36,30},{42,36},{48,42},{54,4... | collective-permute-start | bytes 294920 | tf_op jit(solution)/shard_map/while/body/eval_jaxpr/ppermute | solution.py:24
  213.3 15.3 %collective-permute-start.1 = (bf16[8,8,768]{2,1,0:T(8,128)(2,1)S(1)}, bf16[8,8,768]{2,1,0:T(8,128)(2,1)S(1)}, u32[]{:S(2)}, u32[]{:S(2)}) collective-permute-start(bf16[8,8,768]{2,1,0:T(8,128)(2,1)S(1)} %dynamic-slice_bitcast_fusion.2), channel_id=1, source_target_pairs={{0,6},{6,12},{12,18},{18,24},{24,30},{30,36},{36,42},{42,48},{48,5... | collective-permute-start | bytes 294920 | tf_op jit(solution)/shard_map/while/body/eval_jaxpr/ppermute | solution.py:21
  216.7 11.9 %collective-permute-start.2 = (f32[8,8,768]{2,1,0:T(8,128)S(1)}, f32[8,8,768]{2,1,0:T(8,128)S(1)}, u32[]{:S(2)}, u32[]{:S(2)}) collective-permute-start(f32[8,8,768]{2,1,0:T(8,128)S(1)} %broadcast_select_fusion.2), channel_id=1, source_target_pairs={{1,0},{2,1},{3,2},{4,3},{5,4},{7,6},{8,7},{9,8},{10,9},{11,10},{13... | collective-permute-start | bytes 589832 | tf_op jit(solution)/shard_map/while/body/eval_jaxpr/ppermute | solution.py:13
  230.7 10.5 %collective-permute-start.3 = (f32[8,8,768]{2,1,0:T(8,128)S(1)}, f32[8,8,768]{2,1,0:T(8,128)S(1)}, u32[]{:S(2)}, u32[]{:S(2)}) collective-permute-start(f32[8,8,768]{2,1,0:T(8,128)S(1)} %get-tuple-element.575), channel_id=1, source_target_pairs={{6,0},{12,6},{18,12},{24,18},{30,24},{36,30},{42,36},{48,42},{54,4... | collective-permute-start | bytes 589832 | tf_op jit(solution)/shard_map/while/body/eval_jaxpr/ppermute | solution.py:24
  238.0 16.3 %collective-permute-start.4 = (f32[8,8,768]{2,1,0:T(8,128)S(1)}, f32[8,8,768]{2,1,0:T(8,128)S(1)}, u32[]{:S(2)}, u32[]{:S(2)}) collective-permute-start(f32[8,8,768]{2,1,0:T(8,128)S(1)} %get-tuple-element.576), channel_id=1, source_target_pairs={{0,6},{6,12},{12,18},{18,24},{24,30},{30,36},{36,42},{42,48},{48,5... | collective-permute-start | bytes 589832 | tf_op jit(solution)/shard_map/while/body/eval_jaxpr/ppermute | solution.py:21
  256.2 78.4 %copy-start.4 = (f32[2,8,8,768]{3,2,1,0:T(8,128)S(1)}, f32[2,8,8,768]{3,2,1,0:T(8,128)}, u32[]{:S(2)}) copy-start(f32[2,8,8,768]{3,2,1,0:T(8,128)} %get-tuple-element.622) | copy-start | bytes 1179652 | tf_op jit(solution)/shard_map/while
  257.2 6.7 %collective-permute-start = (bf16[8,8,768]{2,1,0:T(8,128)(2,1)S(1)}, bf16[8,8,768]{2,1,0:T(8,128)(2,1)S(1)}, u32[]{:S(2)}, u32[]{:S(2)}) collective-permute-start(bf16[8,8,768]{2,1,0:T(8,128)(2,1)S(1)} %dynamic-slice_bitcast_fusion.2), channel_id=1, source_target_pairs={{6,0},{12,6},{18,12},{24,18},{30,24},{36,30},{42,36},{48,42},{54,4... | collective-permute-start | bytes 294920 | tf_op jit(solution)/shard_map/while/body/eval_jaxpr/ppermute | solution.py:24
  259.1 15.3 %collective-permute-start.1 = (bf16[8,8,768]{2,1,0:T(8,128)(2,1)S(1)}, bf16[8,8,768]{2,1,0:T(8,128)(2,1)S(1)}, u32[]{:S(2)}, u32[]{:S(2)}) collective-permute-start(bf16[8,8,768]{2,1,0:T(8,128)(2,1)S(1)} %dynamic-slice_bitcast_fusion.2), channel_id=1, source_target_pairs={{0,6},{6,12},{12,18},{18,24},{24,30},{30,36},{36,42},{42,48},{48,5... | collective-permute-start | bytes 294920 | tf_op jit(solution)/shard_map/while/body/eval_jaxpr/ppermute | solution.py:21
  261.5 73.2 %copy-start.2 = (bf16[384,768]{1,0:T(8,128)(2,1)S(1)}, bf16[384,768]{1,0:T(8,128)(2,1)}, u32[]{:S(2)}) copy-start(bf16[384,768]{1,0:T(8,128)(2,1)} %get-tuple-element.627) | copy-start | bytes 1769476 | tf_op jit(solution)/shard_map/while
  262.5 72.1 %collective-permute-start.2 = (f32[8,8,768]{2,1,0:T(8,128)S(1)}, f32[8,8,768]{2,1,0:T(8,128)S(1)}, u32[]{:S(2)}, u32[]{:S(2)}) collective-permute-start(f32[8,8,768]{2,1,0:T(8,128)S(1)} %broadcast_select_fusion.2), channel_id=1, source_target_pairs={{1,0},{2,1},{3,2},{4,3},{5,4},{7,6},{8,7},{9,8},{10,9},{11,10},{13... | collective-permute-start | bytes 589832 | tf_op jit(solution)/shard_map/while/body/eval_jaxpr/ppermute | solution.py:13
  263.9 70.8 %copy-start = (bf16[768,384]{1,0:T(8,128)(2,1)S(1)}, bf16[768,384]{1,0:T(8,128)(2,1)}, u32[]{:S(2)}) copy-start(bf16[768,384]{1,0:T(8,128)(2,1)} %get-tuple-element.626) | copy-start | bytes 1769476 | tf_op jit(solution)/shard_map/while
  263.9 70.8 %copy-start.1 = (bf16[768,384]{1,0:T(8,128)(2,1)S(1)}, bf16[768,384]{1,0:T(8,128)(2,1)}, u32[]{:S(2)}) copy-start(bf16[768,384]{1,0:T(8,128)(2,1)} %get-tuple-element.625) | copy-start | bytes 1769476 | tf_op jit(solution)/shard_map/while
  350.6 28.2 %copy-start.5 = (f32[2,8,8,768]{3,2,1,0:T(8,128)S(1)}, f32[2,8,8,768]{3,2,1,0:T(8,128)}, u32[]{:S(2)}) copy-start(f32[2,8,8,768]{3,2,1,0:T(8,128)} %get-tuple-element.622) | copy-start | bytes 1179652 | tf_op jit(solution)/shard_map/while
  350.6 28.2 %copy-start.6 = (bf16[2,8,8,768]{3,2,1,0:T(8,128)(2,1)S(1)}, bf16[2,8,8,768]{3,2,1,0:T(8,128)(2,1)}, u32[]{:S(2)}) copy-start(bf16[2,8,8,768]{3,2,1,0:T(8,128)(2,1)} %get-tuple-element.623) | copy-start | bytes 589828 | tf_op jit(solution)/shard_map/while
  350.6 28.2 %copy-start.7 = (bf16[2,8,8,768]{3,2,1,0:T(8,128)(2,1)S(1)}, bf16[2,8,8,768]{3,2,1,0:T(8,128)(2,1)}, u32[]{:S(2)}) copy-start(bf16[2,8,8,768]{3,2,1,0:T(8,128)(2,1)} %get-tuple-element.630) | copy-start | bytes 589828 | tf_op jit(solution)/shard_map/while
  350.6 28.2 %copy-start.8 = (f32[8,8,1]{1,0,2:T(8,128)S(1)}, f32[8,8,1]{1,0,2:T(8,128)}, u32[]{:S(2)}) copy-start(f32[8,8,1]{1,0,2:T(8,128)} %get-tuple-element.629) | copy-start | bytes 772 | tf_op jit(solution)/shard_map/while
  351.7 14.0 %collective-permute-start.3 = (f32[8,8,768]{2,1,0:T(8,128)S(1)}, f32[8,8,768]{2,1,0:T(8,128)S(1)}, u32[]{:S(2)}, u32[]{:S(2)}) collective-permute-start(f32[8,8,768]{2,1,0:T(8,128)S(1)} %get-tuple-element.575), channel_id=1, source_target_pairs={{6,0},{12,6},{18,12},{24,18},{30,24},{36,30},{42,36},{48,42},{54,4... | collective-permute-start | bytes 589832 | tf_op jit(solution)/shard_map/while/body/eval_jaxpr/ppermute | solution.py:24
  362.5 16.3 %collective-permute-start.4 = (f32[8,8,768]{2,1,0:T(8,128)S(1)}, f32[8,8,768]{2,1,0:T(8,128)S(1)}, u32[]{:S(2)}, u32[]{:S(2)}) collective-permute-start(f32[8,8,768]{2,1,0:T(8,128)S(1)} %get-tuple-element.576), channel_id=1, source_target_pairs={{0,6},{6,12},{12,18},{18,24},{24,30},{30,36},{36,42},{42,48},{48,5... | collective-permute-start | bytes 589832 | tf_op jit(solution)/shard_map/while/body/eval_jaxpr/ppermute | solution.py:21
  381.7 6.7 %collective-permute-start = (bf16[8,8,768]{2,1,0:T(8,128)(2,1)S(1)}, bf16[8,8,768]{2,1,0:T(8,128)(2,1)S(1)}, u32[]{:S(2)}, u32[]{:S(2)}) collective-permute-start(bf16[8,8,768]{2,1,0:T(8,128)(2,1)S(1)} %dynamic-slice_bitcast_fusion.2), channel_id=1, source_target_pairs={{6,0},{12,6},{18,12},{24,18},{30,24},{36,30},{42,36},{48,42},{54,4... | collective-permute-start | bytes 294920 | tf_op jit(solution)/shard_map/while/body/eval_jaxpr/ppermute | solution.py:24
  383.6 15.3 %collective-permute-start.1 = (bf16[8,8,768]{2,1,0:T(8,128)(2,1)S(1)}, bf16[8,8,768]{2,1,0:T(8,128)(2,1)S(1)}, u32[]{:S(2)}, u32[]{:S(2)}) collective-permute-start(bf16[8,8,768]{2,1,0:T(8,128)(2,1)S(1)} %dynamic-slice_bitcast_fusion.2), channel_id=1, source_target_pairs={{0,6},{6,12},{12,18},{18,24},{24,30},{30,36},{36,42},{42,48},{48,5... | collective-permute-start | bytes 294920 | tf_op jit(solution)/shard_map/while/body/eval_jaxpr/ppermute | solution.py:21
  387.0 11.9 %collective-permute-start.2 = (f32[8,8,768]{2,1,0:T(8,128)S(1)}, f32[8,8,768]{2,1,0:T(8,128)S(1)}, u32[]{:S(2)}, u32[]{:S(2)}) collective-permute-start(f32[8,8,768]{2,1,0:T(8,128)S(1)} %broadcast_select_fusion.2), channel_id=1, source_target_pairs={{1,0},{2,1},{3,2},{4,3},{5,4},{7,6},{8,7},{9,8},{10,9},{11,10},{13... | collective-permute-start | bytes 589832 | tf_op jit(solution)/shard_map/while/body/eval_jaxpr/ppermute | solution.py:13
  416.0 11.5 %collective-permute-start.3 = (f32[8,8,768]{2,1,0:T(8,128)S(1)}, f32[8,8,768]{2,1,0:T(8,128)S(1)}, u32[]{:S(2)}, u32[]{:S(2)}) collective-permute-start(f32[8,8,768]{2,1,0:T(8,128)S(1)} %get-tuple-element.575), channel_id=1, source_target_pairs={{6,0},{12,6},{18,12},{24,18},{30,24},{36,30},{42,36},{48,42},{54,4... | collective-permute-start | bytes 589832 | tf_op jit(solution)/shard_map/while/body/eval_jaxpr/ppermute | solution.py:24
  424.4 16.3 %collective-permute-start.4 = (f32[8,8,768]{2,1,0:T(8,128)S(1)}, f32[8,8,768]{2,1,0:T(8,128)S(1)}, u32[]{:S(2)}, u32[]{:S(2)}) collective-permute-start(f32[8,8,768]{2,1,0:T(8,128)S(1)} %get-tuple-element.576), channel_id=1, source_target_pairs={{0,6},{6,12},{12,18},{18,24},{24,30},{30,36},{36,42},{42,48},{48,5... | collective-permute-start | bytes 589832 | tf_op jit(solution)/shard_map/while/body/eval_jaxpr/ppermute | solution.py:21
  (47 other events, 823.6 us)
where the time goes:
time: 445 us; the launch traced here: 443 us
  waiting for transfers between devices  237 us (53%)
  starting transfers between devices  131 us (29%)
  local copies, waits for them, and re-layouts  31.5 us (7%)
  other arithmetic  21.6 us (5%)
  matrix products  15.6 us (4%)
  loops' own time  5.46 us (1%)
    ppermute x14, waiting for transfers between devices, extended(): lax.ppermute(lax.slice_in_dim(block, block.shape[dim] - width, None, axis...  167 us
    ppermute x14, starting transfers between devices, extended(): lax.ppermute(lax.slice_in_dim(block, 0, width, axis=dim), axis, backward)  92.1 us
    ppermute x7, waiting for transfers between devices, passed_along(): return lax.ppermute(shard, axis, pairs)  60.8 us
    ppermute x14, starting transfers between devices, extended(): lax.ppermute(lax.slice_in_dim(block, block.shape[dim] - width, None, axis...  29.8 us
    select_n x7, other arithmetic, advance(): result = jnp.where(active, stored, result)  13.1 us
    ppermute x14, waiting for transfers between devices, extended(): lax.ppermute(lax.slice_in_dim(block, 0, width, axis=dim), axis, backward)  9.74 us
    ppermute x7, starting transfers between devices, passed_along(): return lax.ppermute(shard, axis, pairs)  9.18 us
  transfers between devices with their start and end apart: 35, of which 23 were waited for; matrix products, arithmetic and copies ran while one was open for 1% of the time, Pallas kernels for 0%

commit v1 on v0

v1 whole, which is shorter than its diff:
```python
import functools

import jax
import jax.numpy as jnp
from jax import lax
from jax.experimental import pallas as pl
from jax.experimental.pallas import tpu as pltpu
from jax.sharding import PartitionSpec as P

HD = 32
WIN = 8
AXES = ("lat", "section")
FLT = jnp.float32
BF = jnp.bfloat16
BAND = 64
SLOT = 128
GROUP = 4


def dot_nn(a, b):
    return lax.dot_general(a, b, (((1,), (0,)), ((), ())), preferred_element_type=FLT)


def dot_nt(a, b):
    return lax.dot_general(a, b, (((1,), (1,)), ((), ())), preferred_element_type=FLT)


def gathered(rows, field, core, offset, own, other, near0, near1):
    near = jnp.where(core == 0, near0[field].astype(FLT), near1[field].astype(FLT))
    rows[0:BAND, :] = near
    rows[pl.ds(pl.multiple_of(BAND + BAND * core, BAND), BAND), :] = own[core, field].astype(FLT)
    rows[pl.ds(pl.multiple_of(2 * BAND - BAND * core, BAND), BAND), :] = other[field].astype(FLT)
    return rows[pl.ds(pl.multiple_of(offset * WIN, WIN), SLOT), :]


def prepare_kernel(
    fields,
    scalars,
    own,
    other,
    near0,
    near1,
    w_query,
    w_key,
    w_value,
    attend_ref,
    attend_t_ref,
    value_ref,
    key_ref,
    query_t_ref,
    out_ref,
    forcing_ref,
    *rest,
):
    rows = rest[-1]
    core, slot, offset = scalars[0], scalars[1], scalars[2]
    x = gathered(rows, 0, core, offset, own, other, near0, near1).astype(BF)
    forcing_ref[...] = gathered(rows, 1, core, offset, own, other, near0, near1).astype(BF)
    if fields == 3:
        rest[0][...] = gathered(rows, 2, core, offset, own, other, near0, near1).astype(BF)
    scale = HD ** (-0.5)
    q = (dot_nn(x, w_query[...]) * scale).astype(BF)
    k = dot_nn(x, w_key[...]).astype(BF)
    v = dot_nn(x, w_value[...]).astype(BF)
    token = lax.broadcasted_iota(jnp.int32, (SLOT, SLOT), 0)
    other_token = lax.broadcasted_iota(jnp.int32, (SLOT, SLOT), 1)
    row_head = token // HD
    lane_head = other_token // HD
    edge = jnp.where(slot == 0, BAND - offset * WIN, 0)
    allowed = ((token // BAND) == (other_token // BAND)) & (
        (token < edge) == (other_token < edge)
    )
    for group in range(3):
        lanes = slice(SLOT * group, SLOT * group + SLOT)
        q_g, k_g, v_g = q[:, lanes], k[:, lanes], v[:, lanes]
        q_t = q_g.astype(FLT).T
        k_t = k_g.astype(FLT).T
        v_t = v_g.astype(FLT).T
        mixed = jnp.zeros((SLOT, SLOT), FLT)
        for h in range(GROUP):
            at = slice(SLOT * h, SLOT * h + SLOT)
            wide = slice(SLOT * (GROUP * group + h), SLOT * (GROUP * group + h) + SLOT)
            in_rows = row_head == h
            in_lanes = lane_head == h
            scores = dot_nn(q_g, jnp.where(in_rows, k_t, 0.0).astype(BF))
            scores = jnp.where(allowed, scores, -1000000000.0)
            scores = scores - jnp.max(scores, axis=-1, keepdims=True)
            expon = jnp.exp(scores)
            attend = expon / jnp.sum(expon, axis=-1, keepdims=True)
            attend_b = attend.astype(BF)
            attend_ref[:, wide] = attend_b
            attend_t_ref[:, wide] = attend.T.astype(BF)
            mixed += dot_nn(attend_b, jnp.where(in_lanes, v_g, jnp.zeros_like(v_g)))
            value_ref[group, 0:SLOT, at] = jnp.where(in_rows, v_t, 0.0).astype(BF)
            value_ref[group, SLOT : 2 * SLOT, at] = jnp.where(in_rows, -1.0, 0.0).astype(BF)
            key_ref[group, at, :] = jnp.where(in_lanes, k_g, jnp.zeros_like(k_g))
            query_t_ref[group, :, at] = jnp.where(in_rows, q_t, 0.0).astype(BF)
        out_ref[:, lanes] = mixed


def step_kernel(
    first,
    scalars,
    *refs,
):
    if first:
        incoming = refs[:1]
        refs = refs[1:]
    else:
        incoming = refs[:3]
        refs = refs[3:]
    (
        forcing_ref,
        attend_ref,
        attend_t_ref,
        value_ref,
        key_ref,
        query_t_ref,
        out_ref,
        w_query,
        w_key,
        w_value,
        w_out,
        all_ref,
        low_ref,
        high_ref,
        rows,
    ) = refs
    scale = HD ** (-0.5)
    if first:
        adjoint = incoming[0][...].astype(FLT)
    else:
        rows[0:BAND, :] = incoming[0][...].astype(FLT)
        rows[BAND : BAND + SLOT, :] = incoming[1][...].astype(FLT)
        rows[BAND + SLOT :, :] = incoming[2][...].astype(FLT)
        shift = scalars[3]
        adjoint = rows[pl.ds(pl.multiple_of(BAND + shift * WIN, WIN), SLOT), :]
    g = dot_nt(adjoint.astype(BF), w_out[...]).astype(BF)
    lane_head = lax.broadcasted_iota(jnp.int32, (SLOT, SLOT), 1) // HD
    g_query, g_key, g_value = [], [], []
    for group in range(3):
        lanes = slice(SLOT * group, SLOT * group + SLOT)
        wide = slice(GROUP * SLOT * group, GROUP * SLOT * (group + 1))
        g_g = g[:, lanes]
        g_o = (g_g.astype(FLT) * out_ref[:, lanes]).astype(BF)
        centred = dot_nn(jnp.concatenate([g_g, g_o], axis=1), value_ref[group])
        g_s = (attend_ref[:, wide].astype(FLT) * centred).astype(BF)
        g_query.append((dot_nn(g_s, key_ref[group]) * scale).astype(BF))
        stacked = jnp.concatenate(
            [g_s[:, SLOT * h : SLOT * h + SLOT] for h in range(GROUP)], axis=0
        )
        g_key.append(dot_nn(query_t_ref[group], stacked).T.astype(BF))
        spread = jnp.concatenate(
            [jnp.where(lane_head == h, g_g, jnp.zeros_like(g_g)) for h in range(GROUP)], axis=0
        )
        g_value.append(dot_nn(attend_t_ref[:, wide], spread).astype(BF))
    change = dot_nt(jnp.concatenate(g_query, axis=1), w_query[...])
    change += dot_nt(jnp.concatenate(g_key, axis=1), w_key[...])
    change += dot_nt(jnp.concatenate(g_value, axis=1), w_value[...])
    updated = (adjoint + change + forcing_ref[...].astype(FLT)).astype(BF)
    all_ref[...] = updated
    low_ref[...] = updated[:BAND]
    high_ref[...] = updated[BAND:]


def split_kernel(ticks, scalars, *refs):
    results = refs[:ticks]
    own_ref, swap_ref, lower_ref, held, rows, sem = refs[ticks:]
    core, offset, section = scalars[0], scalars[2], scalars[4]
    for tick in range(ticks):

        @pl.when(section == ticks - 1 - tick)
        def _():
            copy = pltpu.make_async_copy(results[tick], held, sem)
            copy.start()
            copy.wait()

    lower_ref[...] = held[0:BAND]
    rows[...] = held[...].astype(FLT)
    even = rows[pl.ds(pl.multiple_of(BAND - offset * WIN, WIN), BAND), :].astype(BF)
    odd = held[BAND:SLOT]
    own_ref[...] = jnp.where(core == 0, even, odd)
    swap_ref[...] = jnp.where(core == 0, odd, even)


def final_kernel(scalars, own, other, near0, near1, result, rows):
    core, offset = scalars[0], scalars[2]
    for member, near in ((0, near0), (1, near1)):
        rows[0:BAND, :] = jnp.where(core == member, own[...].astype(FLT), other[...].astype(FLT))
        rows[BAND:SLOT, :] = near[...].astype(FLT)
        start = jnp.where(core == 1, BAND - offset * WIN, 0)
        result[member] = rows[pl.ds(pl.multiple_of(start, WIN), BAND), :]


def vmem(count):
    return [pl.BlockSpec(memory_space=pltpu.VMEM)] * count


SMEM = pl.BlockSpec(memory_space=pltpu.SMEM)
PARAMS = pltpu.CompilerParams(vmem_limit_bytes=40 * 1024 * 1024)


def struct(shape, kind=BF):
    return jax.ShapeDtypeStruct(shape, kind)


def prepare(scalars, own, other, near0, near1, w_query, w_key, w_value):
    fields, _, width = other.shape
    hidden = w_query.shape[1]
    keys = hidden // HD * SLOT
    shapes = [
        struct((SLOT, keys)),
        struct((SLOT, keys)),
        struct((3, 2 * SLOT, GROUP * SLOT)),
        struct((3, GROUP * SLOT, SLOT)),
        struct((3, SLOT, GROUP * SLOT)),
        struct((SLOT, hidden), FLT),
        struct((SLOT, width)),
    ]
    if fields == 3:
        shapes.append(struct((SLOT, width)))
    return pl.pallas_call(
        functools.partial(prepare_kernel, fields),
        out_shape=shapes,
        in_specs=[SMEM] + vmem(7),
        out_specs=vmem(len(shapes)),
        scratch_shapes=[pltpu.VMEM((3 * BAND, width), FLT)],
        compiler_params=PARAMS,
        name="prepare",
    )(scalars, own, other, near0, near1, w_query, w_key, w_value)


def step(first, scalars, incoming, prepared, weights):
    width = incoming[0].shape[-1]
    attend, attend_t, values, keys, queries_t, out, forcing = prepared
    operands = (*incoming, forcing, attend, attend_t, values, keys, queries_t, out, *weights)
    return pl.pallas_call(
        functools.partial(step_kernel, first),
        out_shape=[struct((SLOT, width)), struct((BAND, width)), struct((BAND, width))],
        in_specs=[SMEM] + vmem(len(operands)),
        out_specs=vmem(3),
        scratch_shapes=[pltpu.VMEM((4 * BAND, width), FLT)],
        compiler_params=PARAMS,
        name="step",
    )(scalars, *operands)


def on_device(
    trajectory, observed, obs_mask, shift_rows, final_adjoint, w_query, w_key, w_value, w_out
):
    sections = lax.axis_size("section")
    bands = lax.axis_size("lat")
    chips = bands // 2
    section_at = lax.axis_index("section")
    band_at = lax.axis_index("lat")
    members, rows_here, across, width = trajectory.shape[1:]
    offset = shift_rows[0].astype(jnp.int32)
    core, chip = band_at % 2, band_at // 2
    weights = (w_query[0], w_key[0], w_value[0], w_out[0])

    def at(band, section):
        return (band % bands) * sections + section

    def sent(value, hops):
        return lax.ppermute(value, AXES, hops)

    def exchange(fields, among):
        both = [(at(b, s), at(b ^ 1, s)) for b in range(bands) for s in among]
        up0 = [(at(2 * j + 1, s), at(2 * j + 2, s)) for j in range(chips) for s in among]
        up1 = [(at(2 * j + 1, s), at(2 * j + 3, s)) for j in range(chips) for s in among]
        near0 = sent(fields[0], up0)
        near1 = sent(fields[1], up1)
        other = sent(lax.dynamic_index_in_dim(fields, 1 - core, 0, keepdims=False), both)
        return other, near0, near1

    x = trajectory[0].reshape(members, BAND, width)
    seen = observed[0].reshape(members, BAND, width)
    weight = obs_mask[0].reshape(1, BAND, 1).astype(FLT)
    forcing = (weight * (x.astype(FLT) - seen.astype(FLT))).astype(BF)
    final = final_adjoint.reshape(members, BAND, width).astype(BF)
    with jax.named_scope("first_exchange"):
        last = jnp.stack([x, forcing, final], axis=1)
        got = exchange(last, [sections - 1])
        above = lax.ppermute(
            shift_rows, "section", [(s, s - 1) for s in range(1, sections)]
        )[0].astype(jnp.int32)
    shift = jnp.where(section_at == sections - 1, 0, offset - above)
    scalars = jnp.stack([core, chip, offset, shift, section_at]).astype(jnp.int32)
    *prepared, start = prepare(scalars, last, *got, *weights[:3])

    result = step(True, scalars, (start,), prepared, weights)
    results = [result[0]]
    with jax.named_scope("later_exchange"):
        pair = jnp.stack([x, forcing], axis=1)
        pair, _ = lax.optimization_barrier((pair, prepared[0]))
        got = exchange(pair, list(range(sections - 1)))
    prepared = prepare(scalars, pair, *got, *weights[:3])
    for tick in range(1, sections):
        source = sections - tick
        with jax.named_scope("pass_on"):
            hops = [
                [(at(b + 2 * way, source), at(b, source - 1)) for b in range(bands)]
                for way in (-1, 1, 0)
            ]
            from_low = sent(result[2], hops[0])
            from_high = sent(result[1], hops[1])
            middle = sent(result[0], hops[2])
        result = step(False, scalars, (from_low, middle, from_high), prepared, weights)
        results.append(result[0])

    own, swap, lower = pl.pallas_call(
        functools.partial(split_kernel, sections),
        out_shape=[struct((BAND, width))] * 3,
        in_specs=[SMEM] + [pl.BlockSpec(memory_space=pl.ANY)] * sections,
        out_specs=vmem(3),
        scratch_shapes=[
            pltpu.VMEM((SLOT, width), BF),
            pltpu.VMEM((SLOT, width), FLT),
            pltpu.SemaphoreType.DMA,
        ],
        compiler_params=PARAMS,
        name="split",
    )(scalars, *results)
    with jax.named_scope("last_exchange"):
        every = range(sections)
        near0 = sent(lower, [(at(2 * j + 2, s), at(2 * j + 1, s)) for j in range(chips) for s in every])
        near1 = sent(lower, [(at(2 * j + 3, s), at(2 * j + 1, s)) for j in range(chips) for s in every])
        other = sent(swap, [(at(b, s), at(b ^ 1, s)) for b in range(bands) for s in every])
    field = pl.pallas_call(
        final_kernel,
        out_shape=struct((members, BAND, width), FLT),
        in_specs=[SMEM] + vmem(4),
        out_specs=vmem(1)[0],
        scratch_shapes=[pltpu.VMEM((SLOT, width), FLT)],
        compiler_params=PARAMS,
        name="merge",
    )(scalars, own, other, near0, near1)
    return field.reshape(1, members, rows_here, across, width)


def solution(mesh):
    placed = (
        P("section", None, "lat", None, None),
        P("section", None, "lat", None, None),
        P("section", "lat", None),
        P("section"),
        P(None, "lat", None, None),
        P("section", None, None),
        P("section", None, None),
        P("section", None, None),
        P("section", None, None),
    )
    return jax.shard_map(
        on_device,
        mesh=mesh,
        in_specs=placed,
        out_specs=P("section", None, "lat", None, None),
        check_vma=False,
    )
```

time: 445 us -> 135 us (0.30)
  the two profiles are of different devices: /device:TPU:6 before, /device:TPU:1 now
where the time goes in v1:
time: 135 us
  waiting for transfers between devices  58.8 us (44%)
  starting transfers between devices  47.6 us (35%)
  Pallas kernels  22.4 us (17%)
  other arithmetic  2.2 us (2%)
  between operations  1.85 us (1%)
  local copies, waits for them, and re-layouts  1.77 us (1%)
    ppermute x24, waiting for transfers between devices, sent(): return lax.ppermute(value, AXES, hops)  55.7 us
    ppermute x24, starting transfers between devices, sent(): return lax.ppermute(value, AXES, hops)  46.4 us
    pallas_call x6, Pallas kernels, step(): pl.pallas_call(functools.partial(step_kernel, first), out_shape=[struct((...  15 us
    pallas_call x2, Pallas kernels, prepare(): pl.pallas_call(functools.partial(prepare_kernel, fields), out_shape=shape...  5.1 us
    ppermute x1, waiting for transfers between devices, on_device(): lax.ppermute(shift_rows, 'section', [(s, s - 1) for s in range(1, section...  3.05 us
  transfers between devices with their start and end apart: 25, of which 6 were waited for; matrix products, arithmetic and copies ran while one was open for 1% of the time, Pallas kernels for 3%

profile of v1, /device:TPU:1, one launch (start us, length us, event | category | flops | bytes accessed | tf_op | source)
XLA Modules:
  0.0 134.6 jit_solution(18341839345214769799)
XLA Ops:
  0.0 1.1 convert_bitcast_fusion
  1.1 0.1 convert_element_type.58
  1.2 0.1 fusion.1
  1.4 0.6 copy-done.5
  2.0 0.9 slice_bitcast_fusion
  2.9 0.8 collective-permute-start.1
  3.7 0.7 collective-permute-start.2
  4.4 1.4 %collective-permute-start.3 = (bf16[3,64,768]{2,1,0:T(8,128)(2,1)}, bf16[3,64,768]{2,1,0:T(8,128)(2,1)}, u32[]{:S(2)}, u32[]{:S(2)}) collective-permute-start(bf16[3,64,768]{2,1,0:T(8,128)(2,1)} %get-tuple-element.75), channel_id=1, source_target_pairs={{11,23},{23,35},{35,47},{47,59},{59,71},{71,83},{83,95},{95,107},{... | collective-permute-start | bytes 884744 | tf_op jit(solution)/shard_map/first_exchange/ppermute | solution.py:265
  5.8 1.3 collective-permute-start
  7.8 1.0 pad_maximum_fusion.1.own
  8.7 3.0 %collective-permute-done = s32[1]{0:T(128)} collective-permute-done((s32[1]{0:T(128)}, s32[1]{0:T(128)}, u32[]{:S(2)}, u32[]{:S(2)}) %collective-permute-start) | collective-permute-done | bytes 36 | tf_op jit(solution)/shard_map/first_exchange/ppermute | solution.py:284
  12.5 0.1 stack.28.scalars
  12.6 2.8 %prepare.2 = (bf16[128,1536]{1,0:T(8,128)(2,1)S(1)}, bf16[128,1536]{1,0:T(8,128)(2,1)S(1)}, bf16[3,256,512]{2,1,0:T(8,128)(2,1)S(1)}, bf16[3,512,128]{2,1,0:T(8,...) custom-call(s32[5]{0:T(128)S(1)} %stack.28.scalars, ...), custom_call_target="tpu_custom_call" | custom-call | tf_op jit(solution)/shard_map/prepare/pallas_call | solution.py:222
  15.5 12.1 %collective-permute-start.7 = (bf16[2,64,768]{2,1,0:T(8,128)(2,1)S(1)}, bf16[2,64,768]{2,1,0:T(8,128)(2,1)S(1)}, u32[]{:S(2)}, u32[]{:S(2)}) collective-permute-start(bf16[2,64,768]{2,1,0:T(8,128)(2,1)S(1)} %get-tuple-element.80), channel_id=1, source_target_pairs={{0,6},{1,7},{2,8},{3,9},{4,10},{6,0},{7,1},{8,2},{9,3},{10,4},{12,... | collective-permute-start | bytes 589832 | tf_op jit(solution)/shard_map/later_exchange/ppermute | solution.py:265
  27.6 1.3 collective-permute-start.8
  28.9 1.9 %collective-permute-start.9 = (bf16[2,64,768]{2,1,0:T(8,128)(2,1)S(1)}, bf16[2,64,768]{2,1,0:T(8,128)(2,1)S(1)}, u32[]{:S(2)}, u32[]{:S(2)}) collective-permute-start(bf16[2,64,768]{2,1,0:T(8,128)(2,1)S(1)} %get-tuple-element.78), channel_id=1, source_target_pairs={{6,18},{7,19},{8,20},{9,21},{10,22},{18,30},{19,31},{20,32},{21,33... | collective-permute-start | bytes 589832 | tf_op jit(solution)/shard_map/later_exchange/ppermute | solution.py:265
  30.8 2.4 %step.6 = (bf16[128,768]{1,0:T(8,128)(2,1)S(1)}, bf16[64,768]{1,0:T(8,128)(2,1)S(1)}, bf16[64,768]{1,0:T(8,128)(2,1)S(1)}) custom-call(s32[5]{0:T(128)S(1)} %stack.28.scalars, bf16[128,768]{1,0:T(8,128)(2,1)S(1)} %get-tuple-element.40.refs_0_, bf16[128,768]{1,0:T(8,128)(2,1)S(1)} %get-tuple-element.41.refs_1_, ...), custom_call_target="tpu_custom_call" | custom-call | tf_op jit(solution)/shard_map/step/pallas_call | solution.py:237
  33.2 0.7 collective-permute-start.5
  33.9 0.7 collective-permute-start.4
  34.6 0.7 collective-permute-start.6
  35.3 13.5 %collective-permute-done.9.near1 = bf16[2,64,768]{2,1,0:T(8,128)(2,1)S(1)} collective-permute-done((bf16[2,64,768]{2,1,0:T(8,128)(2,1)S(1)}, bf16[2,64,768]{2,1,0:T(8,128)(2,1)S(1)}, u32[]{:S(2)}, u32[]{:S(2)}) %collective-permute-start.9) | collective-permute-done | bytes 196640 | tf_op jit(solution)/shard_map/later_exchange/ppermute | solution.py:265
  48.8 2.3 %prepare.3 = (bf16[128,1536]{1,0:T(8,128)(2,1)S(1)}, bf16[128,1536]{1,0:T(8,128)(2,1)S(1)}, bf16[3,256,512]{2,1,0:T(8,128)(2,1)S(1)}, bf16[3,512,128]{2,1,0:T(8,...) custom-call(s32[5]{0:T(128)S(1)} %stack.28.scalars, ...), custom_call_target="tpu_custom_call" | custom-call | tf_op jit(solution)/shard_map/prepare/pallas_call | solution.py:222
  51.2 2.4 %step.7 = (bf16[128,768]{1,0:T(8,128)(2,1)S(1)}, bf16[64,768]{1,0:T(8,128)(2,1)S(1)}, bf16[64,768]{1,0:T(8,128)(2,1)S(1)}) custom-call(s32[5]{0:T(128)S(1)} %stack.28.scalars, bf16[64,768]{1,0:T(8,128)(2,1)S(1)} %collective-permute-done.4.refs_0_, bf16[128,768]{1,0:T(8,128)(2,1)S(1)} %collective-permute-done.5.refs_1_, ...), custom_call_target="tpu_custom_call" | custom-call | tf_op jit(solution)/shard_map/step/pallas_call | solution.py:237
  53.6 0.7 collective-permute-start.11
  54.2 0.7 collective-permute-start.10
  54.9 0.7 collective-permute-start.12
  55.6 2.4 %step.8 = (bf16[128,768]{1,0:T(8,128)(2,1)S(1)}, bf16[64,768]{1,0:T(8,128)(2,1)S(1)}, bf16[64,768]{1,0:T(8,128)(2,1)S(1)}) custom-call(s32[5]{0:T(128)S(1)} %stack.28.scalars, bf16[64,768]{1,0:T(8,128)(2,1)S(1)} %collective-permute-done.10.refs_0_, bf16[128,768]{1,0:T(8,128)(2,1)S(1)} %collective-permute-done.11.refs_1_, ...), custom_call_target="tpu_custom_call" | custom-call | tf_op jit(solution)/shard_map/step/pallas_call | solution.py:237
  58.0 0.7 collective-permute-start.14
  58.7 0.7 collective-permute-start.13
  59.4 0.7 collective-permute-start.15
  60.1 2.4 %step.9 = (bf16[128,768]{1,0:T(8,128)(2,1)S(1)}, bf16[64,768]{1,0:T(8,128)(2,1)S(1)}, bf16[64,768]{1,0:T(8,128)(2,1)S(1)}) custom-call(s32[5]{0:T(128)S(1)} %stack.28.scalars, bf16[64,768]{1,0:T(8,128)(2,1)S(1)} %collective-permute-done.13.refs_0_, bf16[128,768]{1,0:T(8,128)(2,1)S(1)} %collective-permute-done.14.refs_1_, ...), custom_call_target="tpu_custom_call" | custom-call | tf_op jit(solution)/shard_map/step/pallas_call | solution.py:237
  62.5 0.7 collective-permute-start.17
  63.2 0.7 collective-permute-start.16
  63.8 0.7 collective-permute-start.18
  64.5 2.4 %step.10 = (bf16[128,768]{1,0:T(8,128)(2,1)S(1)}, bf16[64,768]{1,0:T(8,128)(2,1)S(1)}, bf16[64,768]{1,0:T(8,128)(2,1)S(1)}) custom-call(s32[5]{0:T(128)S(1)} %stack.28.scalars, bf16[64,768]{1,0:T(8,128)(2,1)S(1)} %collective-permute-done.16.refs_0_, bf16[128,768]{1,0:T(8,128)(2,1)S(1)} %collective-permute-done.17.refs_1_, ...), custom_call_target="tpu_custom_call" | custom-call | tf_op jit(solution)/shard_map/step/pallas_call | solution.py:237
  66.9 1.3 collective-permute-start.20
  68.2 1.3 collective-permute-start.19
  69.5 1.3 collective-permute-start.21
  70.8 39.5 %collective-permute-done.19.refs_0_ = bf16[64,768]{1,0:T(8,128)(2,1)S(1)} collective-permute-done((bf16[64,768]{1,0:T(8,128)(2,1)S(1)}, bf16[64,768]{1,0:T(8,128)(2,1)S(1)}, u32[]{:S(2)}, u32[]{:S(2)}) %collective-permute-start.19) | collective-permute-done | bytes 98336 | tf_op jit(solution)/shard_map/pass_on/ppermute | solution.py:265
  110.4 0.2 collective-permute-done.21.refs_2_
  110.6 0.5 collective-permute-done.20.refs_1_
  111.1 3.0 %step.11 = (bf16[128,768]{1,0:T(8,128)(2,1)S(1)}, bf16[64,768]{1,0:T(8,128)(2,1)}, bf16[64,768]{1,0:T(8,128)(2,1)}) custom-call(s32[5]{0:T(128)S(1)} %stack.28.scalars, bf16[64,768]{1,0:T(8,128)(2,1)S(1)} %collective-permute-done.19.refs_0_, bf16[128,768]{1,0:T(8,128)(2,1)S(1)} %collective-permute-done.20.refs_1_, ...), custom_call_target="tpu_custom_call" | custom-call | tf_op jit(solution)/shard_map/step/pallas_call | solution.py:237
  114.1 0.9 split.1
  115.0 4.5 %collective-permute-start.22 = (bf16[64,768]{1,0:T(8,128)(2,1)S(1)}, bf16[64,768]{1,0:T(8,128)(2,1)S(1)}, u32[]{:S(2)}, u32[]{:S(2)}) collective-permute-start(bf16[64,768]{1,0:T(8,128)(2,1)S(1)} %get-tuple-element.73), channel_id=1, source_target_pairs={{0,6},{1,7},{2,8},{3,9},{4,10},{5,11},{6,0},{7,1},{8,2},{9,3},{10,... | collective-permute-start | bytes 294920 | tf_op jit(solution)/shard_map/last_exchange/ppermute | solution.py:265
  119.5 1.3 collective-permute-start.23
  120.8 10.5 %collective-permute-start.24 = (bf16[64,768]{1,0:T(8,128)(2,1)S(1)}, bf16[64,768]{1,0:T(8,128)(2,1)S(1)}, u32[]{:S(2)}, u32[]{:S(2)}) collective-permute-start(bf16[64,768]{1,0:T(8,128)(2,1)S(1)} %get-tuple-element.74), channel_id=1, source_target_pairs={{18,6},{19,7},{20,8},{21,9},{22,10},{23,11},{30,18},{31,19},{32,20... | collective-permute-start | bytes 294920 | tf_op jit(solution)/shard_map/last_exchange/ppermute | solution.py:265
  131.4 1.8 %collective-permute-done.24.near1 = bf16[64,768]{1,0:T(8,128)(2,1)S(1)} collective-permute-done((bf16[64,768]{1,0:T(8,128)(2,1)S(1)}, bf16[64,768]{1,0:T(8,128)(2,1)S(1)}, u32[]{:S(2)}, u32[]{:S(2)}) %collective-permute-start.24) | collective-permute-done | bytes 98336 | tf_op jit(solution)/shard_map/last_exchange/ppermute | solution.py:265
  133.2 1.4 %merge.1 = f32[2,64,768]{2,1,0:T(8,128)} custom-call(s32[5]{0:T(128)S(1)} %stack.28.scalars, bf16[64,768]{1,0:T(8,128)(2,1)S(1)} %get-tuple-element.72.own, bf16[64,768]{1,0:T(8,128)(2,1)S(1)} %collective-permute-done.22.other, bf16[64,768]{1,0:T(8,128)(2,1)S(1)} %collective-permute-done.23.near0, bf16[64,768]{1,0:T(8,128)(2,1)S(1)} %collective-permute-done.24.near1), custom_call_target="tpu_custom_call" | custom-call | tf_op jit(solution)/shard_map/merge/pallas_call | solution.py:329
  (37 shorter events, 0.2 us)
Async XLA Ops:
  0.0 1.1 copy-start.7
  0.0 1.2 copy-start.4
  0.0 1.2 copy-start.6
  1.3 0.7 copy-start.5
  2.0 10.6 %copy-start.1 = (bf16[1,768,384]{2,1,0:T(8,128)(2,1)S(1)}, bf16[1,768,384]{2,1,0:T(8,128)(2,1)}, u32[]{:S(2)}) copy-start(bf16[1,768,384]{2,1,0:T(8,128)(2,1)} %param.15) | copy-start | bytes 1769476
  2.0 10.6 %copy-start.2 = (bf16[1,768,384]{2,1,0:T(8,128)(2,1)S(1)}, bf16[1,768,384]{2,1,0:T(8,128)(2,1)}, u32[]{:S(2)}) copy-start(bf16[1,768,384]{2,1,0:T(8,128)(2,1)} %param.16) | copy-start | bytes 1769476
  2.9 9.7 %copy-start = (bf16[1,768,384]{2,1,0:T(8,128)(2,1)S(1)}, bf16[1,768,384]{2,1,0:T(8,128)(2,1)}, u32[]{:S(2)}) copy-start(bf16[1,768,384]{2,1,0:T(8,128)(2,1)} %param.14) | copy-start | bytes 1769476
  2.9 9.7 %collective-permute-start.1 = (bf16[3,64,768]{2,1,0:T(8,128)(2,1)}, bf16[3,64,768]{2,1,0:T(8,128)(2,1)S(1)}, u32[]{:S(2)}, u32[]{:S(2)}) collective-permute-start(bf16[3,64,768]{2,1,0:T(8,128)(2,1)} %get-tuple-element.77), channel_id=1, source_target_pairs={{5,11},{11,5},{17,23},{23,17},{29,35},{35,29},{41,47},{47,41},{53,... | collective-permute-start | bytes 884744 | tf_op jit(solution)/shard_map/first_exchange/ppermute | solution.py:265
  3.7 8.9 %collective-permute-start.2 = (bf16[3,64,768]{2,1,0:T(8,128)(2,1)}, bf16[3,64,768]{2,1,0:T(8,128)(2,1)S(1)}, u32[]{:S(2)}, u32[]{:S(2)}) collective-permute-start(bf16[3,64,768]{2,1,0:T(8,128)(2,1)} %get-tuple-element.76), channel_id=1, source_target_pairs={{11,17},{23,29},{35,41},{47,53},{59,65},{71,77},{83,89},{95,101},{... | collective-permute-start | bytes 884744 | tf_op jit(solution)/shard_map/first_exchange/ppermute | solution.py:265
  4.4 8.2 %collective-permute-start.3 = (bf16[3,64,768]{2,1,0:T(8,128)(2,1)}, bf16[3,64,768]{2,1,0:T(8,128)(2,1)}, u32[]{:S(2)}, u32[]{:S(2)}) collective-permute-start(bf16[3,64,768]{2,1,0:T(8,128)(2,1)} %get-tuple-element.75), channel_id=1, source_target_pairs={{11,23},{23,35},{35,47},{47,59},{59,71},{71,83},{83,95},{95,107},{... | collective-permute-start | bytes 884744 | tf_op jit(solution)/shard_map/first_exchange/ppermute | solution.py:265
  5.8 6.0 %collective-permute-start = (s32[1]{0:T(128)}, s32[1]{0:T(128)}, u32[]{:S(2)}, u32[]{:S(2)}) collective-permute-start(s32[1]{0:T(128)} %param.12), channel_id=1, source_target_pairs={{1,0},{2,1},{3,2},{4,3},{5,4},{7,6},{8,7},{9,8},{10,9},{11,10},{13... | collective-permute-start | bytes 20 | tf_op jit(solution)/shard_map/first_exchange/ppermute | solution.py:284
  15.4 15.4 %copy-start.3 = (bf16[1,384,768]{2,1,0:T(8,128)(2,1)S(1)}, bf16[1,384,768]{2,1,0:T(8,128)(2,1)}, u32[]{:S(2)}) copy-start(bf16[1,384,768]{2,1,0:T(8,128)(2,1)} %param.17) | copy-start | bytes 1769476
  15.5 19.1 %collective-permute-start.7 = (bf16[2,64,768]{2,1,0:T(8,128)(2,1)S(1)}, bf16[2,64,768]{2,1,0:T(8,128)(2,1)S(1)}, u32[]{:S(2)}, u32[]{:S(2)}) collective-permute-start(bf16[2,64,768]{2,1,0:T(8,128)(2,1)S(1)} %get-tuple-element.80), channel_id=1, source_target_pairs={{0,6},{1,7},{2,8},{3,9},{4,10},{6,0},{7,1},{8,2},{9,3},{10,4},{12,... | collective-permute-start | bytes 589832 | tf_op jit(solution)/shard_map/later_exchange/ppermute | solution.py:265
  27.6 7.7 %collective-permute-start.8 = (bf16[2,64,768]{2,1,0:T(8,128)(2,1)S(1)}, bf16[2,64,768]{2,1,0:T(8,128)(2,1)S(1)}, u32[]{:S(2)}, u32[]{:S(2)}) collective-permute-start(bf16[2,64,768]{2,1,0:T(8,128)(2,1)S(1)} %get-tuple-element.79), channel_id=1, source_target_pairs={{6,12},{7,13},{8,14},{9,15},{10,16},{18,24},{19,25},{20,26},{21,27... | collective-permute-start | bytes 589832 | tf_op jit(solution)/shard_map/later_exchange/ppermute | solution.py:265
  28.9 19.9 %collective-permute-start.9 = (bf16[2,64,768]{2,1,0:T(8,128)(2,1)S(1)}, bf16[2,64,768]{2,1,0:T(8,128)(2,1)S(1)}, u32[]{:S(2)}, u32[]{:S(2)}) collective-permute-start(bf16[2,64,768]{2,1,0:T(8,128)(2,1)S(1)} %get-tuple-element.78), channel_id=1, source_target_pairs={{6,18},{7,19},{8,20},{9,21},{10,22},{18,30},{19,31},{20,32},{21,33... | collective-permute-start | bytes 589832 | tf_op jit(solution)/shard_map/later_exchange/ppermute | solution.py:265
  33.2 17.9 %collective-permute-start.5 = (bf16[128,768]{1,0:T(8,128)(2,1)S(1)}, bf16[128,768]{1,0:T(8,128)(2,1)S(1)}, u32[]{:S(2)}, u32[]{:S(2)}) collective-permute-start(bf16[128,768]{1,0:T(8,128)(2,1)S(1)} %get-tuple-element.48.refs_0_), channel_id=1, source_target_pairs={{5,4},{11,10},{17,16},{23,22},{29,28},{35,34},{41,40},{47,46},{53,... | collective-permute-start | bytes 589832 | tf_op jit(solution)/shard_map/pass_on/ppermute | solution.py:265
  33.9 17.2 %collective-permute-start.4 = (bf16[64,768]{1,0:T(8,128)(2,1)S(1)}, bf16[64,768]{1,0:T(8,128)(2,1)S(1)}, u32[]{:S(2)}, u32[]{:S(2)}) collective-permute-start(bf16[64,768]{1,0:T(8,128)(2,1)S(1)} %get-tuple-element.49), channel_id=1, source_target_pairs={{761,4},{767,10},{5,16},{11,22},{17,28},{23,34},{29,40},{35,46},{4... | collective-permute-start | bytes 294920 | tf_op jit(solution)/shard_map/pass_on/ppermute | solution.py:265
  34.6 16.5 %collective-permute-start.6 = (bf16[64,768]{1,0:T(8,128)(2,1)S(1)}, bf16[64,768]{1,0:T(8,128)(2,1)S(1)}, u32[]{:S(2)}, u32[]{:S(2)}) collective-permute-start(bf16[64,768]{1,0:T(8,128)(2,1)S(1)} %get-tuple-element.50), channel_id=1, source_target_pairs={{17,4},{23,10},{29,16},{35,22},{41,28},{47,34},{53,40},{59,46},{65... | collective-permute-start | bytes 294920 | tf_op jit(solution)/shard_map/pass_on/ppermute | solution.py:265
  53.6 2.1 %collective-permute-start.11 = (bf16[128,768]{1,0:T(8,128)(2,1)S(1)}, bf16[128,768]{1,0:T(8,128)(2,1)S(1)}, u32[]{:S(2)}, u32[]{:S(2)}) collective-permute-start(bf16[128,768]{1,0:T(8,128)(2,1)S(1)} %get-tuple-element.59.refs_1_), channel_id=1, source_target_pairs={{4,3},{10,9},{16,15},{22,21},{28,27},{34,33},{40,39},{46,45},{52,5... | collective-permute-start | bytes 589832 | tf_op jit(solution)/shard_map/pass_on/ppermute | solution.py:265
  54.2 1.4 %collective-permute-start.10 = (bf16[64,768]{1,0:T(8,128)(2,1)S(1)}, bf16[64,768]{1,0:T(8,128)(2,1)S(1)}, u32[]{:S(2)}, u32[]{:S(2)}) collective-permute-start(bf16[64,768]{1,0:T(8,128)(2,1)S(1)} %get-tuple-element.60), channel_id=1, source_target_pairs={{760,3},{766,9},{4,15},{10,21},{16,27},{22,33},{28,39},{34,45},{40... | collective-permute-start | bytes 294920 | tf_op jit(solution)/shard_map/pass_on/ppermute | solution.py:265
  54.9 0.7 collective-permute-start.12
  58.0 2.1 %collective-permute-start.14 = (bf16[128,768]{1,0:T(8,128)(2,1)S(1)}, bf16[128,768]{1,0:T(8,128)(2,1)S(1)}, u32[]{:S(2)}, u32[]{:S(2)}) collective-permute-start(bf16[128,768]{1,0:T(8,128)(2,1)S(1)} %get-tuple-element.62.refs_2_), channel_id=1, source_target_pairs={{3,2},{9,8},{15,14},{21,20},{27,26},{33,32},{39,38},{45,44},{51,50... | collective-permute-start | bytes 589832 | tf_op jit(solution)/shard_map/pass_on/ppermute | solution.py:265
  58.7 1.4 %collective-permute-start.13 = (bf16[64,768]{1,0:T(8,128)(2,1)S(1)}, bf16[64,768]{1,0:T(8,128)(2,1)S(1)}, u32[]{:S(2)}, u32[]{:S(2)}) collective-permute-start(bf16[64,768]{1,0:T(8,128)(2,1)S(1)} %get-tuple-element.63), channel_id=1, source_target_pairs={{759,2},{765,8},{3,14},{9,20},{15,26},{21,32},{27,38},{33,44},{39,... | collective-permute-start | bytes 294920 | tf_op jit(solution)/shard_map/pass_on/ppermute | solution.py:265
  59.4 0.7 collective-permute-start.15
  62.5 2.1 %collective-permute-start.17 = (bf16[128,768]{1,0:T(8,128)(2,1)S(1)}, bf16[128,768]{1,0:T(8,128)(2,1)S(1)}, u32[]{:S(2)}, u32[]{:S(2)}) collective-permute-start(bf16[128,768]{1,0:T(8,128)(2,1)S(1)} %get-tuple-element.65.refs_3_), channel_id=1, source_target_pairs={{2,1},{8,7},{14,13},{20,19},{26,25},{32,31},{38,37},{44,43},{50,49... | collective-permute-start | bytes 589832 | tf_op jit(solution)/shard_map/pass_on/ppermute | solution.py:265
  63.2 1.4 %collective-permute-start.16 = (bf16[64,768]{1,0:T(8,128)(2,1)S(1)}, bf16[64,768]{1,0:T(8,128)(2,1)S(1)}, u32[]{:S(2)}, u32[]{:S(2)}) collective-permute-start(bf16[64,768]{1,0:T(8,128)(2,1)S(1)} %get-tuple-element.66), channel_id=1, source_target_pairs={{758,1},{764,7},{2,13},{8,19},{14,25},{20,31},{26,37},{32,43},{38,... | collective-permute-start | bytes 294920 | tf_op jit(solution)/shard_map/pass_on/ppermute | solution.py:265
  63.8 0.7 collective-permute-start.18
  66.9 44.2 %collective-permute-start.20 = (bf16[128,768]{1,0:T(8,128)(2,1)S(1)}, bf16[128,768]{1,0:T(8,128)(2,1)S(1)}, u32[]{:S(2)}, u32[]{:S(2)}) collective-permute-start(bf16[128,768]{1,0:T(8,128)(2,1)S(1)} %get-tuple-element.68.refs_4_), channel_id=1, source_target_pairs={{1,0},{7,6},{13,12},{19,18},{25,24},{31,30},{37,36},{43,42},{49,48... | collective-permute-start | bytes 589832 | tf_op jit(solution)/shard_map/pass_on/ppermute | solution.py:265
  68.2 42.1 %collective-permute-start.19 = (bf16[64,768]{1,0:T(8,128)(2,1)S(1)}, bf16[64,768]{1,0:T(8,128)(2,1)S(1)}, u32[]{:S(2)}, u32[]{:S(2)}) collective-permute-start(bf16[64,768]{1,0:T(8,128)(2,1)S(1)} %get-tuple-element.69), channel_id=1, source_target_pairs={{757,0},{763,6},{1,12},{7,18},{13,24},{19,30},{25,36},{31,42},{37,... | collective-permute-start | bytes 294920 | tf_op jit(solution)/shard_map/pass_on/ppermute | solution.py:265
  69.5 41.1 %collective-permute-start.21 = (bf16[64,768]{1,0:T(8,128)(2,1)S(1)}, bf16[64,768]{1,0:T(8,128)(2,1)S(1)}, u32[]{:S(2)}, u32[]{:S(2)}) collective-permute-start(bf16[64,768]{1,0:T(8,128)(2,1)S(1)} %get-tuple-element.70), channel_id=1, source_target_pairs={{13,0},{19,6},{25,12},{31,18},{37,24},{43,30},{49,36},{55,42},{61,... | collective-permute-start | bytes 294920 | tf_op jit(solution)/shard_map/pass_on/ppermute | solution.py:265
  115.0 16.3 %collective-permute-start.22 = (bf16[64,768]{1,0:T(8,128)(2,1)S(1)}, bf16[64,768]{1,0:T(8,128)(2,1)S(1)}, u32[]{:S(2)}, u32[]{:S(2)}) collective-permute-start(bf16[64,768]{1,0:T(8,128)(2,1)S(1)} %get-tuple-element.73), channel_id=1, source_target_pairs={{0,6},{1,7},{2,8},{3,9},{4,10},{5,11},{6,0},{7,1},{8,2},{9,3},{10,... | collective-permute-start | bytes 294920 | tf_op jit(solution)/shard_map/last_exchange/ppermute | solution.py:265
  119.5 11.9 %collective-permute-start.23 = (bf16[64,768]{1,0:T(8,128)(2,1)S(1)}, bf16[64,768]{1,0:T(8,128)(2,1)S(1)}, u32[]{:S(2)}, u32[]{:S(2)}) collective-permute-start(bf16[64,768]{1,0:T(8,128)(2,1)S(1)} %get-tuple-element.74), channel_id=1, source_target_pairs={{12,6},{13,7},{14,8},{15,9},{16,10},{17,11},{24,18},{25,19},{26,20... | collective-permute-start | bytes 294920 | tf_op jit(solution)/shard_map/last_exchange/ppermute | solution.py:265
  120.8 12.4 %collective-permute-start.24 = (bf16[64,768]{1,0:T(8,128)(2,1)S(1)}, bf16[64,768]{1,0:T(8,128)(2,1)S(1)}, u32[]{:S(2)}, u32[]{:S(2)}) collective-permute-start(bf16[64,768]{1,0:T(8,128)(2,1)S(1)} %get-tuple-element.74), channel_id=1, source_target_pairs={{18,6},{19,7},{20,8},{21,9},{22,10},{23,11},{30,18},{31,19},{32,20... | collective-permute-start | bytes 294920 | tf_op jit(solution)/shard_map/last_exchange/ppermute | solution.py:265

commit v2 on v1

v2 whole, which is shorter than its diff:
```python
import functools

import jax
import jax.numpy as jnp
from jax import lax
from jax.experimental import pallas as pl
from jax.experimental.pallas import tpu as pltpu
from jax.sharding import PartitionSpec as P

HD = 32
WIN = 8
AXES = ("lat", "section")
FLT = jnp.float32
BF = jnp.bfloat16
BAND = 64
SLOT = 128
GROUP = 4


def dot_nn(a, b):
    return lax.dot_general(a, b, (((1,), (0,)), ((), ())), preferred_element_type=FLT)


def dot_nt(a, b):
    return lax.dot_general(a, b, (((1,), (1,)), ((), ())), preferred_element_type=FLT)


def near_of(core, near0, near1, field):
    return jnp.where(core == 0, near0[field].astype(FLT), near1[field].astype(FLT))


def gathered(rows, field, core, offset, own, other, near0, near1):
    rows[0:BAND, :] = near_of(core, near0, near1, field)
    rows[pl.ds(pl.multiple_of(BAND + BAND * core, BAND), BAND), :] = own[core, field].astype(FLT)
    rows[pl.ds(pl.multiple_of(2 * BAND - BAND * core, BAND), BAND), :] = other[field].astype(FLT)
    return rows[pl.ds(pl.multiple_of(offset * WIN, WIN), SLOT), :]


def gathered_above(rows, core, offset, own, other, next0, next1):
    rows[0:BAND, :] = jnp.where(core == 1, own[core, 0].astype(FLT), other[0].astype(FLT))
    rows[BAND : 2 * BAND, :] = near_of(core, next0, next1, 0)
    rows[2 * BAND :, :] = jnp.zeros_like(rows[2 * BAND :, :])
    return rows[pl.ds(pl.multiple_of(offset * WIN, WIN), SLOT), :]


def prepare_kernel(
    above,
    with_forcing,
    edge_slot,
    scalars,
    own,
    other,
    near0,
    near1,
    w_query,
    w_key,
    w_value,
    attend_ref,
    attend_t_ref,
    value_ref,
    key_ref,
    query_t_ref,
    out_ref,
    *rest,
):
    rows = rest[-1]
    core, slot, offset = scalars[0], scalars[1], scalars[2]
    if above:
        x = gathered_above(rows, core, offset, own, other, near0, near1).astype(BF)
    else:
        x = gathered(rows, 0, core, offset, own, other, near0, near1).astype(BF)
    if with_forcing:
        rest[0][...] = gathered(rows, 1, core, offset, own, other, near0, near1).astype(BF)
    scale = HD ** (-0.5)
    q = (dot_nn(x, w_query[...]) * scale).astype(BF)
    k = dot_nn(x, w_key[...]).astype(BF)
    v = dot_nn(x, w_value[...]).astype(BF)
    token = lax.broadcasted_iota(jnp.int32, (SLOT, SLOT), 0)
    other_token = lax.broadcasted_iota(jnp.int32, (SLOT, SLOT), 1)
    row_head = token // HD
    lane_head = other_token // HD
    edge = jnp.where(slot == edge_slot, BAND - offset * WIN, 0)
    allowed = ((token // BAND) == (other_token // BAND)) & (
        (token < edge) == (other_token < edge)
    )
    for group in range(3):
        lanes = slice(SLOT * group, SLOT * group + SLOT)
        q_g, k_g, v_g = q[:, lanes], k[:, lanes], v[:, lanes]
        q_t = q_g.astype(FLT).T
        k_t = k_g.astype(FLT).T
        v_t = v_g.astype(FLT).T
        mixed = jnp.zeros((SLOT, SLOT), FLT)
        for h in range(GROUP):
            at = slice(SLOT * h, SLOT * h + SLOT)
            wide = slice(SLOT * (GROUP * group + h), SLOT * (GROUP * group + h) + SLOT)
            in_rows = row_head == h
            in_lanes = lane_head == h
            scores = dot_nn(q_g, jnp.where(in_rows, k_t, 0.0).astype(BF))
            scores = jnp.where(allowed, scores, -1000000000.0)
            scores = scores - jnp.max(scores, axis=-1, keepdims=True)
            expon = jnp.exp(scores)
            attend = expon / jnp.sum(expon, axis=-1, keepdims=True)
            attend_b = attend.astype(BF)
            attend_ref[:, wide] = attend_b
            attend_t_ref[:, wide] = attend.T.astype(BF)
            mixed += dot_nn(attend_b, jnp.where(in_lanes, v_g, jnp.zeros_like(v_g)))
            value_ref[group, 0:SLOT, at] = jnp.where(in_rows, v_t, 0.0).astype(BF)
            value_ref[group, SLOT : 2 * SLOT, at] = jnp.where(in_rows, -1.0, 0.0).astype(BF)
            key_ref[group, at, :] = jnp.where(in_lanes, k_g, jnp.zeros_like(k_g))
            query_t_ref[group, :, at] = jnp.where(in_rows, q_t, 0.0).astype(BF)
        out_ref[:, lanes] = mixed


def changed(adjoint, units, w_query, w_key, w_value, w_out):
    scale = HD ** (-0.5)
    g = dot_nt(adjoint.astype(BF), w_out[...]).astype(BF)
    lane_head = lax.broadcasted_iota(jnp.int32, (SLOT, SLOT), 1) // HD
    g_query, g_key, g_value = [], [], []
    for unit, (attend, attend_t, values, keys, queries_t, out) in enumerate(units):
        tokens = slice(SLOT * unit, SLOT * unit + SLOT)
        for group in range(3):
            lanes = slice(SLOT * group, SLOT * group + SLOT)
            wide = slice(GROUP * SLOT * group, GROUP * SLOT * (group + 1))
            g_g = g[tokens, lanes]
            g_o = (g_g.astype(FLT) * out[:, lanes]).astype(BF)
            centred = dot_nn(jnp.concatenate([g_g, g_o], axis=1), values[group])
            g_s = (attend[:, wide].astype(FLT) * centred).astype(BF)
            g_query.append((dot_nn(g_s, keys[group]) * scale).astype(BF))
            stacked = jnp.concatenate(
                [g_s[:, SLOT * h : SLOT * h + SLOT] for h in range(GROUP)], axis=0
            )
            g_key.append(dot_nn(queries_t[group], stacked).T.astype(BF))
            spread = jnp.concatenate(
                [jnp.where(lane_head == h, g_g, jnp.zeros_like(g_g)) for h in range(GROUP)],
                axis=0,
            )
            g_value.append(dot_nn(attend_t[:, wide], spread).astype(BF))

    def whole(parts):
        slots = [jnp.concatenate(parts[3 * u : 3 * u + 3], axis=1) for u in range(len(units))]
        return jnp.concatenate(slots, axis=0)

    change = dot_nt(whole(g_query), w_query[...])
    change += dot_nt(whole(g_key), w_key[...])
    change += dot_nt(whole(g_value), w_value[...])
    return change


def first_kernel(scalars, own, other, near0, near1, *refs):
    prepared, weights = refs[:6], refs[6:10]
    all_ref, low_ref, high_ref, rows = refs[10:]
    core, offset = scalars[0], scalars[2]
    adjoint = gathered(rows, 0, core, offset, own, other, near0, near1)
    forcing = gathered(rows, 1, core, offset, own, other, near0, near1)
    updated = (adjoint + changed(adjoint, [prepared], *weights) + forcing).astype(BF)
    all_ref[...] = updated
    low_ref[...] = updated[:BAND]
    high_ref[...] = updated[BAND:]


def step_kernel(scalars, low, middle, high, *refs):
    prepared, forcing, weights = refs[:6], refs[6], refs[7:11]
    all_ref, low_ref, high_ref, rows = refs[11:]
    rows[0:BAND, :] = low[...].astype(FLT)
    rows[BAND : BAND + SLOT, :] = middle[...].astype(FLT)
    rows[BAND + SLOT :, :] = high[...].astype(FLT)
    shift = scalars[4]
    adjoint = rows[pl.ds(pl.multiple_of(BAND + shift * WIN, WIN), SLOT), :]
    change = changed(adjoint, [prepared], *weights)
    updated = (adjoint + change + forcing[...].astype(FLT)).astype(BF)
    all_ref[...] = updated
    low_ref[...] = updated[:BAND]
    high_ref[...] = updated[BAND:]


def last_kernel(scalars, low, middle, high, *refs):
    units, weights = [refs[:6], refs[6:12]], refs[12:16]
    own_ref, swap_ref, rows = refs[16:]
    rows[0:BAND, :] = low[...].astype(FLT)
    rows[BAND : BAND + SLOT, :] = middle[...].astype(FLT)
    rows[BAND + SLOT : BAND + 2 * SLOT, :] = high[...].astype(FLT)
    rows[BAND + 2 * SLOT :, :] = jnp.zeros_like(rows[BAND + 2 * SLOT :, :])
    core, offset, shift = scalars[0], scalars[2], scalars[4]
    adjoint = rows[pl.ds(pl.multiple_of(BAND + shift * WIN, WIN), 2 * SLOT), :]
    rows[0 : 2 * SLOT, :] = adjoint + changed(adjoint, units, *weights)
    even = rows[pl.ds(pl.multiple_of(BAND - offset * WIN, WIN), BAND), :].astype(BF)
    odd = rows[pl.ds(pl.multiple_of(2 * BAND - offset * WIN, WIN), BAND), :].astype(BF)
    own_ref[...] = jnp.where(core == 0, even, odd)
    swap_ref[...] = jnp.where(core == 0, odd, even)


def split_kernel(scalars, *refs):
    results = refs[:-6]
    own_ref, swap_ref, lower_ref, held, rows, sem = refs[-6:]
    core, offset, section = scalars[0], scalars[2], scalars[3]
    for tick, result in enumerate(results):

        @pl.when(section == len(results) - tick)
        def _():
            copy = pltpu.make_async_copy(result, held, sem)
            copy.start()
            copy.wait()

    lower_ref[...] = held[0:BAND]
    rows[...] = held[...].astype(FLT)
    even = rows[pl.ds(pl.multiple_of(BAND - offset * WIN, WIN), BAND), :].astype(BF)
    odd = held[BAND:SLOT]
    own_ref[...] = jnp.where(core == 0, even, odd)
    swap_ref[...] = jnp.where(core == 0, odd, even)


def merge_kernel(
    scalars, own, other, near0, near1, own_last, other_last, forcing, result, rows
):
    core, offset, section = scalars[0], scalars[2], scalars[3]

    @pl.when(section == 0)
    def _():
        for member in range(2):
            mine = jnp.where(
                core == member, own_last[...].astype(FLT), other_last[...].astype(FLT)
            )
            result[member] = mine + forcing[member].astype(FLT)

    @pl.when(section != 0)
    def _():
        for member, near in ((0, near0), (1, near1)):
            rows[0:BAND, :] = jnp.where(
                core == member, own[...].astype(FLT), other[...].astype(FLT)
            )
            rows[BAND:SLOT, :] = near[...].astype(FLT)
            start = jnp.where(core == 1, BAND - offset * WIN, 0)
            result[member] = rows[pl.ds(pl.multiple_of(start, WIN), BAND), :]


def struct(shape, kind=BF):
    return jax.ShapeDtypeStruct(shape, kind)


SMEM = pl.BlockSpec(memory_space=pltpu.SMEM)
VMEM = pl.BlockSpec(memory_space=pltpu.VMEM)
ANY = pl.BlockSpec(memory_space=pl.ANY)


def call(name, kernel, scalars, operands, shapes, scratch, place=VMEM):
    return pl.pallas_call(
        kernel,
        out_shape=shapes,
        in_specs=[SMEM] + [place] * len(operands),
        out_specs=[VMEM] * len(shapes),
        scratch_shapes=scratch,
        compiler_params=pltpu.CompilerParams(vmem_limit_bytes=40 * 1024 * 1024),
        name=name,
    )(scalars, *operands)


def prepare(scalars, operands, weights, edge_slot, above=False, with_forcing=False):
    width, hidden = weights[0].shape
    keys = hidden // HD * SLOT
    shapes = [
        struct((SLOT, keys)),
        struct((SLOT, keys)),
        struct((3, 2 * SLOT, GROUP * SLOT)),
        struct((3, GROUP * SLOT, SLOT)),
        struct((3, SLOT, GROUP * SLOT)),
        struct((SLOT, hidden), FLT),
    ]
    if with_forcing:
        shapes.append(struct((SLOT, width)))
    return call(
        "prepare",
        functools.partial(prepare_kernel, above, with_forcing, edge_slot),
        scalars,
        (*operands, *weights[:3]),
        shapes,
        [pltpu.VMEM((3 * BAND, width), FLT)],
    )


def on_device(
    trajectory, observed, obs_mask, shift_rows, final_adjoint, w_query, w_key, w_value, w_out
):
    sections = lax.axis_size("section")
    bands = lax.axis_size("lat")
    chips = bands // 2
    section_at = lax.axis_index("section")
    band_at = lax.axis_index("lat")
    members, rows_here, across, width = trajectory.shape[1:]
    offset = shift_rows[0].astype(jnp.int32)
    core, chip = band_at % 2, band_at // 2
    weights = (w_query[0], w_key[0], w_value[0], w_out[0])

    def at(band, section):
        return (band % bands) * sections + section

    def sent(value, hops):
        return lax.ppermute(value, AXES, hops)

    def moved(ways, among):
        return [(at(a, s), at(b, s)) for a, b in ways for s in among]

    def exchange(fields, among):
        near0 = sent(fields[0], moved([(2 * j + 1, 2 * j + 2) for j in range(chips)], among))
        near1 = sent(fields[1], moved([(2 * j + 1, 2 * j + 3) for j in range(chips)], among))
        other = sent(
            lax.dynamic_index_in_dim(fields, 1 - core, 0, keepdims=False),
            moved([(b, b ^ 1) for b in range(bands)], among),
        )
        return other, near0, near1

    def flat(values):
        return values.reshape(members, 1, BAND, width)

    def ints(*values):
        return jnp.stack(values).astype(jnp.int32)

    final_section = [sections - 1]
    x = flat(trajectory[0])
    with jax.named_scope("first_states"):
        first_x = exchange(x, final_section)
    weight = obs_mask[0].reshape(1, 1, BAND, 1).astype(FLT)
    forcing = (weight * (x.astype(FLT) - flat(observed[0]).astype(FLT))).astype(BF)
    final = flat(final_adjoint).astype(BF)
    with jax.named_scope("first_adjoint"):
        begin = jnp.concatenate([final, forcing], axis=1)
        begin, _ = lax.optimization_barrier((begin, first_x[0]))
        first_begin = exchange(begin, final_section)
    with jax.named_scope("shifts"):
        down = [(s, s - 1) for s in range(1, sections)]
        above = lax.ppermute(shift_rows, "section", down)[0].astype(jnp.int32)
    shift = jnp.where(section_at == sections - 1, 0, offset - above)
    place = ints(core, chip, offset, section_at, shift)

    prepared = prepare(place, (x, *first_x), weights, 0)
    result = call(
        "first_step",
        first_kernel,
        place,
        (begin, *first_begin, *prepared, *weights),
        [struct((SLOT, width)), struct((BAND, width)), struct((BAND, width))],
        [pltpu.VMEM((3 * BAND, width), FLT)],
    )
    results = [result[0]]
    with jax.named_scope("later_states"):
        pair = jnp.concatenate([x, forcing], axis=1)
        pair, _ = lax.optimization_barrier((pair, prepared[0]))
        later = exchange(pair, list(range(sections - 1)))
    *prepared, forcing_here = prepare(place, (pair, *later), weights, 0, with_forcing=True)
    for tick in range(1, sections):
        source = sections - tick
        whole, low, high = result

        def across_from(way):
            return [(at(b + 2 * way, source), at(b, source - 1)) for b in range(bands)]

        with jax.named_scope("pass_on"):
            if tick == sections - 1:
                from_low = sent(high, across_from(-1))
                from_high = sent(whole, across_from(1))
                middle = sent(whole, across_from(0))
            else:
                from_low = sent(high, across_from(-1))
                from_high = sent(low, across_from(1))
                middle = sent(whole, across_from(0))
        if tick == sections - 1:
            break
        result = call(
            "step",
            step_kernel,
            place,
            (from_low, middle, from_high, *prepared, forcing_here, *weights),
            [struct((SLOT, width)), struct((BAND, width)), struct((BAND, width))],
            [pltpu.VMEM((4 * BAND, width), FLT)],
        )
        results.append(result[0])

    with jax.named_scope("window_above"):
        ups = [(2 * j + 2, 2 * j) for j in range(chips)], [(2 * j + 2, 2 * j + 1) for j in range(chips)]
        next0 = sent(x[0], moved(ups[0], [0]))
        next1 = sent(x[1], moved(ups[1], [0]))
        extra = prepare(place, (pair, later[0], next0, next1), weights, chips - 1, above=True)
    own, swap, lower = call(
        "split",
        split_kernel,
        place,
        results,
        [struct((BAND, width))] * 3,
        [
            pltpu.VMEM((SLOT, width), BF),
            pltpu.VMEM((SLOT, width), FLT),
            pltpu.SemaphoreType.DMA,
        ],
        place=ANY,
    )
    with jax.named_scope("earlier_results"):
        every = range(1, sections)
        near0 = sent(lower, moved([(2 * j + 2, 2 * j + 1) for j in range(chips)], every))
        near1 = sent(lower, moved([(2 * j + 3, 2 * j + 1) for j in range(chips)], every))
        other = sent(swap, moved([(b, b ^ 1) for b in range(bands)], every))
    own_last, swap_last = call(
        "last_step",
        last_kernel,
        place,
        (from_low, middle, from_high, *prepared, *extra, *weights),
        [struct((BAND, width))] * 2,
        [pltpu.VMEM((6 * BAND, width), FLT)],
    )
    with jax.named_scope("last_result"):
        other_last = sent(swap_last, moved([(b, b ^ 1) for b in range(bands)], [0]))
    (field,) = call(
        "merge",
        merge_kernel,
        place,
        (own, other, near0, near1, own_last, other_last, forcing.reshape(members, BAND, width)),
        [struct((members, BAND, width), FLT)],
        [pltpu.VMEM((SLOT, width), FLT)],
    )
    return field.reshape(1, members, rows_here, across, width)


def solution(mesh):
    placed = (
        P("section", None, "lat", None, None),
        P("section", None, "lat", None, None),
        P("section", "lat", None),
        P("section"),
        P(None, "lat", None, None),
        P("section", None, None),
        P("section", None, None),
        P("section", None, None),
        P("section", None, None),
    )
    return jax.shard_map(
        on_device,
        mesh=mesh,
        in_specs=placed,
        out_specs=P("section", None, "lat", None, None),
        check_vma=False,
    )
```

time: 135 us -> 133 us (0.985); the launches traced: 135 us -> 131 us
  starting transfers between devices: 47.6 us -> 39.3 us
  waiting for transfers between devices: 58.8 us -> 62.1 us
  Pallas kernels: 22.4 us -> 24.5 us
  other arithmetic: 2.2 us -> 0.29 us
    ppermute x24 -> x30, starting transfers between devices: 46.4 us -> 37.9 us  [sent(): return lax.ppermute(value, AXES, hops)]
    ppermute x24 -> x30, waiting for transfers between devices: 55.7 us -> 62.1 us  [sent(): return lax.ppermute(value, AXES, hops)]
    ppermute x1, waiting for transfers between devices: 3.05 us -> 0.01 us  [on_device(): above = lax.ppermute(shift_rows, 'section', down)[0].astype(jnp.int32)]
    pallas_call x10 -> x11, Pallas kernels: 22.4 us -> 24.5 us  [call(): pl.pallas_call(kernel, out_shape=shapes, in_specs=[SMEM] + [place] * len(...]
  transfers between devices with their start and end apart: 25 -> 31, of which waited for: 6 -> 4; matrix products, arithmetic and copies ran while one was open for 1% -> 1% of each run, Pallas kernels for 3% -> 10%
where the time goes in v2:
time: 133 us; the launch traced here: 131 us
  waiting for transfers between devices  62.1 us (47%)
  starting transfers between devices  39.3 us (30%)
  Pallas kernels  24.5 us (18%)
  local copies, waits for them, and re-layouts  2.76 us (2%)
  between operations  2.06 us (2%)
    ppermute x30, waiting for transfers between devices, sent(): return lax.ppermute(value, AXES, hops)  62.1 us
    ppermute x30, starting transfers between devices, sent(): return lax.ppermute(value, AXES, hops)  37.9 us
    pallas_call x11, Pallas kernels, call(): pl.pallas_call(kernel, out_shape=shapes, in_specs=[SMEM] + [place] * len(...  24.5 us
  transfers between devices with their start and end apart: 31, of which 4 were waited for; matrix products, arithmetic and copies ran while one was open for 1% of the time, Pallas kernels for 10%

profile of v2, /device:TPU:1, one launch (start us, length us, event | category | flops | bytes accessed | tf_op | source)
XLA Modules:
  0.0 131.0 jit_solution(3365474447509022839)
XLA Ops:
  0.0 1.4 %collective-permute-start = (s32[1]{0:T(128)}, s32[1]{0:T(128)}, u32[]{:S(2)}, u32[]{:S(2)}) collective-permute-start(s32[1]{0:T(128)} %param.12), channel_id=1, source_target_pairs={{1,0},{2,1},{3,2},{4,3},{5,4},{7,6},{8,7},{9,8},{10,9},{11,10},{13... | collective-permute-start | bytes 20 | tf_op jit(solution)/shard_map/shifts/ppermute | solution.py:330
  1.4 0.9 dynamic-slice_bitcast_fusion.2
  2.3 0.7 collective-permute-start.1
  3.0 0.7 collective-permute-start.5
  3.7 0.7 collective-permute-start.6
  5.1 0.7 copy-done.7
  5.9 0.9 copy-done.5
  7.8 0.8 collective-permute-start.2
  8.7 0.7 collective-permute-start.3
  9.3 0.7 collective-permute-start.4
  10.1 2.2 %prepare.3 = (bf16[128,1536]{1,0:T(8,128)(2,1)S(1)}, bf16[128,1536]{1,0:T(8,128)(2,1)S(1)}, bf16[3,256,512]{2,1,0:T(8,128)(2,1)S(1)}, bf16[3,512,128]{2,1,0:T(8,...) custom-call(s32[5]{0:T(128)S(1)} %stack.19.scalars, bf16[2,1,64,768]{3,2,1,0:T(8,128)(2,1)S(1)} %bitcast.81, ...), custom_call_target="tpu_custom_call" | custom-call | tf_op jit(solution)/shard_map/prepare/pallas_call | solution.py:246
  12.3 12.6 %collective-permute-start.10 = (bf16[2,64,768]{2,1,0:T(8,128)(2,1)S(1)}, bf16[2,64,768]{2,1,0:T(8,128)(2,1)S(1)}, u32[]{:S(2)}, u32[]{:S(2)}) collective-permute-start(bf16[2,64,768]{2,1,0:T(8,128)(2,1)S(1)} %get-tuple-element.87), channel_id=1, source_target_pairs={{0,6},{1,7},{2,8},{3,9},{4,10},{6,0},{7,1},{8,2},{9,3},{10,4},{12,... | collective-permute-start | bytes 589832 | tf_op jit(solution)/shard_map/later_states/ppermute | solution.py:297
  24.9 1.3 collective-permute-start.11
  26.2 1.9 %collective-permute-start.12 = (bf16[2,64,768]{2,1,0:T(8,128)(2,1)S(1)}, bf16[2,64,768]{2,1,0:T(8,128)(2,1)S(1)}, u32[]{:S(2)}, u32[]{:S(2)}) collective-permute-start(bf16[2,64,768]{2,1,0:T(8,128)(2,1)S(1)} %get-tuple-element.85), channel_id=1, source_target_pairs={{6,18},{7,19},{8,20},{9,21},{10,22},{18,30},{19,31},{20,32},{21,33... | collective-permute-start | bytes 589832 | tf_op jit(solution)/shard_map/later_states/ppermute | solution.py:297
  28.2 2.4 %first_step.1 = (bf16[128,768]{1,0:T(8,128)(2,1)S(1)}, bf16[64,768]{1,0:T(8,128)(2,1)S(1)}, bf16[64,768]{1,0:T(8,128)(2,1)S(1)}) custom-call(s32[5]{0:T(128)S(1)} %stack.19.scalars, bf16[2,2,64,768]{3,2,1,0:T(8,128)(2,1)S(1)} %get-tuple-element.45.own, bf16[2,64,768]{2,1,0:T(8,128)(2,1)S(1)} %collective-permute-done.2.other, ...), custom_call_target="tpu_custom_call" | custom-call | tf_op jit(solution)/shard_map/first_step/pallas_call | solution.py:246
  30.6 0.7 collective-permute-start.8
  31.3 0.7 collective-permute-start.7
  31.9 0.7 collective-permute-start.9
  32.6 11.5 %collective-permute-done.12.near1 = bf16[2,64,768]{2,1,0:T(8,128)(2,1)S(1)} collective-permute-done((bf16[2,64,768]{2,1,0:T(8,128)(2,1)S(1)}, bf16[2,64,768]{2,1,0:T(8,128)(2,1)S(1)}, u32[]{:S(2)}, u32[]{:S(2)}) %collective-permute-start.12) | collective-permute-done | bytes 196640 | tf_op jit(solution)/shard_map/later_states/ppermute | solution.py:297
  44.1 2.3 %prepare.4 = (bf16[128,1536]{1,0:T(8,128)(2,1)S(1)}, bf16[128,1536]{1,0:T(8,128)(2,1)S(1)}, bf16[3,256,512]{2,1,0:T(8,128)(2,1)S(1)}, bf16[3,512,128]{2,1,0:T(8,...) custom-call(s32[5]{0:T(128)S(1)} %stack.19.scalars, ...), custom_call_target="tpu_custom_call" | custom-call | tf_op jit(solution)/shard_map/prepare/pallas_call | solution.py:246
  46.4 2.4 %step.4 = (bf16[128,768]{1,0:T(8,128)(2,1)S(1)}, bf16[64,768]{1,0:T(8,128)(2,1)S(1)}, bf16[64,768]{1,0:T(8,128)(2,1)S(1)}) custom-call(s32[5]{0:T(128)S(1)} %stack.19.scalars, bf16[64,768]{1,0:T(8,128)(2,1)S(1)} %collective-permute-done.7.low, bf16[128,768]{1,0:T(8,128)(2,1)S(1)} %collective-permute-done.8.middle, ...), custom_call_target="tpu_custom_call" | custom-call | tf_op jit(solution)/shard_map/step/pallas_call | solution.py:246
  48.8 0.7 collective-permute-start.14
  49.5 0.7 collective-permute-start.13
  50.2 0.7 collective-permute-start.15
  50.9 2.4 %step.5 = (bf16[128,768]{1,0:T(8,128)(2,1)S(1)}, bf16[64,768]{1,0:T(8,128)(2,1)S(1)}, bf16[64,768]{1,0:T(8,128)(2,1)S(1)}) custom-call(s32[5]{0:T(128)S(1)} %stack.19.scalars, bf16[64,768]{1,0:T(8,128)(2,1)S(1)} %collective-permute-done.13.low, bf16[128,768]{1,0:T(8,128)(2,1)S(1)} %collective-permute-done.14.middle, ...), custom_call_target="tpu_custom_call" | custom-call | tf_op jit(solution)/shard_map/step/pallas_call | solution.py:246
  53.3 0.7 collective-permute-start.17
  54.0 0.7 collective-permute-start.16
  54.6 0.7 collective-permute-start.18
  55.3 2.4 %step.6 = (bf16[128,768]{1,0:T(8,128)(2,1)S(1)}, bf16[64,768]{1,0:T(8,128)(2,1)S(1)}, bf16[64,768]{1,0:T(8,128)(2,1)S(1)}) custom-call(s32[5]{0:T(128)S(1)} %stack.19.scalars, bf16[64,768]{1,0:T(8,128)(2,1)S(1)} %collective-permute-done.16.low, bf16[128,768]{1,0:T(8,128)(2,1)S(1)} %collective-permute-done.17.middle, ...), custom_call_target="tpu_custom_call" | custom-call | tf_op jit(solution)/shard_map/step/pallas_call | solution.py:246
  57.7 0.7 collective-permute-start.20
  58.4 0.7 collective-permute-start.19
  59.1 0.7 collective-permute-start.21
  59.8 3.0 %step.7 = (bf16[128,768]{1,0:T(8,128)(2,1)S(1)}, bf16[64,768]{1,0:T(8,128)(2,1)}, bf16[64,768]{1,0:T(8,128)(2,1)S(1)}) custom-call(s32[5]{0:T(128)S(1)} %stack.19.scalars, bf16[64,768]{1,0:T(8,128)(2,1)S(1)} %collective-permute-done.19.low, bf16[128,768]{1,0:T(8,128)(2,1)S(1)} %collective-permute-done.20.middle, ...), custom_call_target="tpu_custom_call" | custom-call | tf_op jit(solution)/shard_map/step/pallas_call | solution.py:246
  62.8 1.3 collective-permute-start.26
  64.1 1.3 collective-permute-start.27
  65.4 0.8 collective-permute-start.28
  66.2 1.3 collective-permute-start.29
  67.5 1.3 collective-permute-start.25
  68.8 3.3 %collective-permute-done.29.near1 = bf16[1,64,768]{2,1,0:T(8,128)(2,1)S(1)} collective-permute-done((bf16[1,64,768]{2,1,0:T(8,128)(2,1)S(1)}, bf16[1,64,768]{2,1,0:T(8,128)(2,1)S(1)}, u32[]{:S(2)}, u32[]{:S(2)}) %collective-permute-start.29) | collective-permute-done | bytes 98336 | tf_op jit(solution)/shard_map/window_above/ppermute | solution.py:297
  72.2 2.2 %prepare.5 = (bf16[128,1536]{1,0:T(8,128)(2,1)S(1)}, bf16[128,1536]{1,0:T(8,128)(2,1)S(1)}, bf16[3,256,512]{2,1,0:T(8,128)(2,1)S(1)}, bf16[3,512,128]{2,1,0:T(8,...) custom-call(s32[5]{0:T(128)S(1)} %stack.19.scalars, ...), custom_call_target="tpu_custom_call" | custom-call | tf_op jit(solution)/shard_map/window_above/prepare/pallas_call | solution.py:246
  75.0 0.7 collective-permute-start.23
  75.7 0.7 collective-permute-start.24
  76.4 46.1 %collective-permute-done.25.low = bf16[64,768]{1,0:T(8,128)(2,1)S(1)} collective-permute-done((bf16[64,768]{1,0:T(8,128)(2,1)S(1)}, bf16[64,768]{1,0:T(8,128)(2,1)S(1)}, u32[]{:S(2)}, u32[]{:S(2)}) %collective-permute-start.25) | collective-permute-done | bytes 98336 | tf_op jit(solution)/shard_map/pass_on/ppermute | solution.py:297
  122.5 0.7 collective-permute-start.22
  123.2 3.3 %last_step.1 = (bf16[64,768]{1,0:T(8,128)(2,1)S(1)}, bf16[64,768]{1,0:T(8,128)(2,1)S(1)}) custom-call(s32[5]{0:T(128)S(1)} %stack.19.scalars, bf16[64,768]{1,0:T(8,128)(2,1)S(1)} %collective-permute-done.25.low, bf16[128,768]{1,0:T(8,128)(2,1)S(1)} %collective-permute-done.26.middle, bf16[128,768]{1,0:T(8,128)(2,1)S(1)} %collective-permute-done.27.high, ...), custom_call_target="tpu_custom_call" | custom-call | tf_op jit(solution)/shard_map/last_step/pallas_call | solution.py:246
  126.5 1.9 %collective-permute-start.30 = (bf16[64,768]{1,0:T(8,128)(2,1)S(1)}, bf16[64,768]{1,0:T(8,128)(2,1)S(1)}, u32[]{:S(2)}, u32[]{:S(2)}) collective-permute-start(bf16[64,768]{1,0:T(8,128)(2,1)S(1)} %get-tuple-element.84), channel_id=1, source_target_pairs={{0,6},{6,0},{12,18},{18,12},{24,30},{30,24},{36,42},{42,36},{48,54... | collective-permute-start | bytes 294920 | tf_op jit(solution)/shard_map/last_result/ppermute | solution.py:297
  128.5 1.1 collective-permute-done.30.other_last
  129.7 1.4 %merge.1 = f32[2,64,768]{2,1,0:T(8,128)} custom-call(s32[5]{0:T(128)S(1)} %stack.19.scalars, bf16[64,768]{1,0:T(8,128)(2,1)S(1)} %get-tuple-element.73.own, bf16[64,768]{1,0:T(8,128)(2,1)S(1)} %collective-permute-done.22.other, bf16[64,768]{1,0:T(8,128)(2,1)S(1)} %collective-permute-done.23.near0, bf16[64,768]{1,0:T(8,128)(2,1)S(1)} %collective-permute-done.24.near1, ...), custom_call_target="tpu_custom_call" | custom-call | tf_op jit(solution)/shard_map/merge/pallas_call | solution.py:246
  (52 shorter events, 1.3 us)
Async XLA Ops:
  0.0 3.0 %copy-start.4 = (bf16[1,2,8,8,768]{4,3,2,1,0:T(8,128)(2,1)S(1)}, bf16[1,2,8,8,768]{4,3,2,1,0:T(8,128)(2,1)}, u32[]{:S(2)}) copy-start(bf16[1,2,8,8,768]{4,3,2,1,0:T(8,128)(2,1)} %param.9) | copy-start | bytes 589828
  0.0 5.8 %copy-start.6 = (f32[2,8,8,768]{3,2,1,0:T(8,128)S(1)}, f32[2,8,8,768]{3,2,1,0:T(8,128)}, u32[]{:S(2)}) copy-start(f32[2,8,8,768]{3,2,1,0:T(8,128)} %param.13) | copy-start | bytes 1179652
  0.0 7.0 %collective-permute-start = (s32[1]{0:T(128)}, s32[1]{0:T(128)}, u32[]{:S(2)}, u32[]{:S(2)}) collective-permute-start(s32[1]{0:T(128)} %param.12), channel_id=1, source_target_pairs={{1,0},{2,1},{3,2},{4,3},{5,4},{7,6},{8,7},{9,8},{10,9},{11,10},{13... | collective-permute-start | bytes 20 | tf_op jit(solution)/shard_map/shifts/ppermute | solution.py:330
  2.3 5.4 %collective-permute-start.1 = (bf16[1,64,768]{2,1,0:T(8,128)(2,1)S(1)}, bf16[1,64,768]{2,1,0:T(8,128)(2,1)S(1)}, u32[]{:S(2)}, u32[]{:S(2)}) collective-permute-start(bf16[1,64,768]{2,1,0:T(8,128)(2,1)S(1)} %dynamic-slice_bitcast_fusion.2), channel_id=1, source_target_pairs={{5,11},{11,5},{17,23},{23,17},{29,35},{35,29},{41,47},{47,41},{53,... | collective-permute-start | bytes 294920 | tf_op jit(solution)/shard_map/first_states/ppermute | solution.py:297
  3.0 7.0 %collective-permute-start.5 = (bf16[1,64,768]{2,1,0:T(8,128)(2,1)S(1)}, bf16[1,64,768]{2,1,0:T(8,128)(2,1)S(1)}, u32[]{:S(2)}, u32[]{:S(2)}) collective-permute-start(bf16[1,64,768]{2,1,0:T(8,128)(2,1)S(1)} %get-tuple-element.94), channel_id=1, source_target_pairs={{11,17},{23,29},{35,41},{47,53},{59,65},{71,77},{83,89},{95,101},{... | collective-permute-start | bytes 294920 | tf_op jit(solution)/shard_map/first_states/ppermute | solution.py:297
  3.7 6.3 %collective-permute-start.6 = (bf16[1,64,768]{2,1,0:T(8,128)(2,1)S(1)}, bf16[1,64,768]{2,1,0:T(8,128)(2,1)S(1)}, u32[]{:S(2)}, u32[]{:S(2)}) collective-permute-start(bf16[1,64,768]{2,1,0:T(8,128)(2,1)S(1)} %get-tuple-element.93), channel_id=1, source_target_pairs={{11,23},{23,35},{35,47},{47,59},{59,71},{71,83},{83,95},{95,107},{... | collective-permute-start | bytes 294920 | tf_op jit(solution)/shard_map/first_states/ppermute | solution.py:297
  5.1 0.7 copy-start.7
  5.8 0.9 copy-start.5
  6.9 3.2 %copy-start.2 = (bf16[1,768,384]{2,1,0:T(8,128)(2,1)S(1)}, bf16[1,768,384]{2,1,0:T(8,128)(2,1)}, u32[]{:S(2)}) copy-start(bf16[1,768,384]{2,1,0:T(8,128)(2,1)} %param.16) | copy-start | bytes 1769476
  7.8 2.3 %copy-start = (bf16[1,768,384]{2,1,0:T(8,128)(2,1)S(1)}, bf16[1,768,384]{2,1,0:T(8,128)(2,1)}, u32[]{:S(2)}) copy-start(bf16[1,768,384]{2,1,0:T(8,128)(2,1)} %param.14) | copy-start | bytes 1769476
  7.8 2.3 %copy-start.1 = (bf16[1,768,384]{2,1,0:T(8,128)(2,1)S(1)}, bf16[1,768,384]{2,1,0:T(8,128)(2,1)}, u32[]{:S(2)}) copy-start(bf16[1,768,384]{2,1,0:T(8,128)(2,1)} %param.15) | copy-start | bytes 1769476
  7.8 18.4 %collective-permute-start.2 = (bf16[2,64,768]{2,1,0:T(8,128)(2,1)S(1)}, bf16[2,64,768]{2,1,0:T(8,128)(2,1)S(1)}, u32[]{:S(2)}, u32[]{:S(2)}) collective-permute-start(bf16[2,64,768]{2,1,0:T(8,128)(2,1)S(1)} %get-tuple-element.90), channel_id=1, source_target_pairs={{5,11},{11,5},{17,23},{23,17},{29,35},{35,29},{41,47},{47,41},{53,... | collective-permute-start | bytes 589832 | tf_op jit(solution)/shard_map/first_adjoint/ppermute | solution.py:297
  8.7 19.5 %collective-permute-start.3 = (bf16[2,64,768]{2,1,0:T(8,128)(2,1)S(1)}, bf16[2,64,768]{2,1,0:T(8,128)(2,1)S(1)}, u32[]{:S(2)}, u32[]{:S(2)}) collective-permute-start(bf16[2,64,768]{2,1,0:T(8,128)(2,1)S(1)} %get-tuple-element.89), channel_id=1, source_target_pairs={{11,17},{23,29},{35,41},{47,53},{59,65},{71,77},{83,89},{95,101},{... | collective-permute-start | bytes 589832 | tf_op jit(solution)/shard_map/first_adjoint/ppermute | solution.py:297
  9.3 18.8 %collective-permute-start.4 = (bf16[2,64,768]{2,1,0:T(8,128)(2,1)S(1)}, bf16[2,64,768]{2,1,0:T(8,128)(2,1)S(1)}, u32[]{:S(2)}, u32[]{:S(2)}) collective-permute-start(bf16[2,64,768]{2,1,0:T(8,128)(2,1)S(1)} %get-tuple-element.88), channel_id=1, source_target_pairs={{11,23},{23,35},{35,47},{47,59},{59,71},{71,83},{83,95},{95,107},{... | collective-permute-start | bytes 589832 | tf_op jit(solution)/shard_map/first_adjoint/ppermute | solution.py:297
  12.3 15.9 %copy-start.3 = (bf16[1,384,768]{2,1,0:T(8,128)(2,1)S(1)}, bf16[1,384,768]{2,1,0:T(8,128)(2,1)}, u32[]{:S(2)}) copy-start(bf16[1,384,768]{2,1,0:T(8,128)(2,1)} %param.17) | copy-start | bytes 1769476
  12.3 19.6 %collective-permute-start.10 = (bf16[2,64,768]{2,1,0:T(8,128)(2,1)S(1)}, bf16[2,64,768]{2,1,0:T(8,128)(2,1)S(1)}, u32[]{:S(2)}, u32[]{:S(2)}) collective-permute-start(bf16[2,64,768]{2,1,0:T(8,128)(2,1)S(1)} %get-tuple-element.87), channel_id=1, source_target_pairs={{0,6},{1,7},{2,8},{3,9},{4,10},{6,0},{7,1},{8,2},{9,3},{10,4},{12,... | collective-permute-start | bytes 589832 | tf_op jit(solution)/shard_map/later_states/ppermute | solution.py:297
  24.9 7.7 %collective-permute-start.11 = (bf16[2,64,768]{2,1,0:T(8,128)(2,1)S(1)}, bf16[2,64,768]{2,1,0:T(8,128)(2,1)S(1)}, u32[]{:S(2)}, u32[]{:S(2)}) collective-permute-start(bf16[2,64,768]{2,1,0:T(8,128)(2,1)S(1)} %get-tuple-element.86), channel_id=1, source_target_pairs={{6,12},{7,13},{8,14},{9,15},{10,16},{18,24},{19,25},{20,26},{21,27... | collective-permute-start | bytes 589832 | tf_op jit(solution)/shard_map/later_states/ppermute | solution.py:297
  26.2 17.9 %collective-permute-start.12 = (bf16[2,64,768]{2,1,0:T(8,128)(2,1)S(1)}, bf16[2,64,768]{2,1,0:T(8,128)(2,1)S(1)}, u32[]{:S(2)}, u32[]{:S(2)}) collective-permute-start(bf16[2,64,768]{2,1,0:T(8,128)(2,1)S(1)} %get-tuple-element.85), channel_id=1, source_target_pairs={{6,18},{7,19},{8,20},{9,21},{10,22},{18,30},{19,31},{20,32},{21,33... | collective-permute-start | bytes 589832 | tf_op jit(solution)/shard_map/later_states/ppermute | solution.py:297
  30.6 15.9 %collective-permute-start.8 = (bf16[128,768]{1,0:T(8,128)(2,1)S(1)}, bf16[128,768]{1,0:T(8,128)(2,1)S(1)}, u32[]{:S(2)}, u32[]{:S(2)}) collective-permute-start(bf16[128,768]{1,0:T(8,128)(2,1)S(1)} %get-tuple-element.52.refs_0_), channel_id=1, source_target_pairs={{5,4},{11,10},{17,16},{23,22},{29,28},{35,34},{41,40},{47,46},{53,... | collective-permute-start | bytes 589832 | tf_op jit(solution)/shard_map/pass_on/ppermute | solution.py:297
  31.3 15.2 %collective-permute-start.7 = (bf16[64,768]{1,0:T(8,128)(2,1)S(1)}, bf16[64,768]{1,0:T(8,128)(2,1)S(1)}, u32[]{:S(2)}, u32[]{:S(2)}) collective-permute-start(bf16[64,768]{1,0:T(8,128)(2,1)S(1)} %get-tuple-element.53), channel_id=1, source_target_pairs={{761,4},{767,10},{5,16},{11,22},{17,28},{23,34},{29,40},{35,46},{4... | collective-permute-start | bytes 294920 | tf_op jit(solution)/shard_map/pass_on/ppermute | solution.py:297
  31.9 14.5 %collective-permute-start.9 = (bf16[64,768]{1,0:T(8,128)(2,1)S(1)}, bf16[64,768]{1,0:T(8,128)(2,1)S(1)}, u32[]{:S(2)}, u32[]{:S(2)}) collective-permute-start(bf16[64,768]{1,0:T(8,128)(2,1)S(1)} %get-tuple-element.54), channel_id=1, source_target_pairs={{17,4},{23,10},{29,16},{35,22},{41,28},{47,34},{53,40},{59,46},{65... | collective-permute-start | bytes 294920 | tf_op jit(solution)/shard_map/pass_on/ppermute | solution.py:297
  48.8 2.1 %collective-permute-start.14 = (bf16[128,768]{1,0:T(8,128)(2,1)S(1)}, bf16[128,768]{1,0:T(8,128)(2,1)S(1)}, u32[]{:S(2)}, u32[]{:S(2)}) collective-permute-start(bf16[128,768]{1,0:T(8,128)(2,1)S(1)} %get-tuple-element.63.refs_1_), channel_id=1, source_target_pairs={{4,3},{10,9},{16,15},{22,21},{28,27},{34,33},{40,39},{46,45},{52,5... | collective-permute-start | bytes 589832 | tf_op jit(solution)/shard_map/pass_on/ppermute | solution.py:297
  49.5 1.4 %collective-permute-start.13 = (bf16[64,768]{1,0:T(8,128)(2,1)S(1)}, bf16[64,768]{1,0:T(8,128)(2,1)S(1)}, u32[]{:S(2)}, u32[]{:S(2)}) collective-permute-start(bf16[64,768]{1,0:T(8,128)(2,1)S(1)} %get-tuple-element.64), channel_id=1, source_target_pairs={{760,3},{766,9},{4,15},{10,21},{16,27},{22,33},{28,39},{34,45},{40... | collective-permute-start | bytes 294920 | tf_op jit(solution)/shard_map/pass_on/ppermute | solution.py:297
  50.2 0.7 collective-permute-start.15
  53.3 2.1 %collective-permute-start.17 = (bf16[128,768]{1,0:T(8,128)(2,1)S(1)}, bf16[128,768]{1,0:T(8,128)(2,1)S(1)}, u32[]{:S(2)}, u32[]{:S(2)}) collective-permute-start(bf16[128,768]{1,0:T(8,128)(2,1)S(1)} %get-tuple-element.66.refs_2_), channel_id=1, source_target_pairs={{3,2},{9,8},{15,14},{21,20},{27,26},{33,32},{39,38},{45,44},{51,50... | collective-permute-start | bytes 589832 | tf_op jit(solution)/shard_map/pass_on/ppermute | solution.py:297
  54.0 1.4 %collective-permute-start.16 = (bf16[64,768]{1,0:T(8,128)(2,1)S(1)}, bf16[64,768]{1,0:T(8,128)(2,1)S(1)}, u32[]{:S(2)}, u32[]{:S(2)}) collective-permute-start(bf16[64,768]{1,0:T(8,128)(2,1)S(1)} %get-tuple-element.67), channel_id=1, source_target_pairs={{759,2},{765,8},{3,14},{9,20},{15,26},{21,32},{27,38},{33,44},{39,... | collective-permute-start | bytes 294920 | tf_op jit(solution)/shard_map/pass_on/ppermute | solution.py:297
  54.6 0.7 collective-permute-start.18
  57.7 2.1 %collective-permute-start.20 = (bf16[128,768]{1,0:T(8,128)(2,1)S(1)}, bf16[128,768]{1,0:T(8,128)(2,1)S(1)}, u32[]{:S(2)}, u32[]{:S(2)}) collective-permute-start(bf16[128,768]{1,0:T(8,128)(2,1)S(1)} %get-tuple-element.69.refs_3_), channel_id=1, source_target_pairs={{2,1},{8,7},{14,13},{20,19},{26,25},{32,31},{38,37},{44,43},{50,49... | collective-permute-start | bytes 589832 | tf_op jit(solution)/shard_map/pass_on/ppermute | solution.py:297
  58.4 1.4 %collective-permute-start.19 = (bf16[64,768]{1,0:T(8,128)(2,1)S(1)}, bf16[64,768]{1,0:T(8,128)(2,1)S(1)}, u32[]{:S(2)}, u32[]{:S(2)}) collective-permute-start(bf16[64,768]{1,0:T(8,128)(2,1)S(1)} %get-tuple-element.70), channel_id=1, source_target_pairs={{758,1},{764,7},{2,13},{8,19},{14,25},{20,31},{26,37},{32,43},{38,... | collective-permute-start | bytes 294920 | tf_op jit(solution)/shard_map/pass_on/ppermute | solution.py:297
  59.1 0.7 collective-permute-start.21
  62.8 60.4 %collective-permute-start.26 = (bf16[128,768]{1,0:T(8,128)(2,1)S(1)}, bf16[128,768]{1,0:T(8,128)(2,1)S(1)}, u32[]{:S(2)}, u32[]{:S(2)}) collective-permute-start(bf16[128,768]{1,0:T(8,128)(2,1)S(1)} %get-tuple-element.72.refs_4_), channel_id=1, source_target_pairs={{1,0},{7,6},{13,12},{19,18},{25,24},{31,30},{37,36},{43,42},{49,48... | collective-permute-start | bytes 589832 | tf_op jit(solution)/shard_map/pass_on/ppermute | solution.py:297
  64.1 59.1 %collective-permute-start.27 = (bf16[128,768]{1,0:T(8,128)(2,1)S(1)}, bf16[128,768]{1,0:T(8,128)(2,1)S(1)}, u32[]{:S(2)}, u32[]{:S(2)}) collective-permute-start(bf16[128,768]{1,0:T(8,128)(2,1)S(1)} %get-tuple-element.72.refs_4_), channel_id=1, source_target_pairs={{13,0},{19,6},{25,12},{31,18},{37,24},{43,30},{49,36},{55,42},{61,... | collective-permute-start | bytes 589832 | tf_op jit(solution)/shard_map/pass_on/ppermute | solution.py:297
  65.4 3.5 %collective-permute-start.28 = (bf16[1,64,768]{2,1,0:T(8,128)(2,1)S(1)}, bf16[1,64,768]{2,1,0:T(8,128)(2,1)S(1)}, u32[]{:S(2)}, u32[]{:S(2)}) collective-permute-start(bf16[1,64,768]{2,1,0:T(8,128)(2,1)S(1)} %get-tuple-element.94), channel_id=1, source_target_pairs={{12,0},{24,12},{36,24},{48,36},{60,48},{72,60},{84,72},{96,84},{10... | collective-permute-start | bytes 294920 | tf_op jit(solution)/shard_map/window_above/ppermute | solution.py:297
  66.2 5.9 %collective-permute-start.29 = (bf16[1,64,768]{2,1,0:T(8,128)(2,1)S(1)}, bf16[1,64,768]{2,1,0:T(8,128)(2,1)S(1)}, u32[]{:S(2)}, u32[]{:S(2)}) collective-permute-start(bf16[1,64,768]{2,1,0:T(8,128)(2,1)S(1)} %get-tuple-element.93), channel_id=1, source_target_pairs={{12,6},{24,18},{36,30},{48,42},{60,54},{72,66},{84,78},{96,90},{10... | collective-permute-start | bytes 294920 | tf_op jit(solution)/shard_map/window_above/ppermute | solution.py:297
  67.5 54.9 %collective-permute-start.25 = (bf16[64,768]{1,0:T(8,128)(2,1)S(1)}, bf16[64,768]{1,0:T(8,128)(2,1)S(1)}, u32[]{:S(2)}, u32[]{:S(2)}) collective-permute-start(bf16[64,768]{1,0:T(8,128)(2,1)S(1)} %get-tuple-element.76), channel_id=1, source_target_pairs={{757,0},{763,6},{1,12},{7,18},{13,24},{19,30},{25,36},{31,42},{37,... | collective-permute-start | bytes 294920 | tf_op jit(solution)/shard_map/pass_on/ppermute | solution.py:297
  75.0 53.5 %collective-permute-start.23 = (bf16[64,768]{1,0:T(8,128)(2,1)S(1)}, bf16[64,768]{1,0:T(8,128)(2,1)S(1)}, u32[]{:S(2)}, u32[]{:S(2)}) collective-permute-start(bf16[64,768]{1,0:T(8,128)(2,1)S(1)} %get-tuple-element.75), channel_id=1, source_target_pairs={{13,7},{14,8},{15,9},{16,10},{17,11},{25,19},{26,20},{27,21},{28,2... | collective-permute-start | bytes 294920 | tf_op jit(solution)/shard_map/earlier_results/ppermute | solution.py:297
  75.7 52.8 %collective-permute-start.24 = (bf16[64,768]{1,0:T(8,128)(2,1)S(1)}, bf16[64,768]{1,0:T(8,128)(2,1)S(1)}, u32[]{:S(2)}, u32[]{:S(2)}) collective-permute-start(bf16[64,768]{1,0:T(8,128)(2,1)S(1)} %get-tuple-element.75), channel_id=1, source_target_pairs={{19,7},{20,8},{21,9},{22,10},{23,11},{31,19},{32,20},{33,21},{34,2... | collective-permute-start | bytes 294920 | tf_op jit(solution)/shard_map/earlier_results/ppermute | solution.py:297
  122.5 6.0 %collective-permute-start.22 = (bf16[64,768]{1,0:T(8,128)(2,1)S(1)}, bf16[64,768]{1,0:T(8,128)(2,1)S(1)}, u32[]{:S(2)}, u32[]{:S(2)}) collective-permute-start(bf16[64,768]{1,0:T(8,128)(2,1)S(1)} %get-tuple-element.74), channel_id=1, source_target_pairs={{1,7},{2,8},{3,9},{4,10},{5,11},{7,1},{8,2},{9,3},{10,4},{11,5},{1... | collective-permute-start | bytes 294920 | tf_op jit(solution)/shard_map/earlier_results/ppermute | solution.py:297
  126.5 3.2 %collective-permute-start.30 = (bf16[64,768]{1,0:T(8,128)(2,1)S(1)}, bf16[64,768]{1,0:T(8,128)(2,1)S(1)}, u32[]{:S(2)}, u32[]{:S(2)}) collective-permute-start(bf16[64,768]{1,0:T(8,128)(2,1)S(1)} %get-tuple-element.84), channel_id=1, source_target_pairs={{0,6},{6,0},{12,18},{18,12},{24,30},{30,24},{36,42},{42,36},{48,54... | collective-permute-start | bytes 294920 | tf_op jit(solution)/shard_map/last_result/ppermute | solution.py:297

commit v3 on v2

--- a/solution.py
+++ b/solution.py
@@ -15,6 +15,7 @@
 BAND = 64
 SLOT = 128
 GROUP = 4
+RUN = 8
 
 
 def dot_nn(a, b):
@@ -29,10 +30,16 @@
     return jnp.where(core == 0, near0[field].astype(FLT), near1[field].astype(FLT))
 
 
-def gathered(rows, field, core, offset, own, other, near0, near1):
-    rows[0:BAND, :] = near_of(core, near0, near1, field)
-    rows[pl.ds(pl.multiple_of(BAND + BAND * core, BAND), BAND), :] = own[core, field].astype(FLT)
-    rows[pl.ds(pl.multiple_of(2 * BAND - BAND * core, BAND), BAND), :] = other[field].astype(FLT)
+def gathered(rows, scalars, own, other, near0, near1, field):
+    core, offset, lift = scalars[0], scalars[2], scalars[4]
+
+    def place(token, value):
+        rows[pl.ds(pl.multiple_of(token, BAND), BAND), :] = value.astype(FLT)
+
+    base = BAND * (1 - lift)
+    place(2 * BAND * lift, near_of(core, near0, near1, field))
+    place(base + BAND * core, own[core, field])
+    place(base + BAND * (1 - core), other[field])
     return rows[pl.ds(pl.multiple_of(offset * WIN, WIN), SLOT), :]
 
 
@@ -46,7 +53,7 @@
 def prepare_kernel(
     above,
     with_forcing,
-    edge_slot,
+    last_slot,
     scalars,
     own,
     other,
@@ -68,9 +75,9 @@
     if above:
         x = gathered_above(rows, core, offset, own, other, near0, near1).astype(BF)
     else:
-        x = gathered(rows, 0, core, offset, own, other, near0, near1).astype(BF)
+        x = gathered(rows, scalars, own, other, near0, near1, 0).astype(BF)
     if with_forcing:
-        rest[0][...] = gathered(rows, 1, core, offset, own, other, near0, near1).astype(BF)
+        rest[0][...] = gathered(rows, scalars, own, other, near0, near1, 1).astype(BF)
     scale = HD ** (-0.5)
     q = (dot_nn(x, w_query[...]) * scale).astype(BF)
     k = dot_nn(x, w_key[...]).astype(BF)
@@ -79,7 +86,13 @@
     other_token = lax.broadcasted_iota(jnp.int32, (SLOT, SLOT), 1)
     row_head = token // HD
     lane_head = other_token // HD
-    edge = jnp.where(slot == edge_slot, BAND - offset * WIN, 0)
+    start = BAND - offset * WIN
+    if above:
+        edge = jnp.where(slot == last_slot, start, 0)
+    else:
+        lift = scalars[4]
+        edge_slot = jnp.where(lift == 0, 0, last_slot)
+        edge = jnp.where(slot == edge_slot, start + BAND * lift, 0)
     allowed = ((token // BAND) == (other_token // BAND)) & (
         (token < edge) == (other_token < edge)
     )
@@ -146,41 +159,37 @@
     return change
 
 
-def first_kernel(scalars, own, other, near0, near1, *refs):
+def first_kernel(scalars, own, final, other, final_other, near0, near1, final0, final1, *refs):
     prepared, weights = refs[:6], refs[6:10]
-    all_ref, low_ref, high_ref, rows = refs[10:]
-    core, offset = scalars[0], scalars[2]
-    adjoint = gathered(rows, 0, core, offset, own, other, near0, near1)
-    forcing = gathered(rows, 1, core, offset, own, other, near0, near1)
-    updated = (adjoint + changed(adjoint, [prepared], *weights) + forcing).astype(BF)
-    all_ref[...] = updated
-    low_ref[...] = updated[:BAND]
-    high_ref[...] = updated[BAND:]
-
-
-def step_kernel(scalars, low, middle, high, *refs):
+    all_ref, rows = refs[10:]
+    forcing = gathered(rows, scalars, own, other, near0, near1, 1)
+    adjoint = gathered(rows, scalars, final, final_other, final0, final1, 0)
+    all_ref[...] = (adjoint + changed(adjoint, [prepared], *weights) + forcing).astype(BF)
+
+
+def step_kernel(scalars, above, low, high, *refs):
     prepared, forcing, weights = refs[:6], refs[6], refs[7:11]
-    all_ref, low_ref, high_ref, rows = refs[11:]
-    rows[0:BAND, :] = low[...].astype(FLT)
-    rows[BAND : BAND + SLOT, :] = middle[...].astype(FLT)
-    rows[BAND + SLOT :, :] = high[...].astype(FLT)
-    shift = scalars[4]
-    adjoint = rows[pl.ds(pl.multiple_of(BAND + shift * WIN, WIN), SLOT), :]
+    outs, rows = refs[11:-1], refs[-1]
+    rows[0:SLOT, :] = low[...].astype(FLT)
+    rows[SLOT:, :] = high[...].astype(FLT)
+    start = BAND + (scalars[2] - above[0]) * WIN
+    adjoint = rows[pl.ds(pl.multiple_of(start, WIN), SLOT), :]
     change = changed(adjoint, [prepared], *weights)
     updated = (adjoint + change + forcing[...].astype(FLT)).astype(BF)
-    all_ref[...] = updated
-    low_ref[...] = updated[:BAND]
-    high_ref[...] = updated[BAND:]
-
-
-def last_kernel(scalars, low, middle, high, *refs):
+    outs[0][...] = updated
+    if len(outs) == 2:
+        outs[1][...] = updated[BAND:]
+
+
+def last_kernel(scalars, above, low, middle, high, *refs):
     units, weights = [refs[:6], refs[6:12]], refs[12:16]
     own_ref, swap_ref, rows = refs[16:]
     rows[0:BAND, :] = low[...].astype(FLT)
     rows[BAND : BAND + SLOT, :] = middle[...].astype(FLT)
     rows[BAND + SLOT : BAND + 2 * SLOT, :] = high[...].astype(FLT)
     rows[BAND + 2 * SLOT :, :] = jnp.zeros_like(rows[BAND + 2 * SLOT :, :])
-    core, offset, shift = scalars[0], scalars[2], scalars[4]
+    core, offset = scalars[0], scalars[2]
+    shift = offset - above[0]
     adjoint = rows[pl.ds(pl.multiple_of(BAND + shift * WIN, WIN), 2 * SLOT), :]
     rows[0 : 2 * SLOT, :] = adjoint + changed(adjoint, units, *weights)
     even = rows[pl.ds(pl.multiple_of(BAND - offset * WIN, WIN), BAND), :].astype(BF)
@@ -192,7 +201,7 @@
 def split_kernel(scalars, *refs):
     results = refs[:-6]
     own_ref, swap_ref, lower_ref, held, rows, sem = refs[-6:]
-    core, offset, section = scalars[0], scalars[2], scalars[3]
+    core, offset, section, lift = scalars[0], scalars[2], scalars[3], scalars[4]
     for tick, result in enumerate(results):
 
         @pl.when(section == len(results) - tick)
@@ -201,10 +210,12 @@
             copy.start()
             copy.wait()
 
-    lower_ref[...] = held[0:BAND]
     rows[...] = held[...].astype(FLT)
-    even = rows[pl.ds(pl.multiple_of(BAND - offset * WIN, WIN), BAND), :].astype(BF)
-    odd = held[BAND:SLOT]
+    inner = rows[pl.ds(pl.multiple_of(BAND - offset * WIN, WIN), BAND), :].astype(BF)
+    lower, upper = held[0:BAND], held[BAND:SLOT]
+    lower_ref[...] = jnp.where(lift == 0, lower, upper)
+    even = jnp.where(lift == 0, inner, lower)
+    odd = jnp.where(lift == 0, upper, inner)
     own_ref[...] = jnp.where(core == 0, even, odd)
     swap_ref[...] = jnp.where(core == 0, odd, even)
 
@@ -212,7 +223,7 @@
 def merge_kernel(
     scalars, own, other, near0, near1, own_last, other_last, forcing, result, rows
 ):
-    core, offset, section = scalars[0], scalars[2], scalars[3]
+    core, offset, section, lift = scalars[0], scalars[2], scalars[3], scalars[4]
 
     @pl.when(section == 0)
     def _():
@@ -225,11 +236,12 @@
     @pl.when(section != 0)
     def _():
         for member, near in ((0, near0), (1, near1)):
-            rows[0:BAND, :] = jnp.where(
+            mine = BAND * lift
+            rows[pl.ds(pl.multiple_of(mine, BAND), BAND), :] = jnp.where(
                 core == member, own[...].astype(FLT), other[...].astype(FLT)
             )
-            rows[BAND:SLOT, :] = near[...].astype(FLT)
-            start = jnp.where(core == 1, BAND - offset * WIN, 0)
+            rows[pl.ds(pl.multiple_of(BAND - mine, BAND), BAND), :] = near[...].astype(FLT)
+            start = jnp.where(core == 1 - lift, BAND - offset * WIN, mine)
             result[member] = rows[pl.ds(pl.multiple_of(start, WIN), BAND), :]
 
 
@@ -242,19 +254,19 @@
 ANY = pl.BlockSpec(memory_space=pl.ANY)
 
 
-def call(name, kernel, scalars, operands, shapes, scratch, place=VMEM):
+def call(name, kernel, scalars, operands, shapes, scratch, place=VMEM, above=()):
     return pl.pallas_call(
         kernel,
         out_shape=shapes,
-        in_specs=[SMEM] + [place] * len(operands),
+        in_specs=[SMEM] * (1 + len(above)) + [place] * len(operands),
         out_specs=[VMEM] * len(shapes),
         scratch_shapes=scratch,
         compiler_params=pltpu.CompilerParams(vmem_limit_bytes=40 * 1024 * 1024),
         name=name,
-    )(scalars, *operands)
-
-
-def prepare(scalars, operands, weights, edge_slot, above=False, with_forcing=False):
+    )(scalars, *above, *operands)
+
+
+def prepare(scalars, operands, weights, last_slot, above=False, with_forcing=False):
     width, hidden = weights[0].shape
     keys = hidden // HD * SLOT
     shapes = [
@@ -269,7 +281,7 @@
         shapes.append(struct((SLOT, width)))
     return call(
         "prepare",
-        functools.partial(prepare_kernel, above, with_forcing, edge_slot),
+        functools.partial(prepare_kernel, above, with_forcing, last_slot),
         scalars,
         (*operands, *weights[:3]),
         shapes,
@@ -299,86 +311,103 @@
     def moved(ways, among):
         return [(at(a, s), at(b, s)) for a, b in ways for s in among]
 
-    def exchange(fields, among):
-        near0 = sent(fields[0], moved([(2 * j + 1, 2 * j + 2) for j in range(chips)], among))
-        near1 = sent(fields[1], moved([(2 * j + 1, 2 * j + 3) for j in range(chips)], among))
-        other = sent(
-            lax.dynamic_index_in_dim(fields, 1 - core, 0, keepdims=False),
-            moved([(b, b ^ 1) for b in range(bands)], among),
-        )
-        return other, near0, near1
-
     def flat(values):
         return values.reshape(members, 1, BAND, width)
 
     def ints(*values):
         return jnp.stack(values).astype(jnp.int32)
 
-    final_section = [sections - 1]
+    last = sections - 1
     x = flat(trajectory[0])
-    with jax.named_scope("first_states"):
-        first_x = exchange(x, final_section)
     weight = obs_mask[0].reshape(1, 1, BAND, 1).astype(FLT)
     forcing = (weight * (x.astype(FLT) - flat(observed[0]).astype(FLT))).astype(BF)
-    final = flat(final_adjoint).astype(BF)
+    pair = jnp.concatenate([x, forcing], axis=1)
+    even_down = [[(2 * j + 2, 2 * j + m) for j in range(chips)] for m in range(2)]
+    odd_up = [[(2 * j + 1, 2 * j + 2 + m) for j in range(chips)] for m in range(2)]
+    swaps = [(b, b ^ 1) for b in range(bands)]
+
+    def begun(ways):
+        run = 2 * RUN
+        return [
+            (at(a, 0 if a // run != b // run else last), at(b, last)) for a, b in ways
+        ]
+
+    with jax.named_scope("first_states"):
+        near = [sent(pair[m], moved(odd_up[m], [last])) for m in range(2)]
     with jax.named_scope("first_adjoint"):
-        begin = jnp.concatenate([final, forcing], axis=1)
-        begin, _ = lax.optimization_barrier((begin, first_x[0]))
-        first_begin = exchange(begin, final_section)
-    with jax.named_scope("shifts"):
-        down = [(s, s - 1) for s in range(1, sections)]
-        above = lax.ppermute(shift_rows, "section", down)[0].astype(jnp.int32)
-    shift = jnp.where(section_at == sections - 1, 0, offset - above)
-    place = ints(core, chip, offset, section_at, shift)
-
-    prepared = prepare(place, (x, *first_x), weights, 0)
+        final, _ = lax.optimization_barrier((final_adjoint, pair))
+        final = flat(final).astype(BF)
+        final_near = [sent(final[m], begun(odd_up[m])) for m in range(2)]
+        first_other = sent(
+            lax.dynamic_index_in_dim(pair, 1 - core, 0, keepdims=False), moved(swaps, [last])
+        )
+        final_other = sent(
+            lax.dynamic_index_in_dim(final, 1 - core, 0, keepdims=False), moved(swaps, [last])
+        )
+    lift = jnp.where(section_at == 0, 0, (last - section_at) % 2)
+    place = ints(core, chip, offset, section_at, lift)
+    prepared = prepare(place, (pair, first_other, *near), weights, chips - 1)
     result = call(
         "first_step",
         first_kernel,
         place,
-        (begin, *first_begin, *prepared, *weights),
-        [struct((SLOT, width)), struct((BAND, width)), struct((BAND, width))],
+        (pair, final, first_other, final_other, *near, *final_near, *prepared, *weights),
+        [struct((SLOT, width))],
         [pltpu.VMEM((3 * BAND, width), FLT)],
     )
     results = [result[0]]
     with jax.named_scope("later_states"):
-        pair = jnp.concatenate([x, forcing], axis=1)
-        pair, _ = lax.optimization_barrier((pair, prepared[0]))
-        later = exchange(pair, list(range(sections - 1)))
-    *prepared, forcing_here = prepare(place, (pair, *later), weights, 0, with_forcing=True)
+        pair_later, _ = lax.optimization_barrier((pair, result[0]))
+        rest = list(range(last))
+        lifted = [s for s in range(1, last) if (last - s) % 2]
+        level = [s for s in rest if s not in lifted]
+        later_near = [
+            sent(pair_later[m], moved(odd_up[m], level) + moved(even_down[m], lifted))
+            for m in range(2)
+        ]
+        later_other = sent(
+            lax.dynamic_index_in_dim(pair_later, 1 - core, 0, keepdims=False),
+            moved(swaps, rest),
+        )
+    with jax.named_scope("shifts"):
+        down = [(s, s - 1) for s in range(1, sections)]
+        tied, _ = lax.optimization_barrier((shift_rows, later_other))
+        above = lax.ppermute(tied, "section", down)
+    *prepared, forcing_here = prepare(
+        place, (pair, later_other, *later_near), weights, chips - 1, with_forcing=True
+    )
     for tick in range(1, sections):
         source = sections - tick
-        whole, low, high = result
+        whole = result[0]
 
         def across_from(way):
             return [(at(b + 2 * way, source), at(b, source - 1)) for b in range(bands)]
 
         with jax.named_scope("pass_on"):
-            if tick == sections - 1:
-                from_low = sent(high, across_from(-1))
+            if tick == last:
+                from_low = sent(result[1], across_from(-1))
                 from_high = sent(whole, across_from(1))
                 middle = sent(whole, across_from(0))
-            else:
-                from_low = sent(high, across_from(-1))
-                from_high = sent(low, across_from(1))
-                middle = sent(whole, across_from(0))
-        if tick == sections - 1:
-            break
+                break
+            side = sent(whole, across_from(1 if tick % 2 else -1))
+            middle = sent(whole, across_from(0))
+        shapes = [struct((SLOT, width))]
+        if tick == last - 1:
+            shapes.append(struct((BAND, width)))
         result = call(
             "step",
             step_kernel,
             place,
-            (from_low, middle, from_high, *prepared, forcing_here, *weights),
-            [struct((SLOT, width)), struct((BAND, width)), struct((BAND, width))],
-            [pltpu.VMEM((4 * BAND, width), FLT)],
+            (*((middle, side) if tick % 2 else (side, middle)), *prepared, forcing_here, *weights),
+            shapes,
+            [pltpu.VMEM((2 * SLOT, width), FLT)],
+            above=(above,),
         )
         results.append(result[0])
 
     with jax.named_scope("window_above"):
-        ups = [(2 * j + 2, 2 * j) for j in range(chips)], [(2 * j + 2, 2 * j + 1) for j in range(chips)]
-        next0 = sent(x[0], moved(ups[0], [0]))
-        next1 = sent(x[1], moved(ups[1], [0]))
-        extra = prepare(place, (pair, later[0], next0, next1), weights, chips - 1, above=True)
+        next0, next1 = [sent(x[m], moved(even_down[m], [0])) for m in range(2)]
+        extra = prepare(place, (pair, later_other, next0, next1), weights, chips - 1, above=True)
     own, swap, lower = call(
         "split",
         split_kernel,
@@ -394,9 +423,16 @@
     )
     with jax.named_scope("earlier_results"):
         every = range(1, sections)
-        near0 = sent(lower, moved([(2 * j + 2, 2 * j + 1) for j in range(chips)], every))
-        near1 = sent(lower, moved([(2 * j + 3, 2 * j + 1) for j in range(chips)], every))
-        other = sent(swap, moved([(b, b ^ 1) for b in range(bands)], every))
+        flatly = [s for s in every if s not in lifted]
+        near0, near1 = [
+            sent(
+                lower,
+                moved([(2 * j + 2 + m, 2 * j + 1) for j in range(chips)], flatly)
+                + moved([(2 * j + m, 2 * j + 2) for j in range(chips)], lifted),
+            )
+            for m in range(2)
+        ]
+        other = sent(swap, moved(swaps, every))
     own_last, swap_last = call(
         "last_step",
         last_kernel,
@@ -404,9 +440,10 @@
         (from_low, middle, from_high, *prepared, *extra, *weights),
         [struct((BAND, width))] * 2,
         [pltpu.VMEM((6 * BAND, width), FLT)],
+        above=(above,),
     )
     with jax.named_scope("last_result"):
-        other_last = sent(swap_last, moved([(b, b ^ 1) for b in range(bands)], [0]))
+        other_last = sent(swap_last, moved(swaps, [0]))
     (field,) = call(
         "merge",
         merge_kernel,

time: 133 us -> 130 us (0.977)
  waiting for transfers between devices: 62.1 us -> 57.8 us
  Pallas kernels: 24.5 us -> 27.2 us
  other arithmetic: 0.29 us -> 2.14 us
    ppermute x30 -> x26, waiting for transfers between devices: 62.1 us -> 57.8 us  [sent(): return lax.ppermute(value, AXES, hops)]
    pallas_call x11, Pallas kernels: 24.5 us -> 27.2 us  [call(): pl.pallas_call(kernel, out_shape=shapes, in_specs=[SMEM] * (1 + len(above...]
    ppermute x30 -> x26, starting transfers between devices: 37.9 us -> 37.6 us  [sent(): return lax.ppermute(value, AXES, hops)]
  transfers between devices with their start and end apart: 31 -> 27, of which waited for: 4 -> 4; matrix products, arithmetic and copies ran while one was open for 1% -> 1% of each run, Pallas kernels for 10% -> 9%
where the time goes in v3:
time: 130 us; the launch traced here: 129 us
  waiting for transfers between devices  57.8 us (44%)
  starting transfers between devices  38.9 us (30%)
  Pallas kernels  27.2 us (21%)
  other arithmetic  2.14 us (2%)
  local copies, waits for them, and re-layouts  1.81 us (1%)
    ppermute x26, waiting for transfers between devices, sent(): return lax.ppermute(value, AXES, hops)  57.8 us
    ppermute x26, starting transfers between devices, sent(): return lax.ppermute(value, AXES, hops)  37.6 us
    pallas_call x11, Pallas kernels, call(): pl.pallas_call(kernel, out_shape=shapes, in_specs=[SMEM] * (1 + len(above...  27.2 us
  transfers between devices with their start and end apart: 27, of which 4 were waited for; matrix products, arithmetic and copies ran while one was open for 1% of the time, Pallas kernels for 9%

profile of v3, /device:TPU:1, one launch (start us, length us, event | category | flops | bytes accessed | tf_op | source)
XLA Modules:
  0.0 129.1 jit_solution(16703980740614345404)
XLA Ops:
  0.0 0.7 copy-done.7
  0.8 1.2 fusion.2
  1.9 0.8 fusion.11
  2.8 0.8 collective-permute-start
  3.6 0.1 copy-done.5
  3.8 0.8 collective-permute-start.1
  4.6 0.7 collective-permute-start.2
  5.3 0.7 collective-permute-start.3
  6.0 0.7 slice_bitcast_fusion.2
  6.7 0.7 collective-permute-start.4
  7.4 0.7 collective-permute-start.5
  8.9 2.2 %prepare.3 = (bf16[128,1536]{1,0:T(8,128)(2,1)S(1)}, bf16[128,1536]{1,0:T(8,128)(2,1)S(1)}, bf16[3,256,512]{2,1,0:T(8,128)(2,1)S(1)}, bf16[3,512,128]{2,1,0:T(8,...) custom-call(s32[5]{0:T(128)S(1)} %stack.19.scalars, ...), custom_call_target="tpu_custom_call" | custom-call | tf_op jit(solution)/shard_map/prepare/pallas_call | solution.py:258
  11.1 2.5 %first_step.1.refs_0_ = bf16[128,768]{1,0:T(8,128)(2,1)S(1)} custom-call(s32[5]{0:T(128)S(1)} %stack.19.scalars, bf16[2,2,64,768]{3,2,1,0:T(8,128)(2,1)S(1)} %pad_maximum_fusion.own, bf16[2,1,64,768]{3,2,1,0:T(8,128)(2,1)S(1)} %convert_bitcast_fusion.1.final, bf16[2,64,768]{2,1,0:T(8,128)(2,1)S(1)} %collective-permute-done.other, ...), custom_call_target="tpu_custom_call" | custom-call | tf_op jit(solution)/shard_map/first_step/pallas_call | solution.py:258
  13.7 12.4 %collective-permute-start.6 = (bf16[2,64,768]{2,1,0:T(8,128)(2,1)S(1)}, bf16[2,64,768]{2,1,0:T(8,128)(2,1)S(1)}, u32[]{:S(2)}, u32[]{:S(2)}) collective-permute-start(bf16[2,64,768]{2,1,0:T(8,128)(2,1)S(1)} %get-tuple-element.65), channel_id=1, source_target_pairs={{0,6},{1,7},{2,8},{3,9},{4,10},{6,0},{7,1},{8,2},{9,3},{10,4},{12,... | collective-permute-start | bytes 589832 | tf_op jit(solution)/shard_map/later_states/ppermute | solution.py:309
  26.1 1.3 %collective-permute-start.10 = (bf16[2,64,768]{2,1,0:T(8,128)(2,1)S(1)}, bf16[2,64,768]{2,1,0:T(8,128)(2,1)S(1)}, u32[]{:S(2)}, u32[]{:S(2)}) collective-permute-start(bf16[2,64,768]{2,1,0:T(8,128)(2,1)S(1)} %get-tuple-element.64), channel_id=1, source_target_pairs={{6,12},{7,13},{9,15},{18,24},{19,25},{21,27},{30,36},{31,37},{33,3... | collective-permute-start | bytes 589832 | tf_op jit(solution)/shard_map/later_states/ppermute | solution.py:309
  27.4 1.9 %collective-permute-start.11 = (bf16[2,64,768]{2,1,0:T(8,128)(2,1)S(1)}, bf16[2,64,768]{2,1,0:T(8,128)(2,1)S(1)}, u32[]{:S(2)}, u32[]{:S(2)}) collective-permute-start(bf16[2,64,768]{2,1,0:T(8,128)(2,1)S(1)} %get-tuple-element.63), channel_id=1, source_target_pairs={{6,18},{7,19},{9,21},{18,30},{19,31},{21,33},{30,42},{31,43},{33,4... | collective-permute-start | bytes 589832 | tf_op jit(solution)/shard_map/later_states/ppermute | solution.py:309
  29.3 0.7 collective-permute-start.8
  30.0 0.7 collective-permute-start.9
  30.7 1.3 %collective-permute-start.7 = (s32[1]{0:T(128)}, s32[1]{0:T(128)}, u32[]{:S(2)}, u32[]{:S(2)}) collective-permute-start(s32[1]{0:T(128)} %param.12), channel_id=1, source_target_pairs={{1,0},{2,1},{3,2},{4,3},{5,4},{7,6},{8,7},{9,8},{10,9},{11,10},{13... | collective-permute-start | bytes 20 | tf_op jit(solution)/shard_map/shifts/ppermute | solution.py:375
  32.0 17.8 %collective-permute-done.11.near1 = bf16[2,64,768]{2,1,0:T(8,128)(2,1)S(1)} collective-permute-done((bf16[2,64,768]{2,1,0:T(8,128)(2,1)S(1)}, bf16[2,64,768]{2,1,0:T(8,128)(2,1)S(1)}, u32[]{:S(2)}, u32[]{:S(2)}) %collective-permute-start.11) | collective-permute-done | bytes 196640 | tf_op jit(solution)/shard_map/later_states/ppermute | solution.py:309
  49.8 2.3 %prepare.4 = (bf16[128,1536]{1,0:T(8,128)(2,1)S(1)}, bf16[128,1536]{1,0:T(8,128)(2,1)S(1)}, bf16[3,256,512]{2,1,0:T(8,128)(2,1)S(1)}, bf16[3,512,128]{2,1,0:T(8,...) custom-call(s32[5]{0:T(128)S(1)} %stack.19.scalars, ...), custom_call_target="tpu_custom_call" | custom-call | tf_op jit(solution)/shard_map/prepare/pallas_call | solution.py:258
  52.1 3.0 %step.4.refs_1_ = bf16[128,768]{1,0:T(8,128)(2,1)S(1)} custom-call(s32[5]{0:T(128)S(1)} %stack.19.scalars, s32[1]{0:T(128)} %collective-permute-done.7.above, bf16[128,768]{1,0:T(8,128)(2,1)S(1)} %collective-permute-done.8.low, bf16[128,768]{1,0:T(8,128)(2,1)S(1)} %collective-permute-done.9.high, bf16[128,1536]{1,0:T(8,128)(2,1)S(1)} %get-tuple-element.43.refs_0_, ...), custom_call_target="tpu_custom_call" | custom-call | tf_op jit(solution)/shard_map/step/pallas_call | solution.py:258
  55.1 0.7 collective-permute-start.12
  55.8 0.7 collective-permute-start.13
  56.5 3.0 %step.5.refs_2_ = bf16[128,768]{1,0:T(8,128)(2,1)S(1)} custom-call(s32[5]{0:T(128)S(1)} %stack.19.scalars, s32[1]{0:T(128)} %collective-permute-done.7.above, bf16[128,768]{1,0:T(8,128)(2,1)S(1)} %collective-permute-done.12.low, bf16[128,768]{1,0:T(8,128)(2,1)S(1)} %collective-permute-done.13.high, bf16[128,1536]{1,0:T(8,128)(2,1)S(1)} %get-tuple-element.43.refs_0_, ...), custom_call_target="tpu_custom_call" | custom-call | tf_op jit(solution)/shard_map/step/pallas_call | solution.py:258
  59.5 0.7 collective-permute-start.14
  60.2 0.7 collective-permute-start.15
  60.9 3.0 %step.6.refs_3_ = bf16[128,768]{1,0:T(8,128)(2,1)S(1)} custom-call(s32[5]{0:T(128)S(1)} %stack.19.scalars, s32[1]{0:T(128)} %collective-permute-done.7.above, bf16[128,768]{1,0:T(8,128)(2,1)S(1)} %collective-permute-done.14.low, bf16[128,768]{1,0:T(8,128)(2,1)S(1)} %collective-permute-done.15.high, bf16[128,1536]{1,0:T(8,128)(2,1)S(1)} %get-tuple-element.43.refs_0_, ...), custom_call_target="tpu_custom_call" | custom-call | tf_op jit(solution)/shard_map/step/pallas_call | solution.py:258
  63.9 0.7 collective-permute-start.16
  64.6 0.7 collective-permute-start.17
  65.3 3.0 %step.7 = (bf16[128,768]{1,0:T(8,128)(2,1)S(1)}, bf16[64,768]{1,0:T(8,128)(2,1)S(1)}) custom-call(s32[5]{0:T(128)S(1)} %stack.19.scalars, s32[1]{0:T(128)} %collective-permute-done.7.above, bf16[128,768]{1,0:T(8,128)(2,1)S(1)} %collective-permute-done.16.low, bf16[128,768]{1,0:T(8,128)(2,1)S(1)} %collective-permute-done.17.high, ...), custom_call_target="tpu_custom_call" | custom-call | tf_op jit(solution)/shard_map/step/pallas_call | solution.py:258
  68.3 1.3 %collective-permute-start.22 = (bf16[128,768]{1,0:T(8,128)(2,1)S(1)}, bf16[128,768]{1,0:T(8,128)(2,1)S(1)}, u32[]{:S(2)}, u32[]{:S(2)}) collective-permute-start(bf16[128,768]{1,0:T(8,128)(2,1)S(1)} %get-tuple-element.50.refs_4_), channel_id=1, source_target_pairs={{1,0},{7,6},{13,12},{19,18},{25,24},{31,30},{37,36},{43,42},{49,48... | collective-permute-start | bytes 589832 | tf_op jit(solution)/shard_map/pass_on/ppermute | solution.py:309
  69.6 1.3 %collective-permute-start.23 = (bf16[128,768]{1,0:T(8,128)(2,1)S(1)}, bf16[128,768]{1,0:T(8,128)(2,1)S(1)}, u32[]{:S(2)}, u32[]{:S(2)}) collective-permute-start(bf16[128,768]{1,0:T(8,128)(2,1)S(1)} %get-tuple-element.50.refs_4_), channel_id=1, source_target_pairs={{13,0},{19,6},{25,12},{31,18},{37,24},{43,30},{49,36},{55,42},{61,... | collective-permute-start | bytes 589832 | tf_op jit(solution)/shard_map/pass_on/ppermute | solution.py:309
  70.9 0.7 collective-permute-start.24
  71.6 1.3 %collective-permute-start.25 = (bf16[1,64,768]{2,1,0:T(8,128)(2,1)S(1)}, bf16[1,64,768]{2,1,0:T(8,128)(2,1)S(1)}, u32[]{:S(2)}, u32[]{:S(2)}) collective-permute-start(bf16[1,64,768]{2,1,0:T(8,128)(2,1)S(1)} %get-tuple-element.69), channel_id=1, source_target_pairs={{12,6},{24,18},{36,30},{48,42},{60,54},{72,66},{84,78},{96,90},{10... | collective-permute-start | bytes 294920 | tf_op jit(solution)/shard_map/window_above/ppermute | solution.py:309
  72.9 1.5 %collective-permute-start.21 = (bf16[64,768]{1,0:T(8,128)(2,1)S(1)}, bf16[64,768]{1,0:T(8,128)(2,1)S(1)}, u32[]{:S(2)}, u32[]{:S(2)}) collective-permute-start(bf16[64,768]{1,0:T(8,128)(2,1)S(1)} %get-tuple-element.54), channel_id=1, source_target_pairs={{757,0},{763,6},{1,12},{7,18},{13,24},{19,30},{25,36},{31,42},{37,... | collective-permute-start | bytes 294920 | tf_op jit(solution)/shard_map/pass_on/ppermute | solution.py:309
  74.4 3.1 %collective-permute-done.25.near1 = bf16[1,64,768]{2,1,0:T(8,128)(2,1)S(1)} collective-permute-done((bf16[1,64,768]{2,1,0:T(8,128)(2,1)S(1)}, bf16[1,64,768]{2,1,0:T(8,128)(2,1)S(1)}, u32[]{:S(2)}, u32[]{:S(2)}) %collective-permute-start.25) | collective-permute-done | bytes 98336 | tf_op jit(solution)/shard_map/window_above/ppermute | solution.py:309
  77.5 2.2 %prepare.5 = (bf16[128,1536]{1,0:T(8,128)(2,1)S(1)}, bf16[128,1536]{1,0:T(8,128)(2,1)S(1)}, bf16[3,256,512]{2,1,0:T(8,128)(2,1)S(1)}, bf16[3,512,128]{2,1,0:T(8,...) custom-call(s32[5]{0:T(128)S(1)} %stack.19.scalars, ...), custom_call_target="tpu_custom_call" | custom-call | tf_op jit(solution)/shard_map/window_above/prepare/pallas_call | solution.py:258
  79.7 0.7 split.1
  80.4 0.7 collective-permute-start.19
  81.1 0.7 collective-permute-start.20
  81.7 36.1 %collective-permute-done.21.low = bf16[64,768]{1,0:T(8,128)(2,1)S(1)} collective-permute-done((bf16[64,768]{1,0:T(8,128)(2,1)S(1)}, bf16[64,768]{1,0:T(8,128)(2,1)S(1)}, u32[]{:S(2)}, u32[]{:S(2)}) %collective-permute-start.21) | collective-permute-done | bytes 98336 | tf_op jit(solution)/shard_map/pass_on/ppermute | solution.py:309
  117.8 0.7 collective-permute-start.18
  118.5 4.0 %last_step.1 = (bf16[64,768]{1,0:T(8,128)(2,1)S(1)}, bf16[64,768]{1,0:T(8,128)(2,1)S(1)}) custom-call(s32[5]{0:T(128)S(1)} %stack.19.scalars, s32[1]{0:T(128)} %collective-permute-done.7.above, bf16[64,768]{1,0:T(8,128)(2,1)S(1)} %collective-permute-done.21.low, bf16[128,768]{1,0:T(8,128)(2,1)S(1)} %collective-permute-done.22.middle, ...), custom_call_target="tpu_custom_call" | custom-call | tf_op jit(solution)/shard_map/last_step/pallas_call | solution.py:258
  122.5 4.3 %collective-permute-start.26 = (bf16[64,768]{1,0:T(8,128)(2,1)S(1)}, bf16[64,768]{1,0:T(8,128)(2,1)S(1)}, u32[]{:S(2)}, u32[]{:S(2)}) collective-permute-start(bf16[64,768]{1,0:T(8,128)(2,1)S(1)} %get-tuple-element.62), channel_id=1, source_target_pairs={{0,6},{6,0},{12,18},{18,12},{24,30},{30,24},{36,42},{42,36},{48,54... | collective-permute-start | bytes 294920 | tf_op jit(solution)/shard_map/last_result/ppermute | solution.py:309
  126.8 0.1 fusion.5.forcing
  126.9 0.8 collective-permute-done.26.other_last
  127.7 1.4 %merge.1 = f32[2,64,768]{2,1,0:T(8,128)} custom-call(s32[5]{0:T(128)S(1)} %stack.19.scalars, bf16[64,768]{1,0:T(8,128)(2,1)S(1)} %get-tuple-element.51.own, bf16[64,768]{1,0:T(8,128)(2,1)S(1)} %collective-permute-done.18.other, bf16[64,768]{1,0:T(8,128)(2,1)S(1)} %collective-permute-done.19.near0, bf16[64,768]{1,0:T(8,128)(2,1)S(1)} %collective-permute-done.20.near1, ...), custom_call_target="tpu_custom_call" | custom-call | tf_op jit(solution)/shard_map/merge/pallas_call | solution.py:258
  (46 shorter events, 0.4 us)
Async XLA Ops:
  0.0 0.7 copy-start.7
  0.8 1.2 copy-start.4
  2.8 1.0 copy-start.5
  2.8 4.6 %collective-permute-start = (bf16[2,64,768]{2,1,0:T(8,128)(2,1)S(1)}, bf16[2,64,768]{2,1,0:T(8,128)(2,1)S(1)}, u32[]{:S(2)}, u32[]{:S(2)}) collective-permute-start(bf16[2,64,768]{2,1,0:T(8,128)(2,1)S(1)} %get-tuple-element.68), channel_id=1, source_target_pairs={{5,11},{11,5},{17,23},{23,17},{29,35},{35,29},{41,47},{47,41},{53,... | collective-permute-start | bytes 589832 | tf_op jit(solution)/shard_map/first_adjoint/ppermute | solution.py:309
  3.7 5.1 %copy-start.2 = (bf16[1,768,384]{2,1,0:T(8,128)(2,1)S(1)}, bf16[1,768,384]{2,1,0:T(8,128)(2,1)}, u32[]{:S(2)}) copy-start(bf16[1,768,384]{2,1,0:T(8,128)(2,1)} %param.16) | copy-start | bytes 1769476
  3.8 5.1 %copy-start = (bf16[1,768,384]{2,1,0:T(8,128)(2,1)S(1)}, bf16[1,768,384]{2,1,0:T(8,128)(2,1)}, u32[]{:S(2)}) copy-start(bf16[1,768,384]{2,1,0:T(8,128)(2,1)} %param.14) | copy-start | bytes 1769476
  3.8 5.1 %copy-start.1 = (bf16[1,768,384]{2,1,0:T(8,128)(2,1)S(1)}, bf16[1,768,384]{2,1,0:T(8,128)(2,1)}, u32[]{:S(2)}) copy-start(bf16[1,768,384]{2,1,0:T(8,128)(2,1)} %param.15) | copy-start | bytes 1769476
  3.8 7.3 %collective-permute-start.1 = (bf16[1,64,768]{2,1,0:T(8,128)(2,1)S(1)}, bf16[1,64,768]{2,1,0:T(8,128)(2,1)S(1)}, u32[]{:S(2)}, u32[]{:S(2)}) collective-permute-start(bf16[1,64,768]{2,1,0:T(8,128)(2,1)S(1)} %dynamic-slice_bitcast_fusion.1), channel_id=1, source_target_pairs={{5,11},{11,5},{17,23},{23,17},{29,35},{35,29},{41,47},{47,41},{53,... | collective-permute-start | bytes 294920 | tf_op jit(solution)/shard_map/first_adjoint/ppermute | solution.py:309
  4.6 4.2 %collective-permute-start.2 = (bf16[2,64,768]{2,1,0:T(8,128)(2,1)}, bf16[2,64,768]{2,1,0:T(8,128)(2,1)S(1)}, u32[]{:S(2)}, u32[]{:S(2)}) collective-permute-start(bf16[2,64,768]{2,1,0:T(8,128)(2,1)} %get-tuple-element.67), channel_id=1, source_target_pairs={{11,17},{23,29},{35,41},{47,53},{59,65},{71,77},{83,89},{95,101},{... | collective-permute-start | bytes 589832 | tf_op jit(solution)/shard_map/first_states/ppermute | solution.py:309
  5.3 3.5 %collective-permute-start.3 = (bf16[2,64,768]{2,1,0:T(8,128)(2,1)}, bf16[2,64,768]{2,1,0:T(8,128)(2,1)S(1)}, u32[]{:S(2)}, u32[]{:S(2)}) collective-permute-start(bf16[2,64,768]{2,1,0:T(8,128)(2,1)} %get-tuple-element.66), channel_id=1, source_target_pairs={{11,23},{23,35},{35,47},{47,59},{59,71},{71,83},{83,95},{95,107},{... | collective-permute-start | bytes 589832 | tf_op jit(solution)/shard_map/first_states/ppermute | solution.py:309
  6.7 4.4 %collective-permute-start.4 = (bf16[1,64,768]{2,1,0:T(8,128)(2,1)}, bf16[1,64,768]{2,1,0:T(8,128)(2,1)S(1)}, u32[]{:S(2)}, u32[]{:S(2)}) collective-permute-start(bf16[1,64,768]{2,1,0:T(8,128)(2,1)} %get-tuple-element.72), channel_id=1, source_target_pairs={{11,17},{23,29},{35,41},{47,53},{59,65},{71,77},{83,89},{90,101},{... | collective-permute-start | bytes 294920 | tf_op jit(solution)/shard_map/first_adjoint/ppermute | solution.py:309
  7.4 3.7 %collective-permute-start.5 = (bf16[1,64,768]{2,1,0:T(8,128)(2,1)}, bf16[1,64,768]{2,1,0:T(8,128)(2,1)S(1)}, u32[]{:S(2)}, u32[]{:S(2)}) collective-permute-start(bf16[1,64,768]{2,1,0:T(8,128)(2,1)} %get-tuple-element.71), channel_id=1, source_target_pairs={{11,23},{23,35},{35,47},{47,59},{59,71},{71,83},{83,95},{90,107},{... | collective-permute-start | bytes 294920 | tf_op jit(solution)/shard_map/first_adjoint/ppermute | solution.py:309
  8.9 2.2 %copy-start.3 = (bf16[1,384,768]{2,1,0:T(8,128)(2,1)S(1)}, bf16[1,384,768]{2,1,0:T(8,128)(2,1)}, u32[]{:S(2)}) copy-start(bf16[1,384,768]{2,1,0:T(8,128)(2,1)} %param.17) | copy-start | bytes 1769476
  13.7 17.0 %collective-permute-start.6 = (bf16[2,64,768]{2,1,0:T(8,128)(2,1)S(1)}, bf16[2,64,768]{2,1,0:T(8,128)(2,1)S(1)}, u32[]{:S(2)}, u32[]{:S(2)}) collective-permute-start(bf16[2,64,768]{2,1,0:T(8,128)(2,1)S(1)} %get-tuple-element.65), channel_id=1, source_target_pairs={{0,6},{1,7},{2,8},{3,9},{4,10},{6,0},{7,1},{8,2},{9,3},{10,4},{12,... | collective-permute-start | bytes 589832 | tf_op jit(solution)/shard_map/later_states/ppermute | solution.py:309
  26.1 5.9 %collective-permute-start.10 = (bf16[2,64,768]{2,1,0:T(8,128)(2,1)S(1)}, bf16[2,64,768]{2,1,0:T(8,128)(2,1)S(1)}, u32[]{:S(2)}, u32[]{:S(2)}) collective-permute-start(bf16[2,64,768]{2,1,0:T(8,128)(2,1)S(1)} %get-tuple-element.64), channel_id=1, source_target_pairs={{6,12},{7,13},{9,15},{18,24},{19,25},{21,27},{30,36},{31,37},{33,3... | collective-permute-start | bytes 589832 | tf_op jit(solution)/shard_map/later_states/ppermute | solution.py:309
  27.4 22.4 %collective-permute-start.11 = (bf16[2,64,768]{2,1,0:T(8,128)(2,1)S(1)}, bf16[2,64,768]{2,1,0:T(8,128)(2,1)S(1)}, u32[]{:S(2)}, u32[]{:S(2)}) collective-permute-start(bf16[2,64,768]{2,1,0:T(8,128)(2,1)S(1)} %get-tuple-element.63), channel_id=1, source_target_pairs={{6,18},{7,19},{9,21},{18,30},{19,31},{21,33},{30,42},{31,43},{33,4... | collective-permute-start | bytes 589832 | tf_op jit(solution)/shard_map/later_states/ppermute | solution.py:309
  29.3 22.7 %collective-permute-start.8 = (bf16[128,768]{1,0:T(8,128)(2,1)S(1)}, bf16[128,768]{1,0:T(8,128)(2,1)S(1)}, u32[]{:S(2)}, u32[]{:S(2)}) collective-permute-start(bf16[128,768]{1,0:T(8,128)(2,1)S(1)} %first_step.1.refs_0_), channel_id=1, source_target_pairs={{5,4},{11,10},{17,16},{23,22},{29,28},{35,34},{41,40},{47,46},{53,... | collective-permute-start | bytes 589832 | tf_op jit(solution)/shard_map/pass_on/ppermute | solution.py:309
  30.0 22.1 %collective-permute-start.9 = (bf16[128,768]{1,0:T(8,128)(2,1)S(1)}, bf16[128,768]{1,0:T(8,128)(2,1)S(1)}, u32[]{:S(2)}, u32[]{:S(2)}) collective-permute-start(bf16[128,768]{1,0:T(8,128)(2,1)S(1)} %first_step.1.refs_0_), channel_id=1, source_target_pairs={{17,4},{23,10},{29,16},{35,22},{41,28},{47,34},{53,40},{59,46},{65... | collective-permute-start | bytes 589832 | tf_op jit(solution)/shard_map/pass_on/ppermute | solution.py:309
  30.7 21.4 %collective-permute-start.7 = (s32[1]{0:T(128)}, s32[1]{0:T(128)}, u32[]{:S(2)}, u32[]{:S(2)}) collective-permute-start(s32[1]{0:T(128)} %param.12), channel_id=1, source_target_pairs={{1,0},{2,1},{3,2},{4,3},{5,4},{7,6},{8,7},{9,8},{10,9},{11,10},{13... | collective-permute-start | bytes 20 | tf_op jit(solution)/shard_map/shifts/ppermute | solution.py:375
  55.1 1.4 %collective-permute-start.12 = (bf16[128,768]{1,0:T(8,128)(2,1)S(1)}, bf16[128,768]{1,0:T(8,128)(2,1)S(1)}, u32[]{:S(2)}, u32[]{:S(2)}) collective-permute-start(bf16[128,768]{1,0:T(8,128)(2,1)S(1)} %step.4.refs_1_), channel_id=1, source_target_pairs={{760,3},{766,9},{4,15},{10,21},{16,27},{22,33},{28,39},{34,45},{40... | collective-permute-start | bytes 589832 | tf_op jit(solution)/shard_map/pass_on/ppermute | solution.py:309
  55.8 0.7 collective-permute-start.13
  59.5 1.4 %collective-permute-start.14 = (bf16[128,768]{1,0:T(8,128)(2,1)S(1)}, bf16[128,768]{1,0:T(8,128)(2,1)S(1)}, u32[]{:S(2)}, u32[]{:S(2)}) collective-permute-start(bf16[128,768]{1,0:T(8,128)(2,1)S(1)} %step.5.refs_2_), channel_id=1, source_target_pairs={{3,2},{9,8},{15,14},{21,20},{27,26},{33,32},{39,38},{45,44},{51,50... | collective-permute-start | bytes 589832 | tf_op jit(solution)/shard_map/pass_on/ppermute | solution.py:309
  60.2 0.7 collective-permute-start.15
  63.9 1.4 %collective-permute-start.16 = (bf16[128,768]{1,0:T(8,128)(2,1)S(1)}, bf16[128,768]{1,0:T(8,128)(2,1)S(1)}, u32[]{:S(2)}, u32[]{:S(2)}) collective-permute-start(bf16[128,768]{1,0:T(8,128)(2,1)S(1)} %step.6.refs_3_), channel_id=1, source_target_pairs={{758,1},{764,7},{2,13},{8,19},{14,25},{20,31},{26,37},{32,43},{38,... | collective-permute-start | bytes 589832 | tf_op jit(solution)/shard_map/pass_on/ppermute | solution.py:309
  64.6 0.7 collective-permute-start.17
  68.3 50.2 %collective-permute-start.22 = (bf16[128,768]{1,0:T(8,128)(2,1)S(1)}, bf16[128,768]{1,0:T(8,128)(2,1)S(1)}, u32[]{:S(2)}, u32[]{:S(2)}) collective-permute-start(bf16[128,768]{1,0:T(8,128)(2,1)S(1)} %get-tuple-element.50.refs_4_), channel_id=1, source_target_pairs={{1,0},{7,6},{13,12},{19,18},{25,24},{31,30},{37,36},{43,42},{49,48... | collective-permute-start | bytes 589832 | tf_op jit(solution)/shard_map/pass_on/ppermute | solution.py:309
  69.6 48.9 %collective-permute-start.23 = (bf16[128,768]{1,0:T(8,128)(2,1)S(1)}, bf16[128,768]{1,0:T(8,128)(2,1)S(1)}, u32[]{:S(2)}, u32[]{:S(2)}) collective-permute-start(bf16[128,768]{1,0:T(8,128)(2,1)S(1)} %get-tuple-element.50.refs_4_), channel_id=1, source_target_pairs={{13,0},{19,6},{25,12},{31,18},{37,24},{43,30},{49,36},{55,42},{61,... | collective-permute-start | bytes 589832 | tf_op jit(solution)/shard_map/pass_on/ppermute | solution.py:309
  70.9 3.5 %collective-permute-start.24 = (bf16[1,64,768]{2,1,0:T(8,128)(2,1)S(1)}, bf16[1,64,768]{2,1,0:T(8,128)(2,1)S(1)}, u32[]{:S(2)}, u32[]{:S(2)}) collective-permute-start(bf16[1,64,768]{2,1,0:T(8,128)(2,1)S(1)} %get-tuple-element.70), channel_id=1, source_target_pairs={{12,0},{24,12},{36,24},{48,36},{60,48},{72,60},{84,72},{96,84},{10... | collective-permute-start | bytes 294920 | tf_op jit(solution)/shard_map/window_above/ppermute | solution.py:309
  71.6 5.9 %collective-permute-start.25 = (bf16[1,64,768]{2,1,0:T(8,128)(2,1)S(1)}, bf16[1,64,768]{2,1,0:T(8,128)(2,1)S(1)}, u32[]{:S(2)}, u32[]{:S(2)}) collective-permute-start(bf16[1,64,768]{2,1,0:T(8,128)(2,1)S(1)} %get-tuple-element.69), channel_id=1, source_target_pairs={{12,6},{24,18},{36,30},{48,42},{60,54},{72,66},{84,78},{96,90},{10... | collective-permute-start | bytes 294920 | tf_op jit(solution)/shard_map/window_above/ppermute | solution.py:309
  72.9 44.9 %collective-permute-start.21 = (bf16[64,768]{1,0:T(8,128)(2,1)S(1)}, bf16[64,768]{1,0:T(8,128)(2,1)S(1)}, u32[]{:S(2)}, u32[]{:S(2)}) collective-permute-start(bf16[64,768]{1,0:T(8,128)(2,1)S(1)} %get-tuple-element.54), channel_id=1, source_target_pairs={{757,0},{763,6},{1,12},{7,18},{13,24},{19,30},{25,36},{31,42},{37,... | collective-permute-start | bytes 294920 | tf_op jit(solution)/shard_map/pass_on/ppermute | solution.py:309
  80.4 46.5 %collective-permute-start.19 = (bf16[64,768]{1,0:T(8,128)(2,1)S(1)}, bf16[64,768]{1,0:T(8,128)(2,1)S(1)}, u32[]{:S(2)}, u32[]{:S(2)}) collective-permute-start(bf16[64,768]{1,0:T(8,128)(2,1)S(1)} %get-tuple-element.53), channel_id=1, source_target_pairs={{13,7},{15,9},{17,11},{25,19},{27,21},{29,23},{37,31},{39,33},{41,... | collective-permute-start | bytes 294920 | tf_op jit(solution)/shard_map/earlier_results/ppermute | solution.py:309
  81.1 45.8 %collective-permute-start.20 = (bf16[64,768]{1,0:T(8,128)(2,1)S(1)}, bf16[64,768]{1,0:T(8,128)(2,1)S(1)}, u32[]{:S(2)}, u32[]{:S(2)}) collective-permute-start(bf16[64,768]{1,0:T(8,128)(2,1)S(1)} %get-tuple-element.53), channel_id=1, source_target_pairs={{19,7},{21,9},{23,11},{31,19},{33,21},{35,23},{43,31},{45,33},{47,... | collective-permute-start | bytes 294920 | tf_op jit(solution)/shard_map/earlier_results/ppermute | solution.py:309
  117.8 9.1 %collective-permute-start.18 = (bf16[64,768]{1,0:T(8,128)(2,1)S(1)}, bf16[64,768]{1,0:T(8,128)(2,1)S(1)}, u32[]{:S(2)}, u32[]{:S(2)}) collective-permute-start(bf16[64,768]{1,0:T(8,128)(2,1)S(1)} %get-tuple-element.52), channel_id=1, source_target_pairs={{1,7},{2,8},{3,9},{4,10},{5,11},{7,1},{8,2},{9,3},{10,4},{11,5},{1... | collective-permute-start | bytes 294920 | tf_op jit(solution)/shard_map/earlier_results/ppermute | solution.py:309
  118.5 8.3 %copy-start.6 = (bf16[1,2,8,8,768]{4,3,2,1,0:T(8,128)(2,1)S(1)}, bf16[1,2,8,8,768]{4,3,2,1,0:T(8,128)(2,1)}, u32[]{:S(2)}) copy-start(bf16[1,2,8,8,768]{4,3,2,1,0:T(8,128)(2,1)} %param.10) | copy-start | bytes 589828
  122.5 5.2 %collective-permute-start.26 = (bf16[64,768]{1,0:T(8,128)(2,1)S(1)}, bf16[64,768]{1,0:T(8,128)(2,1)S(1)}, u32[]{:S(2)}, u32[]{:S(2)}) collective-permute-start(bf16[64,768]{1,0:T(8,128)(2,1)S(1)} %get-tuple-element.62), channel_id=1, source_target_pairs={{0,6},{6,0},{12,18},{18,12},{24,30},{30,24},{36,42},{42,36},{48,54... | collective-permute-start | bytes 294920 | tf_op jit(solution)/shard_map/last_result/ppermute | solution.py:309

commit v4 on v3

--- a/solution.py
+++ b/solution.py
@@ -15,7 +15,6 @@
 BAND = 64
 SLOT = 128
 GROUP = 4
-RUN = 8
 
 
 def dot_nn(a, b):
@@ -159,20 +158,26 @@
     return change
 
 
-def first_kernel(scalars, own, final, other, final_other, near0, near1, final0, final1, *refs):
+def shift_kernel(scalars, above, moving):
+    for i in range(5):
+        moving[i] = scalars[i]
+    moving[5] = scalars[2] - above[0]
+
+
+def first_kernel(scalars, own, other, near0, near1, *refs):
     prepared, weights = refs[:6], refs[6:10]
     all_ref, rows = refs[10:]
     forcing = gathered(rows, scalars, own, other, near0, near1, 1)
-    adjoint = gathered(rows, scalars, final, final_other, final0, final1, 0)
+    adjoint = gathered(rows, scalars, own, other, near0, near1, 2)
     all_ref[...] = (adjoint + changed(adjoint, [prepared], *weights) + forcing).astype(BF)
 
 
-def step_kernel(scalars, above, low, high, *refs):
+def step_kernel(scalars, low, high, *refs):
     prepared, forcing, weights = refs[:6], refs[6], refs[7:11]
     outs, rows = refs[11:-1], refs[-1]
     rows[0:SLOT, :] = low[...].astype(FLT)
     rows[SLOT:, :] = high[...].astype(FLT)
-    start = BAND + (scalars[2] - above[0]) * WIN
+    start = BAND + scalars[5] * WIN
     adjoint = rows[pl.ds(pl.multiple_of(start, WIN), SLOT), :]
     change = changed(adjoint, [prepared], *weights)
     updated = (adjoint + change + forcing[...].astype(FLT)).astype(BF)
@@ -181,15 +186,14 @@
         outs[1][...] = updated[BAND:]
 
 
-def last_kernel(scalars, above, low, middle, high, *refs):
+def last_kernel(scalars, low, middle, high, *refs):
     units, weights = [refs[:6], refs[6:12]], refs[12:16]
     own_ref, swap_ref, rows = refs[16:]
     rows[0:BAND, :] = low[...].astype(FLT)
     rows[BAND : BAND + SLOT, :] = middle[...].astype(FLT)
     rows[BAND + SLOT : BAND + 2 * SLOT, :] = high[...].astype(FLT)
     rows[BAND + 2 * SLOT :, :] = jnp.zeros_like(rows[BAND + 2 * SLOT :, :])
-    core, offset = scalars[0], scalars[2]
-    shift = offset - above[0]
+    core, offset, shift = scalars[0], scalars[2], scalars[5]
     adjoint = rows[pl.ds(pl.multiple_of(BAND + shift * WIN, WIN), 2 * SLOT), :]
     rows[0 : 2 * SLOT, :] = adjoint + changed(adjoint, units, *weights)
     even = rows[pl.ds(pl.multiple_of(BAND - offset * WIN, WIN), BAND), :].astype(BF)
@@ -254,16 +258,16 @@
 ANY = pl.BlockSpec(memory_space=pl.ANY)
 
 
-def call(name, kernel, scalars, operands, shapes, scratch, place=VMEM, above=()):
+def call(name, kernel, scalars, operands, shapes, scratch, place=VMEM):
     return pl.pallas_call(
         kernel,
         out_shape=shapes,
-        in_specs=[SMEM] * (1 + len(above)) + [place] * len(operands),
+        in_specs=[SMEM] + [place] * len(operands),
         out_specs=[VMEM] * len(shapes),
         scratch_shapes=scratch,
         compiler_params=pltpu.CompilerParams(vmem_limit_bytes=40 * 1024 * 1024),
         name=name,
-    )(scalars, *above, *operands)
+    )(scalars, *operands)
 
 
 def prepare(scalars, operands, weights, last_slot, above=False, with_forcing=False):
@@ -326,32 +330,20 @@
     odd_up = [[(2 * j + 1, 2 * j + 2 + m) for j in range(chips)] for m in range(2)]
     swaps = [(b, b ^ 1) for b in range(bands)]
 
-    def begun(ways):
-        run = 2 * RUN
-        return [
-            (at(a, 0 if a // run != b // run else last), at(b, last)) for a, b in ways
-        ]
-
+    begin = jnp.concatenate([pair, flat(final_adjoint).astype(BF)], axis=1)
     with jax.named_scope("first_states"):
-        near = [sent(pair[m], moved(odd_up[m], [last])) for m in range(2)]
-    with jax.named_scope("first_adjoint"):
-        final, _ = lax.optimization_barrier((final_adjoint, pair))
-        final = flat(final).astype(BF)
-        final_near = [sent(final[m], begun(odd_up[m])) for m in range(2)]
+        near = [sent(begin[m], moved(odd_up[m], [last])) for m in range(2)]
         first_other = sent(
-            lax.dynamic_index_in_dim(pair, 1 - core, 0, keepdims=False), moved(swaps, [last])
-        )
-        final_other = sent(
-            lax.dynamic_index_in_dim(final, 1 - core, 0, keepdims=False), moved(swaps, [last])
+            lax.dynamic_index_in_dim(begin, 1 - core, 0, keepdims=False), moved(swaps, [last])
         )
     lift = jnp.where(section_at == 0, 0, (last - section_at) % 2)
     place = ints(core, chip, offset, section_at, lift)
-    prepared = prepare(place, (pair, first_other, *near), weights, chips - 1)
+    prepared = prepare(place, (begin, first_other, *near), weights, chips - 1)
     result = call(
         "first_step",
         first_kernel,
         place,
-        (pair, final, first_other, final_other, *near, *final_near, *prepared, *weights),
+        (begin, first_other, *near, *prepared, *weights),
         [struct((SLOT, width))],
         [pltpu.VMEM((3 * BAND, width), FLT)],
     )
@@ -373,9 +365,22 @@
         down = [(s, s - 1) for s in range(1, sections)]
         tied, _ = lax.optimization_barrier((shift_rows, later_other))
         above = lax.ppermute(tied, "section", down)
+        moving = pl.pallas_call(
+            shift_kernel,
+            out_shape=struct((6,), jnp.int32),
+            in_specs=[SMEM] * 2,
+            out_specs=SMEM,
+            compiler_params=pltpu.CompilerParams(vmem_limit_bytes=64 * 1024),
+            name="shift",
+        )(place, above)
     *prepared, forcing_here = prepare(
         place, (pair, later_other, *later_near), weights, chips - 1, with_forcing=True
     )
+    with jax.named_scope("window_above"):
+        x_later, _ = lax.optimization_barrier((x, later_other))
+        next0, next1 = [sent(x_later[m], moved(even_down[m], [0])) for m in range(2)]
+        extra = prepare(place, (pair, later_other, next0, next1), weights, chips - 1, above=True)
+    forcing_here, _ = lax.optimization_barrier((forcing_here, extra[0]))
     for tick in range(1, sections):
         source = sections - tick
         whole = result[0]
@@ -397,17 +402,13 @@
         result = call(
             "step",
             step_kernel,
-            place,
+            moving,
             (*((middle, side) if tick % 2 else (side, middle)), *prepared, forcing_here, *weights),
             shapes,
             [pltpu.VMEM((2 * SLOT, width), FLT)],
-            above=(above,),
         )
         results.append(result[0])
 
-    with jax.named_scope("window_above"):
-        next0, next1 = [sent(x[m], moved(even_down[m], [0])) for m in range(2)]
-        extra = prepare(place, (pair, later_other, next0, next1), weights, chips - 1, above=True)
     own, swap, lower = call(
         "split",
         split_kernel,
@@ -436,11 +437,10 @@
     own_last, swap_last = call(
         "last_step",
         last_kernel,
-        place,
+        moving,
         (from_low, middle, from_high, *prepared, *extra, *weights),
         [struct((BAND, width))] * 2,
         [pltpu.VMEM((6 * BAND, width), FLT)],
-        above=(above,),
     )
     with jax.named_scope("last_result"):
         other_last = sent(swap_last, moved(swaps, [0]))

time: 130 us -> 129 us (level)
  starting transfers between devices: 38.9 us -> 36.8 us
  waiting for transfers between devices: 57.8 us -> 59.6 us
  Pallas kernels: 27.2 us -> 25.7 us
    ppermute x26 -> x23, starting transfers between devices: 37.6 us -> 35.6 us  [sent(): return lax.ppermute(value, AXES, hops)]
    ppermute x1, waiting for transfers between devices: 0.01 us -> 1.87 us  [on_device(): above = lax.ppermute(tied, 'section', down)]
    pallas_call x11 -> x12, Pallas kernels: 27.2 us -> 25.7 us  [the longest x11 24 us: call(): pl.pallas_call(kernel, out_shape=shapes, in_specs=[SMEM] + [place] * len(...]
    ppermute x26 -> x23, waiting for transfers between devices: 57.8 us -> 57.8 us  [sent(): return lax.ppermute(value, AXES, hops)]
  transfers between devices with their start and end apart: 27 -> 24, of which waited for: 4 -> 4; matrix products, arithmetic and copies ran while one was open for 1% -> 1% of each run, Pallas kernels for 9% -> 8%
where the time goes in v4:
time: 129 us; the launch traced here: 128 us
  waiting for transfers between devices  59.6 us (46%)
  starting transfers between devices  36.8 us (29%)
  Pallas kernels  25.7 us (20%)
  local copies, waits for them, and re-layouts  2.6 us (2%)
  other arithmetic  2.29 us (2%)
    ppermute x23, waiting for transfers between devices, sent(): return lax.ppermute(value, AXES, hops)  57.8 us
    ppermute x23, starting transfers between devices, sent(): return lax.ppermute(value, AXES, hops)  35.6 us
    pallas_call x11, Pallas kernels, call(): pl.pallas_call(kernel, out_shape=shapes, in_specs=[SMEM] + [place] * len(...  24 us
  transfers between devices with their start and end apart: 24, of which 4 were waited for; matrix products, arithmetic and copies ran while one was open for 1% of the time, Pallas kernels for 8%

profile of v4, /device:TPU:1, one launch (start us, length us, event | category | flops | bytes accessed | tf_op | source)
XLA Modules:
  0.0 128.4 jit_solution(6522609155415370005)
XLA Ops:
  0.0 0.7 copy-done.8
  0.8 1.1 convert_bitcast_fusion.1
  1.9 0.1 fusion.2
  2.0 0.7 copy-done.5
  2.8 0.9 slice_bitcast_fusion
  3.7 0.8 collective-permute-start
  4.5 0.7 collective-permute-start.1
  5.2 0.7 collective-permute-start.2
  6.6 0.1 stack.19.scalars
  6.7 1.0 pad_maximum_fusion.1.own
  7.7 2.2 %prepare.3 = (bf16[128,1536]{1,0:T(8,128)(2,1)S(1)}, bf16[128,1536]{1,0:T(8,128)(2,1)S(1)}, bf16[3,256,512]{2,1,0:T(8,128)(2,1)S(1)}, bf16[3,512,128]{2,1,0:T(8,...) custom-call(s32[5]{0:T(128)S(1)} %stack.19.scalars, ...), custom_call_target="tpu_custom_call" | custom-call | tf_op jit(solution)/shard_map/prepare/pallas_call | solution.py:262
  9.9 2.5 %first_step.1.refs_0_ = bf16[128,768]{1,0:T(8,128)(2,1)S(1)} custom-call(s32[5]{0:T(128)S(1)} %stack.19.scalars, bf16[2,3,64,768]{3,2,1,0:T(8,128)(2,1)S(1)} %pad_maximum_fusion.own, bf16[3,64,768]{2,1,0:T(8,128)(2,1)S(1)} %collective-permute-done.other, bf16[3,64,768]{2,1,0:T(8,128)(2,1)S(1)} %collective-permute-done.1.near0, ...), custom_call_target="tpu_custom_call" | custom-call | tf_op jit(solution)/shard_map/first_step/pallas_call | solution.py:262
  12.5 12.4 %collective-permute-start.3 = (bf16[2,64,768]{2,1,0:T(8,128)(2,1)S(1)}, bf16[2,64,768]{2,1,0:T(8,128)(2,1)S(1)}, u32[]{:S(2)}, u32[]{:S(2)}) collective-permute-start(bf16[2,64,768]{2,1,0:T(8,128)(2,1)S(1)} %get-tuple-element.70), channel_id=1, source_target_pairs={{0,6},{1,7},{2,8},{3,9},{4,10},{6,0},{7,1},{8,2},{9,3},{10,4},{12,... | collective-permute-start | bytes 589832 | tf_op jit(solution)/shard_map/later_states/ppermute | solution.py:313
  24.9 0.7 collective-permute-start.5
  25.6 0.7 collective-permute-start.6
  26.3 1.3 %collective-permute-start.7 = (bf16[2,64,768]{2,1,0:T(8,128)(2,1)S(1)}, bf16[2,64,768]{2,1,0:T(8,128)(2,1)S(1)}, u32[]{:S(2)}, u32[]{:S(2)}) collective-permute-start(bf16[2,64,768]{2,1,0:T(8,128)(2,1)S(1)} %get-tuple-element.69), channel_id=1, source_target_pairs={{6,12},{7,13},{9,15},{18,24},{19,25},{21,27},{30,36},{31,37},{33,3... | collective-permute-start | bytes 589832 | tf_op jit(solution)/shard_map/later_states/ppermute | solution.py:313
  27.6 1.9 %collective-permute-start.8 = (bf16[2,64,768]{2,1,0:T(8,128)(2,1)S(1)}, bf16[2,64,768]{2,1,0:T(8,128)(2,1)S(1)}, u32[]{:S(2)}, u32[]{:S(2)}) collective-permute-start(bf16[2,64,768]{2,1,0:T(8,128)(2,1)S(1)} %get-tuple-element.68), channel_id=1, source_target_pairs={{6,18},{7,19},{9,21},{18,30},{19,31},{21,33},{30,42},{31,43},{33,4... | collective-permute-start | bytes 589832 | tf_op jit(solution)/shard_map/later_states/ppermute | solution.py:313
  29.6 1.3 %collective-permute-start.10 = (bf16[1,64,768]{2,1,0:T(8,128)(2,1)S(1)}, bf16[1,64,768]{2,1,0:T(8,128)(2,1)S(1)}, u32[]{:S(2)}, u32[]{:S(2)}) collective-permute-start(bf16[1,64,768]{2,1,0:T(8,128)(2,1)S(1)} %get-tuple-element.71), channel_id=1, source_target_pairs={{12,6},{24,18},{36,30},{48,42},{60,54},{72,66},{84,78},{96,90},{10... | collective-permute-start | bytes 294920 | tf_op jit(solution)/shard_map/window_above/ppermute | solution.py:313
  30.9 0.7 collective-permute-start.9
  31.5 13.7 %collective-permute-done.8.near1 = bf16[2,64,768]{2,1,0:T(8,128)(2,1)S(1)} collective-permute-done((bf16[2,64,768]{2,1,0:T(8,128)(2,1)S(1)}, bf16[2,64,768]{2,1,0:T(8,128)(2,1)S(1)}, u32[]{:S(2)}, u32[]{:S(2)}) %collective-permute-start.8) | collective-permute-done | bytes 196640 | tf_op jit(solution)/shard_map/later_states/ppermute | solution.py:313
  45.2 1.3 collective-permute-start.4
  46.5 2.3 %prepare.4 = (bf16[128,1536]{1,0:T(8,128)(2,1)S(1)}, bf16[128,1536]{1,0:T(8,128)(2,1)S(1)}, bf16[3,256,512]{2,1,0:T(8,128)(2,1)S(1)}, bf16[3,512,128]{2,1,0:T(8,...) custom-call(s32[5]{0:T(128)S(1)} %stack.19.scalars, ...), custom_call_target="tpu_custom_call" | custom-call | tf_op jit(solution)/shard_map/prepare/pallas_call | solution.py:262
  48.8 1.9 %collective-permute-done.4.above = s32[1]{0:T(128)} collective-permute-done((s32[1]{0:T(128)}, s32[1]{0:T(128)}, u32[]{:S(2)}, u32[]{:S(2)}) %collective-permute-start.4) | collective-permute-done | bytes 36 | tf_op jit(solution)/shard_map/shifts/ppermute | solution.py:367
  50.7 1.8 %shift.1.scalars = s32[6]{0:T(128)S(1)} custom-call(s32[5]{0:T(128)S(1)} %stack.19.scalars, s32[1]{0:T(128)} %collective-permute-done.4.above), custom_call_target="tpu_custom_call" | custom-call | tf_op jit(solution)/shard_map/shifts/shift/pallas_call | solution.py:368
  52.5 2.2 %prepare.5 = (bf16[128,1536]{1,0:T(8,128)(2,1)S(1)}, bf16[128,1536]{1,0:T(8,128)(2,1)S(1)}, bf16[3,256,512]{2,1,0:T(8,128)(2,1)S(1)}, bf16[3,512,128]{2,1,0:T(8,...) custom-call(s32[5]{0:T(128)S(1)} %stack.19.scalars, ...), custom_call_target="tpu_custom_call" | custom-call | tf_op jit(solution)/shard_map/window_above/prepare/pallas_call | solution.py:262
  54.8 2.4 %step.4.refs_1_ = bf16[128,768]{1,0:T(8,128)(2,1)S(1)} custom-call(s32[6]{0:T(128)S(1)} %shift.1.scalars, bf16[128,768]{1,0:T(8,128)(2,1)S(1)} %collective-permute-done.5.low, bf16[128,768]{1,0:T(8,128)(2,1)S(1)} %collective-permute-done.6.high, bf16[128,1536]{1,0:T(8,128)(2,1)S(1)} %get-tuple-element.43.refs_0_, ...), custom_call_target="tpu_custom_call" | custom-call | tf_op jit(solution)/shard_map/step/pallas_call | solution.py:262
  57.1 0.7 collective-permute-start.11
  57.8 0.7 collective-permute-start.12
  58.5 2.4 %step.5.refs_2_ = bf16[128,768]{1,0:T(8,128)(2,1)S(1)} custom-call(s32[6]{0:T(128)S(1)} %shift.1.scalars, bf16[128,768]{1,0:T(8,128)(2,1)S(1)} %collective-permute-done.11.low, bf16[128,768]{1,0:T(8,128)(2,1)S(1)} %collective-permute-done.12.high, bf16[128,1536]{1,0:T(8,128)(2,1)S(1)} %get-tuple-element.43.refs_0_, ...), custom_call_target="tpu_custom_call" | custom-call | tf_op jit(solution)/shard_map/step/pallas_call | solution.py:262
  60.9 0.7 collective-permute-start.13
  61.5 0.7 collective-permute-start.14
  62.3 2.4 %step.6.refs_3_ = bf16[128,768]{1,0:T(8,128)(2,1)S(1)} custom-call(s32[6]{0:T(128)S(1)} %shift.1.scalars, bf16[128,768]{1,0:T(8,128)(2,1)S(1)} %collective-permute-done.13.low, bf16[128,768]{1,0:T(8,128)(2,1)S(1)} %collective-permute-done.14.high, bf16[128,1536]{1,0:T(8,128)(2,1)S(1)} %get-tuple-element.43.refs_0_, ...), custom_call_target="tpu_custom_call" | custom-call | tf_op jit(solution)/shard_map/step/pallas_call | solution.py:262
  64.6 0.7 collective-permute-start.15
  65.3 0.9 collective-permute-start.16
  66.2 2.4 %step.7 = (bf16[128,768]{1,0:T(8,128)(2,1)S(1)}, bf16[64,768]{1,0:T(8,128)(2,1)S(1)}) custom-call(s32[6]{0:T(128)S(1)} %shift.1.scalars, bf16[128,768]{1,0:T(8,128)(2,1)S(1)} %collective-permute-done.15.low, bf16[128,768]{1,0:T(8,128)(2,1)S(1)} %collective-permute-done.16.high, bf16[128,1536]{1,0:T(8,128)(2,1)S(1)} %get-tuple-element.43.refs_0_, ...), custom_call_target="tpu_custom_call" | custom-call | tf_op jit(solution)/shard_map/step/pallas_call | solution.py:262
  68.5 1.3 %collective-permute-start.21 = (bf16[128,768]{1,0:T(8,128)(2,1)S(1)}, bf16[128,768]{1,0:T(8,128)(2,1)S(1)}, u32[]{:S(2)}, u32[]{:S(2)}) collective-permute-start(bf16[128,768]{1,0:T(8,128)(2,1)S(1)} %get-tuple-element.53.refs_4_), channel_id=1, source_target_pairs={{1,0},{7,6},{13,12},{19,18},{25,24},{31,30},{37,36},{43,42},{49,48... | collective-permute-start | bytes 589832 | tf_op jit(solution)/shard_map/pass_on/ppermute | solution.py:313
  69.8 1.3 %collective-permute-start.22 = (bf16[128,768]{1,0:T(8,128)(2,1)S(1)}, bf16[128,768]{1,0:T(8,128)(2,1)S(1)}, u32[]{:S(2)}, u32[]{:S(2)}) collective-permute-start(bf16[128,768]{1,0:T(8,128)(2,1)S(1)} %get-tuple-element.53.refs_4_), channel_id=1, source_target_pairs={{13,0},{19,6},{25,12},{31,18},{37,24},{43,30},{49,36},{55,42},{61,... | collective-permute-start | bytes 589832 | tf_op jit(solution)/shard_map/pass_on/ppermute | solution.py:313
  71.1 1.3 %collective-permute-start.20 = (bf16[64,768]{1,0:T(8,128)(2,1)S(1)}, bf16[64,768]{1,0:T(8,128)(2,1)S(1)}, u32[]{:S(2)}, u32[]{:S(2)}) collective-permute-start(bf16[64,768]{1,0:T(8,128)(2,1)S(1)} %get-tuple-element.57), channel_id=1, source_target_pairs={{757,0},{763,6},{1,12},{7,18},{13,24},{19,30},{25,36},{31,42},{37,... | collective-permute-start | bytes 294920 | tf_op jit(solution)/shard_map/pass_on/ppermute | solution.py:313
  72.4 0.7 split.1
  73.1 0.7 collective-permute-start.18
  73.8 0.7 collective-permute-start.19
  74.5 43.2 %collective-permute-done.20.low = bf16[64,768]{1,0:T(8,128)(2,1)S(1)} collective-permute-done((bf16[64,768]{1,0:T(8,128)(2,1)S(1)}, bf16[64,768]{1,0:T(8,128)(2,1)S(1)}, u32[]{:S(2)}, u32[]{:S(2)}) %collective-permute-start.20) | collective-permute-done | bytes 98336 | tf_op jit(solution)/shard_map/pass_on/ppermute | solution.py:313
  117.7 0.7 collective-permute-start.17
  118.4 3.3 %last_step.1 = (bf16[64,768]{1,0:T(8,128)(2,1)S(1)}, bf16[64,768]{1,0:T(8,128)(2,1)S(1)}) custom-call(s32[6]{0:T(128)S(1)} %shift.1.scalars, bf16[64,768]{1,0:T(8,128)(2,1)S(1)} %collective-permute-done.20.low, bf16[128,768]{1,0:T(8,128)(2,1)S(1)} %collective-permute-done.21.middle, bf16[128,768]{1,0:T(8,128)(2,1)S(1)} %collective-permute-done.22.high, ...), custom_call_target="tpu_custom_call" | custom-call | tf_op jit(solution)/shard_map/last_step/pallas_call | solution.py:262
  121.7 4.4 %collective-permute-start.23 = (bf16[64,768]{1,0:T(8,128)(2,1)S(1)}, bf16[64,768]{1,0:T(8,128)(2,1)S(1)}, u32[]{:S(2)}, u32[]{:S(2)}) collective-permute-start(bf16[64,768]{1,0:T(8,128)(2,1)S(1)} %get-tuple-element.64), channel_id=1, source_target_pairs={{0,6},{6,0},{12,18},{18,12},{24,30},{30,24},{36,42},{42,36},{48,54... | collective-permute-start | bytes 294920 | tf_op jit(solution)/shard_map/last_result/ppermute | solution.py:313
  126.1 0.1 fusion.5.forcing
  126.2 0.8 collective-permute-done.23.other_last
  127.0 1.4 %merge.1 = f32[2,64,768]{2,1,0:T(8,128)} custom-call(s32[5]{0:T(128)S(1)} %stack.19.scalars, bf16[64,768]{1,0:T(8,128)(2,1)S(1)} %get-tuple-element.54.own, bf16[64,768]{1,0:T(8,128)(2,1)S(1)} %collective-permute-done.17.other, bf16[64,768]{1,0:T(8,128)(2,1)S(1)} %collective-permute-done.18.near0, bf16[64,768]{1,0:T(8,128)(2,1)S(1)} %collective-permute-done.19.near1, ...), custom_call_target="tpu_custom_call" | custom-call | tf_op jit(solution)/shard_map/merge/pallas_call | solution.py:262
  (41 shorter events, 0.3 us)
Async XLA Ops:
  0.0 0.7 copy-start.8
  0.8 1.1 copy-start.4
  0.8 1.1 copy-start.6
  2.0 0.7 copy-start.5
  2.8 4.9 %copy-start.1 = (bf16[1,768,384]{2,1,0:T(8,128)(2,1)S(1)}, bf16[1,768,384]{2,1,0:T(8,128)(2,1)}, u32[]{:S(2)}) copy-start(bf16[1,768,384]{2,1,0:T(8,128)(2,1)} %param.15) | copy-start | bytes 1769476
  2.8 4.9 %copy-start.2 = (bf16[1,768,384]{2,1,0:T(8,128)(2,1)S(1)}, bf16[1,768,384]{2,1,0:T(8,128)(2,1)}, u32[]{:S(2)}) copy-start(bf16[1,768,384]{2,1,0:T(8,128)(2,1)} %param.16) | copy-start | bytes 1769476
  3.7 4.0 %copy-start = (bf16[1,768,384]{2,1,0:T(8,128)(2,1)S(1)}, bf16[1,768,384]{2,1,0:T(8,128)(2,1)}, u32[]{:S(2)}) copy-start(bf16[1,768,384]{2,1,0:T(8,128)(2,1)} %param.14) | copy-start | bytes 1769476
  3.7 3.9 %collective-permute-start = (bf16[3,64,768]{2,1,0:T(8,128)(2,1)}, bf16[3,64,768]{2,1,0:T(8,128)(2,1)S(1)}, u32[]{:S(2)}, u32[]{:S(2)}) collective-permute-start(bf16[3,64,768]{2,1,0:T(8,128)(2,1)} %get-tuple-element.67), channel_id=1, source_target_pairs={{5,11},{11,5},{17,23},{23,17},{29,35},{35,29},{41,47},{47,41},{53,... | collective-permute-start | bytes 884744 | tf_op jit(solution)/shard_map/first_states/ppermute | solution.py:313
  4.5 3.1 %collective-permute-start.1 = (bf16[3,64,768]{2,1,0:T(8,128)(2,1)}, bf16[3,64,768]{2,1,0:T(8,128)(2,1)S(1)}, u32[]{:S(2)}, u32[]{:S(2)}) collective-permute-start(bf16[3,64,768]{2,1,0:T(8,128)(2,1)} %get-tuple-element.66), channel_id=1, source_target_pairs={{11,17},{23,29},{35,41},{47,53},{59,65},{71,77},{83,89},{95,101},{... | collective-permute-start | bytes 884744 | tf_op jit(solution)/shard_map/first_states/ppermute | solution.py:313
  5.2 2.5 %collective-permute-start.2 = (bf16[3,64,768]{2,1,0:T(8,128)(2,1)}, bf16[3,64,768]{2,1,0:T(8,128)(2,1)S(1)}, u32[]{:S(2)}, u32[]{:S(2)}) collective-permute-start(bf16[3,64,768]{2,1,0:T(8,128)(2,1)} %get-tuple-element.65), channel_id=1, source_target_pairs={{11,23},{23,35},{35,47},{47,59},{59,71},{71,83},{83,95},{95,107},{... | collective-permute-start | bytes 884744 | tf_op jit(solution)/shard_map/first_states/ppermute | solution.py:313
  7.7 2.2 %copy-start.3 = (bf16[1,384,768]{2,1,0:T(8,128)(2,1)S(1)}, bf16[1,384,768]{2,1,0:T(8,128)(2,1)}, u32[]{:S(2)}) copy-start(bf16[1,384,768]{2,1,0:T(8,128)(2,1)} %param.17) | copy-start | bytes 1769476
  12.5 17.0 %collective-permute-start.3 = (bf16[2,64,768]{2,1,0:T(8,128)(2,1)S(1)}, bf16[2,64,768]{2,1,0:T(8,128)(2,1)S(1)}, u32[]{:S(2)}, u32[]{:S(2)}) collective-permute-start(bf16[2,64,768]{2,1,0:T(8,128)(2,1)S(1)} %get-tuple-element.70), channel_id=1, source_target_pairs={{0,6},{1,7},{2,8},{3,9},{4,10},{6,0},{7,1},{8,2},{9,3},{10,4},{12,... | collective-permute-start | bytes 589832 | tf_op jit(solution)/shard_map/later_states/ppermute | solution.py:313
  24.9 29.8 %collective-permute-start.5 = (bf16[128,768]{1,0:T(8,128)(2,1)S(1)}, bf16[128,768]{1,0:T(8,128)(2,1)S(1)}, u32[]{:S(2)}, u32[]{:S(2)}) collective-permute-start(bf16[128,768]{1,0:T(8,128)(2,1)S(1)} %first_step.1.refs_0_), channel_id=1, source_target_pairs={{5,4},{11,10},{17,16},{23,22},{29,28},{35,34},{41,40},{47,46},{53,... | collective-permute-start | bytes 589832 | tf_op jit(solution)/shard_map/pass_on/ppermute | solution.py:313
  25.6 29.1 %collective-permute-start.6 = (bf16[128,768]{1,0:T(8,128)(2,1)S(1)}, bf16[128,768]{1,0:T(8,128)(2,1)S(1)}, u32[]{:S(2)}, u32[]{:S(2)}) collective-permute-start(bf16[128,768]{1,0:T(8,128)(2,1)S(1)} %first_step.1.refs_0_), channel_id=1, source_target_pairs={{17,4},{23,10},{29,16},{35,22},{41,28},{47,34},{53,40},{59,46},{65... | collective-permute-start | bytes 589832 | tf_op jit(solution)/shard_map/pass_on/ppermute | solution.py:313
  26.3 4.6 %collective-permute-start.7 = (bf16[2,64,768]{2,1,0:T(8,128)(2,1)S(1)}, bf16[2,64,768]{2,1,0:T(8,128)(2,1)S(1)}, u32[]{:S(2)}, u32[]{:S(2)}) collective-permute-start(bf16[2,64,768]{2,1,0:T(8,128)(2,1)S(1)} %get-tuple-element.69), channel_id=1, source_target_pairs={{6,12},{7,13},{9,15},{18,24},{19,25},{21,27},{30,36},{31,37},{33,3... | collective-permute-start | bytes 589832 | tf_op jit(solution)/shard_map/later_states/ppermute | solution.py:313
  27.6 17.6 %collective-permute-start.8 = (bf16[2,64,768]{2,1,0:T(8,128)(2,1)S(1)}, bf16[2,64,768]{2,1,0:T(8,128)(2,1)S(1)}, u32[]{:S(2)}, u32[]{:S(2)}) collective-permute-start(bf16[2,64,768]{2,1,0:T(8,128)(2,1)S(1)} %get-tuple-element.68), channel_id=1, source_target_pairs={{6,18},{7,19},{9,21},{18,30},{19,31},{21,33},{30,42},{31,43},{33,4... | collective-permute-start | bytes 589832 | tf_op jit(solution)/shard_map/later_states/ppermute | solution.py:313
  29.6 22.9 %collective-permute-start.10 = (bf16[1,64,768]{2,1,0:T(8,128)(2,1)S(1)}, bf16[1,64,768]{2,1,0:T(8,128)(2,1)S(1)}, u32[]{:S(2)}, u32[]{:S(2)}) collective-permute-start(bf16[1,64,768]{2,1,0:T(8,128)(2,1)S(1)} %get-tuple-element.71), channel_id=1, source_target_pairs={{12,6},{24,18},{36,30},{48,42},{60,54},{72,66},{84,78},{96,90},{10... | collective-permute-start | bytes 294920 | tf_op jit(solution)/shard_map/window_above/ppermute | solution.py:313
  30.9 21.6 %collective-permute-start.9 = (bf16[1,64,768]{2,1,0:T(8,128)(2,1)S(1)}, bf16[1,64,768]{2,1,0:T(8,128)(2,1)S(1)}, u32[]{:S(2)}, u32[]{:S(2)}) collective-permute-start(bf16[1,64,768]{2,1,0:T(8,128)(2,1)S(1)} %get-tuple-element.72), channel_id=1, source_target_pairs={{12,0},{24,12},{36,24},{48,36},{60,48},{72,60},{84,72},{96,84},{10... | collective-permute-start | bytes 294920 | tf_op jit(solution)/shard_map/window_above/ppermute | solution.py:313
  45.2 5.5 %collective-permute-start.4 = (s32[1]{0:T(128)}, s32[1]{0:T(128)}, u32[]{:S(2)}, u32[]{:S(2)}) collective-permute-start(s32[1]{0:T(128)} %param.12), channel_id=1, source_target_pairs={{1,0},{2,1},{3,2},{4,3},{5,4},{7,6},{8,7},{9,8},{10,9},{11,10},{13... | collective-permute-start | bytes 20 | tf_op jit(solution)/shard_map/shifts/ppermute | solution.py:367
  57.1 1.4 %collective-permute-start.11 = (bf16[128,768]{1,0:T(8,128)(2,1)S(1)}, bf16[128,768]{1,0:T(8,128)(2,1)S(1)}, u32[]{:S(2)}, u32[]{:S(2)}) collective-permute-start(bf16[128,768]{1,0:T(8,128)(2,1)S(1)} %step.4.refs_1_), channel_id=1, source_target_pairs={{760,3},{766,9},{4,15},{10,21},{16,27},{22,33},{28,39},{34,45},{40... | collective-permute-start | bytes 589832 | tf_op jit(solution)/shard_map/pass_on/ppermute | solution.py:313
  57.8 0.7 collective-permute-start.12
  60.9 1.4 %collective-permute-start.13 = (bf16[128,768]{1,0:T(8,128)(2,1)S(1)}, bf16[128,768]{1,0:T(8,128)(2,1)S(1)}, u32[]{:S(2)}, u32[]{:S(2)}) collective-permute-start(bf16[128,768]{1,0:T(8,128)(2,1)S(1)} %step.5.refs_2_), channel_id=1, source_target_pairs={{3,2},{9,8},{15,14},{21,20},{27,26},{33,32},{39,38},{45,44},{51,50... | collective-permute-start | bytes 589832 | tf_op jit(solution)/shard_map/pass_on/ppermute | solution.py:313
  61.5 0.7 collective-permute-start.14
  64.6 1.5 %collective-permute-start.15 = (bf16[128,768]{1,0:T(8,128)(2,1)S(1)}, bf16[128,768]{1,0:T(8,128)(2,1)S(1)}, u32[]{:S(2)}, u32[]{:S(2)}) collective-permute-start(bf16[128,768]{1,0:T(8,128)(2,1)S(1)} %step.6.refs_3_), channel_id=1, source_target_pairs={{758,1},{764,7},{2,13},{8,19},{14,25},{20,31},{26,37},{32,43},{38,... | collective-permute-start | bytes 589832 | tf_op jit(solution)/shard_map/pass_on/ppermute | solution.py:313
  65.3 0.9 collective-permute-start.16
  68.5 49.8 %collective-permute-start.21 = (bf16[128,768]{1,0:T(8,128)(2,1)S(1)}, bf16[128,768]{1,0:T(8,128)(2,1)S(1)}, u32[]{:S(2)}, u32[]{:S(2)}) collective-permute-start(bf16[128,768]{1,0:T(8,128)(2,1)S(1)} %get-tuple-element.53.refs_4_), channel_id=1, source_target_pairs={{1,0},{7,6},{13,12},{19,18},{25,24},{31,30},{37,36},{43,42},{49,48... | collective-permute-start | bytes 589832 | tf_op jit(solution)/shard_map/pass_on/ppermute | solution.py:313
  69.8 48.5 %collective-permute-start.22 = (bf16[128,768]{1,0:T(8,128)(2,1)S(1)}, bf16[128,768]{1,0:T(8,128)(2,1)S(1)}, u32[]{:S(2)}, u32[]{:S(2)}) collective-permute-start(bf16[128,768]{1,0:T(8,128)(2,1)S(1)} %get-tuple-element.53.refs_4_), channel_id=1, source_target_pairs={{13,0},{19,6},{25,12},{31,18},{37,24},{43,30},{49,36},{55,42},{61,... | collective-permute-start | bytes 589832 | tf_op jit(solution)/shard_map/pass_on/ppermute | solution.py:313
  71.1 46.6 %collective-permute-start.20 = (bf16[64,768]{1,0:T(8,128)(2,1)S(1)}, bf16[64,768]{1,0:T(8,128)(2,1)S(1)}, u32[]{:S(2)}, u32[]{:S(2)}) collective-permute-start(bf16[64,768]{1,0:T(8,128)(2,1)S(1)} %get-tuple-element.57), channel_id=1, source_target_pairs={{757,0},{763,6},{1,12},{7,18},{13,24},{19,30},{25,36},{31,42},{37,... | collective-permute-start | bytes 294920 | tf_op jit(solution)/shard_map/pass_on/ppermute | solution.py:313
  73.1 53.1 %collective-permute-start.18 = (bf16[64,768]{1,0:T(8,128)(2,1)S(1)}, bf16[64,768]{1,0:T(8,128)(2,1)S(1)}, u32[]{:S(2)}, u32[]{:S(2)}) collective-permute-start(bf16[64,768]{1,0:T(8,128)(2,1)S(1)} %get-tuple-element.56), channel_id=1, source_target_pairs={{13,7},{15,9},{17,11},{25,19},{27,21},{29,23},{37,31},{39,33},{41,... | collective-permute-start | bytes 294920 | tf_op jit(solution)/shard_map/earlier_results/ppermute | solution.py:313
  73.8 52.4 %collective-permute-start.19 = (bf16[64,768]{1,0:T(8,128)(2,1)S(1)}, bf16[64,768]{1,0:T(8,128)(2,1)S(1)}, u32[]{:S(2)}, u32[]{:S(2)}) collective-permute-start(bf16[64,768]{1,0:T(8,128)(2,1)S(1)} %get-tuple-element.56), channel_id=1, source_target_pairs={{19,7},{21,9},{23,11},{31,19},{33,21},{35,23},{43,31},{45,33},{47,... | collective-permute-start | bytes 294920 | tf_op jit(solution)/shard_map/earlier_results/ppermute | solution.py:313
  117.7 8.5 %collective-permute-start.17 = (bf16[64,768]{1,0:T(8,128)(2,1)S(1)}, bf16[64,768]{1,0:T(8,128)(2,1)S(1)}, u32[]{:S(2)}, u32[]{:S(2)}) collective-permute-start(bf16[64,768]{1,0:T(8,128)(2,1)S(1)} %get-tuple-element.55), channel_id=1, source_target_pairs={{1,7},{2,8},{3,9},{4,10},{5,11},{7,1},{8,2},{9,3},{10,4},{11,5},{1... | collective-permute-start | bytes 294920 | tf_op jit(solution)/shard_map/earlier_results/ppermute | solution.py:313
  118.4 7.7 %copy-start.7 = (bf16[1,2,8,8,768]{4,3,2,1,0:T(8,128)(2,1)S(1)}, bf16[1,2,8,8,768]{4,3,2,1,0:T(8,128)(2,1)}, u32[]{:S(2)}) copy-start(bf16[1,2,8,8,768]{4,3,2,1,0:T(8,128)(2,1)} %param.10) | copy-start | bytes 589828
  121.7 5.3 %collective-permute-start.23 = (bf16[64,768]{1,0:T(8,128)(2,1)S(1)}, bf16[64,768]{1,0:T(8,128)(2,1)S(1)}, u32[]{:S(2)}, u32[]{:S(2)}) collective-permute-start(bf16[64,768]{1,0:T(8,128)(2,1)S(1)} %get-tuple-element.64), channel_id=1, source_target_pairs={{0,6},{6,0},{12,18},{18,12},{24,30},{30,24},{36,42},{42,36},{48,54... | collective-permute-start | bytes 294920 | tf_op jit(solution)/shard_map/last_result/ppermute | solution.py:313

commit v5 on v4

--- a/solution.py
+++ b/solution.py
@@ -258,7 +258,18 @@
 ANY = pl.BlockSpec(memory_space=pl.ANY)
 
 
-def call(name, kernel, scalars, operands, shapes, scratch, place=VMEM):
+def gated(kernel, section):
+    def body(scalars, *refs):
+        @pl.when(scalars[3] == section)
+        def _():
+            kernel(scalars, *refs)
+
+    return body
+
+
+def call(name, kernel, scalars, operands, shapes, scratch, place=VMEM, only=None):
+    if only is not None:
+        kernel = gated(kernel, only)
     return pl.pallas_call(
         kernel,
         out_shape=shapes,
@@ -270,7 +281,7 @@
     )(scalars, *operands)
 
 
-def prepare(scalars, operands, weights, last_slot, above=False, with_forcing=False):
+def prepare(scalars, operands, weights, last_slot, above=False, with_forcing=False, only=None):
     width, hidden = weights[0].shape
     keys = hidden // HD * SLOT
     shapes = [
@@ -290,6 +301,7 @@
         (*operands, *weights[:3]),
         shapes,
         [pltpu.VMEM((3 * BAND, width), FLT)],
+        only=only,
     )
 
 
@@ -338,7 +350,7 @@
         )
     lift = jnp.where(section_at == 0, 0, (last - section_at) % 2)
     place = ints(core, chip, offset, section_at, lift)
-    prepared = prepare(place, (begin, first_other, *near), weights, chips - 1)
+    prepared = prepare(place, (begin, first_other, *near), weights, chips - 1, only=last)
     result = call(
         "first_step",
         first_kernel,
@@ -346,6 +358,7 @@
         (begin, first_other, *near, *prepared, *weights),
         [struct((SLOT, width))],
         [pltpu.VMEM((3 * BAND, width), FLT)],
+        only=last,
     )
     results = [result[0]]
     with jax.named_scope("later_states"):
@@ -379,7 +392,7 @@
     with jax.named_scope("window_above"):
         x_later, _ = lax.optimization_barrier((x, later_other))
         next0, next1 = [sent(x_later[m], moved(even_down[m], [0])) for m in range(2)]
-        extra = prepare(place, (pair, later_other, next0, next1), weights, chips - 1, above=True)
+        extra = prepare(place, (pair, later_other, next0, next1), weights, chips - 1, above=True, only=0)
     forcing_here, _ = lax.optimization_barrier((forcing_here, extra[0]))
     for tick in range(1, sections):
         source = sections - tick

time: 129 us -> 126 us (0.977)
  Pallas kernels: 25.7 us -> 22.3 us
  starting transfers between devices: 36.8 us -> 39.3 us
  waiting for transfers between devices: 59.6 us -> 57.7 us
    ppermute x23, waiting for transfers between devices: 57.8 us -> 52.9 us  [sent(): return lax.ppermute(value, AXES, hops)]
    pallas_call x11, Pallas kernels: 24 us -> 20.5 us  [call(): pl.pallas_call(kernel, out_shape=shapes, in_specs=[SMEM] + [place] * len(...]
    ppermute x1, waiting for transfers between devices: 1.87 us -> 4.77 us  [on_device(): above = lax.ppermute(tied, 'section', down)]
    ppermute x23, starting transfers between devices: 35.6 us -> 38 us  [sent(): return lax.ppermute(value, AXES, hops)]
where the time goes in v5:
time: 126 us
  waiting for transfers between devices  57.7 us (46%)
  starting transfers between devices  39.3 us (31%)
  Pallas kernels  22.3 us (18%)
  local copies, waits for them, and re-layouts  3.1 us (2%)
  other arithmetic  2.29 us (2%)
    ppermute x23, waiting for transfers between devices, sent(): return lax.ppermute(value, AXES, hops)  52.9 us
    ppermute x23, starting transfers between devices, sent(): return lax.ppermute(value, AXES, hops)  38 us
    pallas_call x11, Pallas kernels, call(): pl.pallas_call(kernel, out_shape=shapes, in_specs=[SMEM] + [place] * len(...  20.5 us
    ppermute x1, waiting for transfers between devices, on_device(): above = lax.ppermute(tied, 'section', down)  4.77 us
  transfers between devices with their start and end apart: 24, of which 4 were waited for; matrix products, arithmetic and copies ran while one was open for 1% of the time, Pallas kernels for 8%

profile of v5, /device:TPU:1, one launch (start us, length us, event | category | flops | bytes accessed | tf_op | source)
XLA Modules:
  0.0 125.8 jit_solution(816617291754474117)
XLA Ops:
  0.0 0.7 copy-done.8
  0.8 1.1 convert_bitcast_fusion.1
  1.9 0.1 fusion.2
  2.0 0.7 copy-done.5
  2.8 0.9 slice_bitcast_fusion
  3.7 0.8 collective-permute-start
  4.5 0.7 collective-permute-start.1
  5.2 0.7 collective-permute-start.2
  6.7 1.0 pad_maximum_fusion.1.own.refs_0_
  7.7 0.6 prepare.3
  8.3 0.5 copy-done.3
  8.8 0.5 first_step.1.refs_0_
  9.4 12.4 %collective-permute-start.3 = (bf16[2,64,768]{2,1,0:T(8,128)(2,1)S(1)}, bf16[2,64,768]{2,1,0:T(8,128)(2,1)S(1)}, u32[]{:S(2)}, u32[]{:S(2)}) collective-permute-start(bf16[2,64,768]{2,1,0:T(8,128)(2,1)S(1)} %get-tuple-element.70), channel_id=1, source_target_pairs={{0,6},{1,7},{2,8},{3,9},{4,10},{6,0},{7,1},{8,2},{9,3},{10,4},{12,... | collective-permute-start | bytes 589832 | tf_op jit(solution)/shard_map/later_states/ppermute | solution.py:325
  21.8 0.7 collective-permute-start.5
  22.5 0.7 collective-permute-start.6
  23.2 1.3 %collective-permute-start.7 = (bf16[2,64,768]{2,1,0:T(8,128)(2,1)S(1)}, bf16[2,64,768]{2,1,0:T(8,128)(2,1)S(1)}, u32[]{:S(2)}, u32[]{:S(2)}) collective-permute-start(bf16[2,64,768]{2,1,0:T(8,128)(2,1)S(1)} %get-tuple-element.69), channel_id=1, source_target_pairs={{6,12},{7,13},{9,15},{18,24},{19,25},{21,27},{30,36},{31,37},{33,3... | collective-permute-start | bytes 589832 | tf_op jit(solution)/shard_map/later_states/ppermute | solution.py:325
  24.5 1.9 %collective-permute-start.8 = (bf16[2,64,768]{2,1,0:T(8,128)(2,1)S(1)}, bf16[2,64,768]{2,1,0:T(8,128)(2,1)S(1)}, u32[]{:S(2)}, u32[]{:S(2)}) collective-permute-start(bf16[2,64,768]{2,1,0:T(8,128)(2,1)S(1)} %get-tuple-element.68), channel_id=1, source_target_pairs={{6,18},{7,19},{9,21},{18,30},{19,31},{21,33},{30,42},{31,43},{33,4... | collective-permute-start | bytes 589832 | tf_op jit(solution)/shard_map/later_states/ppermute | solution.py:325
  26.5 1.3 %collective-permute-start.10 = (bf16[1,64,768]{2,1,0:T(8,128)(2,1)S(1)}, bf16[1,64,768]{2,1,0:T(8,128)(2,1)S(1)}, u32[]{:S(2)}, u32[]{:S(2)}) collective-permute-start(bf16[1,64,768]{2,1,0:T(8,128)(2,1)S(1)} %get-tuple-element.71), channel_id=1, source_target_pairs={{12,6},{24,18},{36,30},{48,42},{60,54},{72,66},{84,78},{96,90},{10... | collective-permute-start | bytes 294920 | tf_op jit(solution)/shard_map/window_above/ppermute | solution.py:325
  27.8 0.7 collective-permute-start.9
  28.4 13.7 %collective-permute-done.8.near1 = bf16[2,64,768]{2,1,0:T(8,128)(2,1)S(1)} collective-permute-done((bf16[2,64,768]{2,1,0:T(8,128)(2,1)S(1)}, bf16[2,64,768]{2,1,0:T(8,128)(2,1)S(1)}, u32[]{:S(2)}, u32[]{:S(2)}) %collective-permute-start.8) | collective-permute-done | bytes 196640 | tf_op jit(solution)/shard_map/later_states/ppermute | solution.py:325
  42.1 1.3 %collective-permute-start.4 = (s32[1]{0:T(128)}, s32[1]{0:T(128)}, u32[]{:S(2)}, u32[]{:S(2)}) collective-permute-start(s32[1]{0:T(128)} %param.12), channel_id=1, source_target_pairs={{1,0},{2,1},{3,2},{4,3},{5,4},{7,6},{8,7},{9,8},{10,9},{11,10},{13... | collective-permute-start | bytes 20 | tf_op jit(solution)/shard_map/shifts/ppermute | solution.py:380
  43.4 2.3 %prepare.4 = (bf16[128,1536]{1,0:T(8,128)(2,1)S(1)}, bf16[128,1536]{1,0:T(8,128)(2,1)S(1)}, bf16[3,256,512]{2,1,0:T(8,128)(2,1)S(1)}, bf16[3,512,128]{2,1,0:T(8,...) custom-call(s32[5]{0:T(128)S(1)} %stack.19.scalars, ...), custom_call_target="tpu_custom_call" | custom-call | tf_op jit(solution)/shard_map/prepare/pallas_call | solution.py:273
  45.7 4.8 %collective-permute-done.4.above = s32[1]{0:T(128)} collective-permute-done((s32[1]{0:T(128)}, s32[1]{0:T(128)}, u32[]{:S(2)}, u32[]{:S(2)}) %collective-permute-start.4) | collective-permute-done | bytes 36 | tf_op jit(solution)/shard_map/shifts/ppermute | solution.py:380
  50.5 1.8 %shift.1.scalars = s32[6]{0:T(128)S(1)} custom-call(s32[5]{0:T(128)S(1)} %stack.19.scalars, s32[1]{0:T(128)} %collective-permute-done.4.above), custom_call_target="tpu_custom_call" | custom-call | tf_op jit(solution)/shard_map/shifts/shift/pallas_call | solution.py:381
  52.3 2.2 %prepare.5 = (bf16[128,1536]{1,0:T(8,128)(2,1)S(1)}, bf16[128,1536]{1,0:T(8,128)(2,1)S(1)}, bf16[3,256,512]{2,1,0:T(8,128)(2,1)S(1)}, bf16[3,512,128]{2,1,0:T(8,...) custom-call(s32[5]{0:T(128)S(1)} %stack.19.scalars, ...), custom_call_target="tpu_custom_call" | custom-call | tf_op jit(solution)/shard_map/window_above/prepare/pallas_call | solution.py:273
  54.6 2.4 %step.4.refs_1_ = bf16[128,768]{1,0:T(8,128)(2,1)S(1)} custom-call(s32[6]{0:T(128)S(1)} %shift.1.scalars, bf16[128,768]{1,0:T(8,128)(2,1)S(1)} %collective-permute-done.5.low, bf16[128,768]{1,0:T(8,128)(2,1)S(1)} %collective-permute-done.6.high, bf16[128,1536]{1,0:T(8,128)(2,1)S(1)} %get-tuple-element.43.refs_0_, ...), custom_call_target="tpu_custom_call" | custom-call | tf_op jit(solution)/shard_map/step/pallas_call | solution.py:273
  56.9 0.7 collective-permute-start.11
  57.6 0.7 collective-permute-start.12
  58.3 2.4 %step.5.refs_2_ = bf16[128,768]{1,0:T(8,128)(2,1)S(1)} custom-call(s32[6]{0:T(128)S(1)} %shift.1.scalars, bf16[128,768]{1,0:T(8,128)(2,1)S(1)} %collective-permute-done.11.low, bf16[128,768]{1,0:T(8,128)(2,1)S(1)} %collective-permute-done.12.high, bf16[128,1536]{1,0:T(8,128)(2,1)S(1)} %get-tuple-element.43.refs_0_, ...), custom_call_target="tpu_custom_call" | custom-call | tf_op jit(solution)/shard_map/step/pallas_call | solution.py:273
  60.7 0.7 collective-permute-start.13
  61.4 0.7 collective-permute-start.14
  62.1 2.4 %step.6.refs_3_ = bf16[128,768]{1,0:T(8,128)(2,1)S(1)} custom-call(s32[6]{0:T(128)S(1)} %shift.1.scalars, bf16[128,768]{1,0:T(8,128)(2,1)S(1)} %collective-permute-done.13.low, bf16[128,768]{1,0:T(8,128)(2,1)S(1)} %collective-permute-done.14.high, bf16[128,1536]{1,0:T(8,128)(2,1)S(1)} %get-tuple-element.43.refs_0_, ...), custom_call_target="tpu_custom_call" | custom-call | tf_op jit(solution)/shard_map/step/pallas_call | solution.py:273
  64.5 0.7 collective-permute-start.15
  65.1 0.9 collective-permute-start.16
  66.0 2.4 %step.7 = (bf16[128,768]{1,0:T(8,128)(2,1)S(1)}, bf16[64,768]{1,0:T(8,128)(2,1)S(1)}) custom-call(s32[6]{0:T(128)S(1)} %shift.1.scalars, bf16[128,768]{1,0:T(8,128)(2,1)S(1)} %collective-permute-done.15.low, bf16[128,768]{1,0:T(8,128)(2,1)S(1)} %collective-permute-done.16.high, bf16[128,1536]{1,0:T(8,128)(2,1)S(1)} %get-tuple-element.43.refs_0_, ...), custom_call_target="tpu_custom_call" | custom-call | tf_op jit(solution)/shard_map/step/pallas_call | solution.py:273
  68.4 1.3 %collective-permute-start.21 = (bf16[128,768]{1,0:T(8,128)(2,1)S(1)}, bf16[128,768]{1,0:T(8,128)(2,1)S(1)}, u32[]{:S(2)}, u32[]{:S(2)}) collective-permute-start(bf16[128,768]{1,0:T(8,128)(2,1)S(1)} %get-tuple-element.53.refs_4_), channel_id=1, source_target_pairs={{1,0},{7,6},{13,12},{19,18},{25,24},{31,30},{37,36},{43,42},{49,48... | collective-permute-start | bytes 589832 | tf_op jit(solution)/shard_map/pass_on/ppermute | solution.py:325
  69.7 1.3 %collective-permute-start.22 = (bf16[128,768]{1,0:T(8,128)(2,1)S(1)}, bf16[128,768]{1,0:T(8,128)(2,1)S(1)}, u32[]{:S(2)}, u32[]{:S(2)}) collective-permute-start(bf16[128,768]{1,0:T(8,128)(2,1)S(1)} %get-tuple-element.53.refs_4_), channel_id=1, source_target_pairs={{13,0},{19,6},{25,12},{31,18},{37,24},{43,30},{49,36},{55,42},{61,... | collective-permute-start | bytes 589832 | tf_op jit(solution)/shard_map/pass_on/ppermute | solution.py:325
  71.0 1.3 %collective-permute-start.20 = (bf16[64,768]{1,0:T(8,128)(2,1)S(1)}, bf16[64,768]{1,0:T(8,128)(2,1)S(1)}, u32[]{:S(2)}, u32[]{:S(2)}) collective-permute-start(bf16[64,768]{1,0:T(8,128)(2,1)S(1)} %get-tuple-element.57), channel_id=1, source_target_pairs={{757,0},{763,6},{1,12},{7,18},{13,24},{19,30},{25,36},{31,42},{37,... | collective-permute-start | bytes 294920 | tf_op jit(solution)/shard_map/pass_on/ppermute | solution.py:325
  72.3 0.7 split.1
  73.0 0.7 collective-permute-start.18
  73.7 0.7 collective-permute-start.19
  74.4 38.4 %collective-permute-done.20.low = bf16[64,768]{1,0:T(8,128)(2,1)S(1)} collective-permute-done((bf16[64,768]{1,0:T(8,128)(2,1)S(1)}, bf16[64,768]{1,0:T(8,128)(2,1)S(1)}, u32[]{:S(2)}, u32[]{:S(2)}) %collective-permute-start.20) | collective-permute-done | bytes 98336 | tf_op jit(solution)/shard_map/pass_on/ppermute | solution.py:325
  112.8 0.7 collective-permute-start.17
  113.5 3.3 %last_step.1 = (bf16[64,768]{1,0:T(8,128)(2,1)S(1)}, bf16[64,768]{1,0:T(8,128)(2,1)S(1)}) custom-call(s32[6]{0:T(128)S(1)} %shift.1.scalars, bf16[64,768]{1,0:T(8,128)(2,1)S(1)} %collective-permute-done.20.low, bf16[128,768]{1,0:T(8,128)(2,1)S(1)} %collective-permute-done.21.middle, bf16[128,768]{1,0:T(8,128)(2,1)S(1)} %collective-permute-done.22.high, ...), custom_call_target="tpu_custom_call" | custom-call | tf_op jit(solution)/shard_map/last_step/pallas_call | solution.py:273
  116.8 6.8 %collective-permute-start.23 = (bf16[64,768]{1,0:T(8,128)(2,1)S(1)}, bf16[64,768]{1,0:T(8,128)(2,1)S(1)}, u32[]{:S(2)}, u32[]{:S(2)}) collective-permute-start(bf16[64,768]{1,0:T(8,128)(2,1)S(1)} %get-tuple-element.64), channel_id=1, source_target_pairs={{0,6},{6,0},{12,18},{18,12},{24,30},{30,24},{36,42},{42,36},{48,54... | collective-permute-start | bytes 294920 | tf_op jit(solution)/shard_map/last_result/ppermute | solution.py:325
  123.6 0.1 fusion.5.forcing
  123.7 0.8 collective-permute-done.23.other_last
  124.5 1.4 %merge.1 = f32[2,64,768]{2,1,0:T(8,128)} custom-call(s32[5]{0:T(128)S(1)} %stack.19.scalars, bf16[64,768]{1,0:T(8,128)(2,1)S(1)} %get-tuple-element.54.own, bf16[64,768]{1,0:T(8,128)(2,1)S(1)} %collective-permute-done.17.other, bf16[64,768]{1,0:T(8,128)(2,1)S(1)} %collective-permute-done.18.near0, bf16[64,768]{1,0:T(8,128)(2,1)S(1)} %collective-permute-done.19.near1, ...), custom_call_target="tpu_custom_call" | custom-call | tf_op jit(solution)/shard_map/merge/pallas_call | solution.py:273
  (41 shorter events, 0.4 us)
Async XLA Ops:
  0.0 0.7 copy-start.8
  0.8 1.1 copy-start.4
  0.8 1.1 copy-start.6
  2.0 0.7 copy-start.5
  2.8 4.9 %copy-start.1 = (bf16[1,768,384]{2,1,0:T(8,128)(2,1)S(1)}, bf16[1,768,384]{2,1,0:T(8,128)(2,1)}, u32[]{:S(2)}) copy-start(bf16[1,768,384]{2,1,0:T(8,128)(2,1)} %param.15) | copy-start | bytes 1769476
  2.8 4.9 %copy-start.2 = (bf16[1,768,384]{2,1,0:T(8,128)(2,1)S(1)}, bf16[1,768,384]{2,1,0:T(8,128)(2,1)}, u32[]{:S(2)}) copy-start(bf16[1,768,384]{2,1,0:T(8,128)(2,1)} %param.16) | copy-start | bytes 1769476
  3.7 4.0 %copy-start = (bf16[1,768,384]{2,1,0:T(8,128)(2,1)S(1)}, bf16[1,768,384]{2,1,0:T(8,128)(2,1)}, u32[]{:S(2)}) copy-start(bf16[1,768,384]{2,1,0:T(8,128)(2,1)} %param.14) | copy-start | bytes 1769476
  3.7 3.9 %collective-permute-start = (bf16[3,64,768]{2,1,0:T(8,128)(2,1)}, bf16[3,64,768]{2,1,0:T(8,128)(2,1)S(1)}, u32[]{:S(2)}, u32[]{:S(2)}) collective-permute-start(bf16[3,64,768]{2,1,0:T(8,128)(2,1)} %get-tuple-element.67), channel_id=1, source_target_pairs={{5,11},{11,5},{17,23},{23,17},{29,35},{35,29},{41,47},{47,41},{53,... | collective-permute-start | bytes 884744 | tf_op jit(solution)/shard_map/first_states/ppermute | solution.py:325
  4.5 3.1 %collective-permute-start.1 = (bf16[3,64,768]{2,1,0:T(8,128)(2,1)}, bf16[3,64,768]{2,1,0:T(8,128)(2,1)S(1)}, u32[]{:S(2)}, u32[]{:S(2)}) collective-permute-start(bf16[3,64,768]{2,1,0:T(8,128)(2,1)} %get-tuple-element.66), channel_id=1, source_target_pairs={{11,17},{23,29},{35,41},{47,53},{59,65},{71,77},{83,89},{95,101},{... | collective-permute-start | bytes 884744 | tf_op jit(solution)/shard_map/first_states/ppermute | solution.py:325
  5.2 2.5 %collective-permute-start.2 = (bf16[3,64,768]{2,1,0:T(8,128)(2,1)}, bf16[3,64,768]{2,1,0:T(8,128)(2,1)S(1)}, u32[]{:S(2)}, u32[]{:S(2)}) collective-permute-start(bf16[3,64,768]{2,1,0:T(8,128)(2,1)} %get-tuple-element.65), channel_id=1, source_target_pairs={{11,23},{23,35},{35,47},{47,59},{59,71},{71,83},{83,95},{95,107},{... | collective-permute-start | bytes 884744 | tf_op jit(solution)/shard_map/first_states/ppermute | solution.py:325
  7.7 1.1 copy-start.3
  9.4 17.0 %collective-permute-start.3 = (bf16[2,64,768]{2,1,0:T(8,128)(2,1)S(1)}, bf16[2,64,768]{2,1,0:T(8,128)(2,1)S(1)}, u32[]{:S(2)}, u32[]{:S(2)}) collective-permute-start(bf16[2,64,768]{2,1,0:T(8,128)(2,1)S(1)} %get-tuple-element.70), channel_id=1, source_target_pairs={{0,6},{1,7},{2,8},{3,9},{4,10},{6,0},{7,1},{8,2},{9,3},{10,4},{12,... | collective-permute-start | bytes 589832 | tf_op jit(solution)/shard_map/later_states/ppermute | solution.py:325
  21.8 32.7 %collective-permute-start.5 = (bf16[128,768]{1,0:T(8,128)(2,1)S(1)}, bf16[128,768]{1,0:T(8,128)(2,1)S(1)}, u32[]{:S(2)}, u32[]{:S(2)}) collective-permute-start(bf16[128,768]{1,0:T(8,128)(2,1)S(1)} %first_step.1.refs_0_), channel_id=1, source_target_pairs={{5,4},{11,10},{17,16},{23,22},{29,28},{35,34},{41,40},{47,46},{53,... | collective-permute-start | bytes 589832 | tf_op jit(solution)/shard_map/pass_on/ppermute | solution.py:325
  22.5 32.0 %collective-permute-start.6 = (bf16[128,768]{1,0:T(8,128)(2,1)S(1)}, bf16[128,768]{1,0:T(8,128)(2,1)S(1)}, u32[]{:S(2)}, u32[]{:S(2)}) collective-permute-start(bf16[128,768]{1,0:T(8,128)(2,1)S(1)} %first_step.1.refs_0_), channel_id=1, source_target_pairs={{17,4},{23,10},{29,16},{35,22},{41,28},{47,34},{53,40},{59,46},{65... | collective-permute-start | bytes 589832 | tf_op jit(solution)/shard_map/pass_on/ppermute | solution.py:325
  23.2 4.6 %collective-permute-start.7 = (bf16[2,64,768]{2,1,0:T(8,128)(2,1)S(1)}, bf16[2,64,768]{2,1,0:T(8,128)(2,1)S(1)}, u32[]{:S(2)}, u32[]{:S(2)}) collective-permute-start(bf16[2,64,768]{2,1,0:T(8,128)(2,1)S(1)} %get-tuple-element.69), channel_id=1, source_target_pairs={{6,12},{7,13},{9,15},{18,24},{19,25},{21,27},{30,36},{31,37},{33,3... | collective-permute-start | bytes 589832 | tf_op jit(solution)/shard_map/later_states/ppermute | solution.py:325
  24.5 17.6 %collective-permute-start.8 = (bf16[2,64,768]{2,1,0:T(8,128)(2,1)S(1)}, bf16[2,64,768]{2,1,0:T(8,128)(2,1)S(1)}, u32[]{:S(2)}, u32[]{:S(2)}) collective-permute-start(bf16[2,64,768]{2,1,0:T(8,128)(2,1)S(1)} %get-tuple-element.68), channel_id=1, source_target_pairs={{6,18},{7,19},{9,21},{18,30},{19,31},{21,33},{30,42},{31,43},{33,4... | collective-permute-start | bytes 589832 | tf_op jit(solution)/shard_map/later_states/ppermute | solution.py:325
  26.5 25.8 %collective-permute-start.10 = (bf16[1,64,768]{2,1,0:T(8,128)(2,1)S(1)}, bf16[1,64,768]{2,1,0:T(8,128)(2,1)S(1)}, u32[]{:S(2)}, u32[]{:S(2)}) collective-permute-start(bf16[1,64,768]{2,1,0:T(8,128)(2,1)S(1)} %get-tuple-element.71), channel_id=1, source_target_pairs={{12,6},{24,18},{36,30},{48,42},{60,54},{72,66},{84,78},{96,90},{10... | collective-permute-start | bytes 294920 | tf_op jit(solution)/shard_map/window_above/ppermute | solution.py:325
  27.8 24.5 %collective-permute-start.9 = (bf16[1,64,768]{2,1,0:T(8,128)(2,1)S(1)}, bf16[1,64,768]{2,1,0:T(8,128)(2,1)S(1)}, u32[]{:S(2)}, u32[]{:S(2)}) collective-permute-start(bf16[1,64,768]{2,1,0:T(8,128)(2,1)S(1)} %get-tuple-element.72), channel_id=1, source_target_pairs={{12,0},{24,12},{36,24},{48,36},{60,48},{72,60},{84,72},{96,84},{10... | collective-permute-start | bytes 294920 | tf_op jit(solution)/shard_map/window_above/ppermute | solution.py:325
  42.1 8.4 %collective-permute-start.4 = (s32[1]{0:T(128)}, s32[1]{0:T(128)}, u32[]{:S(2)}, u32[]{:S(2)}) collective-permute-start(s32[1]{0:T(128)} %param.12), channel_id=1, source_target_pairs={{1,0},{2,1},{3,2},{4,3},{5,4},{7,6},{8,7},{9,8},{10,9},{11,10},{13... | collective-permute-start | bytes 20 | tf_op jit(solution)/shard_map/shifts/ppermute | solution.py:380
  56.9 1.4 %collective-permute-start.11 = (bf16[128,768]{1,0:T(8,128)(2,1)S(1)}, bf16[128,768]{1,0:T(8,128)(2,1)S(1)}, u32[]{:S(2)}, u32[]{:S(2)}) collective-permute-start(bf16[128,768]{1,0:T(8,128)(2,1)S(1)} %step.4.refs_1_), channel_id=1, source_target_pairs={{760,3},{766,9},{4,15},{10,21},{16,27},{22,33},{28,39},{34,45},{40... | collective-permute-start | bytes 589832 | tf_op jit(solution)/shard_map/pass_on/ppermute | solution.py:325
  57.6 0.7 collective-permute-start.12
  60.7 1.4 %collective-permute-start.13 = (bf16[128,768]{1,0:T(8,128)(2,1)S(1)}, bf16[128,768]{1,0:T(8,128)(2,1)S(1)}, u32[]{:S(2)}, u32[]{:S(2)}) collective-permute-start(bf16[128,768]{1,0:T(8,128)(2,1)S(1)} %step.5.refs_2_), channel_id=1, source_target_pairs={{3,2},{9,8},{15,14},{21,20},{27,26},{33,32},{39,38},{45,44},{51,50... | collective-permute-start | bytes 589832 | tf_op jit(solution)/shard_map/pass_on/ppermute | solution.py:325
  61.4 0.7 collective-permute-start.14
  64.5 1.5 %collective-permute-start.15 = (bf16[128,768]{1,0:T(8,128)(2,1)S(1)}, bf16[128,768]{1,0:T(8,128)(2,1)S(1)}, u32[]{:S(2)}, u32[]{:S(2)}) collective-permute-start(bf16[128,768]{1,0:T(8,128)(2,1)S(1)} %step.6.refs_3_), channel_id=1, source_target_pairs={{758,1},{764,7},{2,13},{8,19},{14,25},{20,31},{26,37},{32,43},{38,... | collective-permute-start | bytes 589832 | tf_op jit(solution)/shard_map/pass_on/ppermute | solution.py:325
  65.1 0.9 collective-permute-start.16
  68.4 45.0 %collective-permute-start.21 = (bf16[128,768]{1,0:T(8,128)(2,1)S(1)}, bf16[128,768]{1,0:T(8,128)(2,1)S(1)}, u32[]{:S(2)}, u32[]{:S(2)}) collective-permute-start(bf16[128,768]{1,0:T(8,128)(2,1)S(1)} %get-tuple-element.53.refs_4_), channel_id=1, source_target_pairs={{1,0},{7,6},{13,12},{19,18},{25,24},{31,30},{37,36},{43,42},{49,48... | collective-permute-start | bytes 589832 | tf_op jit(solution)/shard_map/pass_on/ppermute | solution.py:325
  69.7 43.7 %collective-permute-start.22 = (bf16[128,768]{1,0:T(8,128)(2,1)S(1)}, bf16[128,768]{1,0:T(8,128)(2,1)S(1)}, u32[]{:S(2)}, u32[]{:S(2)}) collective-permute-start(bf16[128,768]{1,0:T(8,128)(2,1)S(1)} %get-tuple-element.53.refs_4_), channel_id=1, source_target_pairs={{13,0},{19,6},{25,12},{31,18},{37,24},{43,30},{49,36},{55,42},{61,... | collective-permute-start | bytes 589832 | tf_op jit(solution)/shard_map/pass_on/ppermute | solution.py:325
  71.0 41.7 %collective-permute-start.20 = (bf16[64,768]{1,0:T(8,128)(2,1)S(1)}, bf16[64,768]{1,0:T(8,128)(2,1)S(1)}, u32[]{:S(2)}, u32[]{:S(2)}) collective-permute-start(bf16[64,768]{1,0:T(8,128)(2,1)S(1)} %get-tuple-element.57), channel_id=1, source_target_pairs={{757,0},{763,6},{1,12},{7,18},{13,24},{19,30},{25,36},{31,42},{37,... | collective-permute-start | bytes 294920 | tf_op jit(solution)/shard_map/pass_on/ppermute | solution.py:325
  73.0 50.7 %collective-permute-start.18 = (bf16[64,768]{1,0:T(8,128)(2,1)S(1)}, bf16[64,768]{1,0:T(8,128)(2,1)S(1)}, u32[]{:S(2)}, u32[]{:S(2)}) collective-permute-start(bf16[64,768]{1,0:T(8,128)(2,1)S(1)} %get-tuple-element.56), channel_id=1, source_target_pairs={{13,7},{15,9},{17,11},{25,19},{27,21},{29,23},{37,31},{39,33},{41,... | collective-permute-start | bytes 294920 | tf_op jit(solution)/shard_map/earlier_results/ppermute | solution.py:325
  73.7 50.0 %collective-permute-start.19 = (bf16[64,768]{1,0:T(8,128)(2,1)S(1)}, bf16[64,768]{1,0:T(8,128)(2,1)S(1)}, u32[]{:S(2)}, u32[]{:S(2)}) collective-permute-start(bf16[64,768]{1,0:T(8,128)(2,1)S(1)} %get-tuple-element.56), channel_id=1, source_target_pairs={{19,7},{21,9},{23,11},{31,19},{33,21},{35,23},{43,31},{45,33},{47,... | collective-permute-start | bytes 294920 | tf_op jit(solution)/shard_map/earlier_results/ppermute | solution.py:325
  112.8 10.9 %collective-permute-start.17 = (bf16[64,768]{1,0:T(8,128)(2,1)S(1)}, bf16[64,768]{1,0:T(8,128)(2,1)S(1)}, u32[]{:S(2)}, u32[]{:S(2)}) collective-permute-start(bf16[64,768]{1,0:T(8,128)(2,1)S(1)} %get-tuple-element.55), channel_id=1, source_target_pairs={{1,7},{2,8},{3,9},{4,10},{5,11},{7,1},{8,2},{9,3},{10,4},{11,5},{1... | collective-permute-start | bytes 294920 | tf_op jit(solution)/shard_map/earlier_results/ppermute | solution.py:325
  113.4 10.1 %copy-start.7 = (bf16[1,2,8,8,768]{4,3,2,1,0:T(8,128)(2,1)S(1)}, bf16[1,2,8,8,768]{4,3,2,1,0:T(8,128)(2,1)}, u32[]{:S(2)}) copy-start(bf16[1,2,8,8,768]{4,3,2,1,0:T(8,128)(2,1)} %param.10) | copy-start | bytes 589828
  116.8 7.7 %collective-permute-start.23 = (bf16[64,768]{1,0:T(8,128)(2,1)S(1)}, bf16[64,768]{1,0:T(8,128)(2,1)S(1)}, u32[]{:S(2)}, u32[]{:S(2)}) collective-permute-start(bf16[64,768]{1,0:T(8,128)(2,1)S(1)} %get-tuple-element.64), channel_id=1, source_target_pairs={{0,6},{6,0},{12,18},{18,12},{24,30},{30,24},{36,42},{42,36},{48,54... | collective-permute-start | bytes 294920 | tf_op jit(solution)/shard_map/last_result/ppermute | solution.py:325

commit v6 on v5

--- a/solution.py
+++ b/solution.py
@@ -55,9 +55,9 @@
     last_slot,
     scalars,
     own,
-    other,
     near0,
     near1,
+    other,
     w_query,
     w_key,
     w_value,
@@ -164,7 +164,7 @@
     moving[5] = scalars[2] - above[0]
 
 
-def first_kernel(scalars, own, other, near0, near1, *refs):
+def first_kernel(scalars, own, near0, near1, other, *refs):
     prepared, weights = refs[:6], refs[6:10]
     all_ref, rows = refs[10:]
     forcing = gathered(rows, scalars, own, other, near0, near1, 1)
@@ -350,12 +350,12 @@
         )
     lift = jnp.where(section_at == 0, 0, (last - section_at) % 2)
     place = ints(core, chip, offset, section_at, lift)
-    prepared = prepare(place, (begin, first_other, *near), weights, chips - 1, only=last)
+    prepared = prepare(place, (begin, *near, first_other), weights, chips - 1, only=last)
     result = call(
         "first_step",
         first_kernel,
         place,
-        (begin, first_other, *near, *prepared, *weights),
+        (begin, *near, first_other, *prepared, *weights),
         [struct((SLOT, width))],
         [pltpu.VMEM((3 * BAND, width), FLT)],
         only=last,
@@ -387,12 +387,12 @@
             name="shift",
         )(place, above)
     *prepared, forcing_here = prepare(
-        place, (pair, later_other, *later_near), weights, chips - 1, with_forcing=True
+        place, (pair, *later_near, later_other), weights, chips - 1, with_forcing=True
     )
     with jax.named_scope("window_above"):
         x_later, _ = lax.optimization_barrier((x, later_other))
         next0, next1 = [sent(x_later[m], moved(even_down[m], [0])) for m in range(2)]
-        extra = prepare(place, (pair, later_other, next0, next1), weights, chips - 1, above=True, only=0)
+        extra = prepare(place, (pair, next0, next1, later_other), weights, chips - 1, above=True, only=0)
     forcing_here, _ = lax.optimization_barrier((forcing_here, extra[0]))
     for tick in range(1, sections):
         source = sections - tick

time: 126 us -> 125 us (level)
  starting transfers between devices: 39.3 us -> 35.8 us
  waiting for transfers between devices: 57.7 us -> 60.2 us
    ppermute x23, waiting for transfers between devices: 52.9 us -> 57.3 us  [sent(): return lax.ppermute(value, AXES, hops)]
    ppermute x23, starting transfers between devices: 38 us -> 34.5 us  [sent(): return lax.ppermute(value, AXES, hops)]
    ppermute x1, waiting for transfers between devices: 4.77 us -> 2.97 us  [on_device(): above = lax.ppermute(tied, 'section', down)]
where the time goes in v6:
time: 125 us
  waiting for transfers between devices  60.2 us (48%)
  starting transfers between devices  35.8 us (29%)
  Pallas kernels  22.2 us (18%)
  local copies, waits for them, and re-layouts  3.1 us (2%)
  other arithmetic  2.29 us (2%)
    ppermute x23, waiting for transfers between devices, sent(): return lax.ppermute(value, AXES, hops)  57.3 us
    ppermute x23, starting transfers between devices, sent(): return lax.ppermute(value, AXES, hops)  34.5 us
    pallas_call x11, Pallas kernels, call(): pl.pallas_call(kernel, out_shape=shapes, in_specs=[SMEM] + [place] * len(...  20.5 us
    ppermute x1, waiting for transfers between devices, on_device(): above = lax.ppermute(tied, 'section', down)  2.97 us
  transfers between devices with their start and end apart: 24, of which 4 were waited for; matrix products, arithmetic and copies ran while one was open for 1% of the time, Pallas kernels for 8%

profile of v6, /device:TPU:1, one launch (start us, length us, event | category | flops | bytes accessed | tf_op | source)
XLA Modules:
  0.0 124.9 jit_solution(148473670642440104)
XLA Ops:
  0.0 0.7 copy-done.8
  0.8 1.1 convert_bitcast_fusion.1
  1.9 0.1 fusion.2
  2.0 0.7 copy-done.5
  2.8 0.9 dynamic-slice_bitcast_fusion
  3.7 0.8 collective-permute-start
  4.5 0.7 collective-permute-start.1
  5.2 0.7 collective-permute-start.2
  6.7 1.0 pad_maximum_fusion.1.own.refs_0_
  7.7 0.6 prepare.3
  8.3 0.5 copy-done.3
  8.8 0.5 first_step.1.refs_0_
  9.4 12.4 %collective-permute-start.3 = (bf16[2,64,768]{2,1,0:T(8,128)(2,1)S(1)}, bf16[2,64,768]{2,1,0:T(8,128)(2,1)S(1)}, u32[]{:S(2)}, u32[]{:S(2)}) collective-permute-start(bf16[2,64,768]{2,1,0:T(8,128)(2,1)S(1)} %get-tuple-element.70), channel_id=1, source_target_pairs={{0,6},{1,7},{2,8},{3,9},{4,10},{6,0},{7,1},{8,2},{9,3},{10,4},{12,... | collective-permute-start | bytes 589832 | tf_op jit(solution)/shard_map/later_states/ppermute | solution.py:325
  21.8 0.7 collective-permute-start.5
  22.5 0.7 collective-permute-start.6
  23.2 1.3 %collective-permute-start.7 = (bf16[2,64,768]{2,1,0:T(8,128)(2,1)S(1)}, bf16[2,64,768]{2,1,0:T(8,128)(2,1)S(1)}, u32[]{:S(2)}, u32[]{:S(2)}) collective-permute-start(bf16[2,64,768]{2,1,0:T(8,128)(2,1)S(1)} %get-tuple-element.69), channel_id=1, source_target_pairs={{6,12},{7,13},{9,15},{18,24},{19,25},{21,27},{30,36},{31,37},{33,3... | collective-permute-start | bytes 589832 | tf_op jit(solution)/shard_map/later_states/ppermute | solution.py:325
  24.5 1.9 %collective-permute-start.8 = (bf16[2,64,768]{2,1,0:T(8,128)(2,1)S(1)}, bf16[2,64,768]{2,1,0:T(8,128)(2,1)S(1)}, u32[]{:S(2)}, u32[]{:S(2)}) collective-permute-start(bf16[2,64,768]{2,1,0:T(8,128)(2,1)S(1)} %get-tuple-element.68), channel_id=1, source_target_pairs={{6,18},{7,19},{9,21},{18,30},{19,31},{21,33},{30,42},{31,43},{33,4... | collective-permute-start | bytes 589832 | tf_op jit(solution)/shard_map/later_states/ppermute | solution.py:325
  26.5 1.3 %collective-permute-start.10 = (bf16[1,64,768]{2,1,0:T(8,128)(2,1)S(1)}, bf16[1,64,768]{2,1,0:T(8,128)(2,1)S(1)}, u32[]{:S(2)}, u32[]{:S(2)}) collective-permute-start(bf16[1,64,768]{2,1,0:T(8,128)(2,1)S(1)} %get-tuple-element.71), channel_id=1, source_target_pairs={{12,6},{24,18},{36,30},{48,42},{60,54},{72,66},{84,78},{96,90},{10... | collective-permute-start | bytes 294920 | tf_op jit(solution)/shard_map/window_above/ppermute | solution.py:325
  27.8 0.7 collective-permute-start.9
  28.4 13.7 %collective-permute-done.8.near1 = bf16[2,64,768]{2,1,0:T(8,128)(2,1)S(1)} collective-permute-done((bf16[2,64,768]{2,1,0:T(8,128)(2,1)S(1)}, bf16[2,64,768]{2,1,0:T(8,128)(2,1)S(1)}, u32[]{:S(2)}, u32[]{:S(2)}) %collective-permute-start.8) | collective-permute-done | bytes 196640 | tf_op jit(solution)/shard_map/later_states/ppermute | solution.py:325
  42.1 1.3 %collective-permute-start.4 = (s32[1]{0:T(128)}, s32[1]{0:T(128)}, u32[]{:S(2)}, u32[]{:S(2)}) collective-permute-start(s32[1]{0:T(128)} %param.12), channel_id=1, source_target_pairs={{1,0},{2,1},{3,2},{4,3},{5,4},{7,6},{8,7},{9,8},{10,9},{11,10},{13... | collective-permute-start | bytes 20 | tf_op jit(solution)/shard_map/shifts/ppermute | solution.py:380
  43.4 2.3 %prepare.4 = (bf16[128,1536]{1,0:T(8,128)(2,1)S(1)}, bf16[128,1536]{1,0:T(8,128)(2,1)S(1)}, bf16[3,256,512]{2,1,0:T(8,128)(2,1)S(1)}, bf16[3,512,128]{2,1,0:T(8,...) custom-call(s32[5]{0:T(128)S(1)} %stack.19.scalars, ...), custom_call_target="tpu_custom_call" | custom-call | tf_op jit(solution)/shard_map/prepare/pallas_call | solution.py:273
  45.7 3.0 %collective-permute-done.4.above = s32[1]{0:T(128)} collective-permute-done((s32[1]{0:T(128)}, s32[1]{0:T(128)}, u32[]{:S(2)}, u32[]{:S(2)}) %collective-permute-start.4) | collective-permute-done | bytes 36 | tf_op jit(solution)/shard_map/shifts/ppermute | solution.py:380
  48.7 1.8 %shift.1.scalars = s32[6]{0:T(128)S(1)} custom-call(s32[5]{0:T(128)S(1)} %stack.19.scalars, s32[1]{0:T(128)} %collective-permute-done.4.above), custom_call_target="tpu_custom_call" | custom-call | tf_op jit(solution)/shard_map/shifts/shift/pallas_call | solution.py:381
  50.5 2.2 %prepare.5 = (bf16[128,1536]{1,0:T(8,128)(2,1)S(1)}, bf16[128,1536]{1,0:T(8,128)(2,1)S(1)}, bf16[3,256,512]{2,1,0:T(8,128)(2,1)S(1)}, bf16[3,512,128]{2,1,0:T(8,...) custom-call(s32[5]{0:T(128)S(1)} %stack.19.scalars, ...), custom_call_target="tpu_custom_call" | custom-call | tf_op jit(solution)/shard_map/window_above/prepare/pallas_call | solution.py:273
  52.7 2.4 %step.4.refs_1_ = bf16[128,768]{1,0:T(8,128)(2,1)S(1)} custom-call(s32[6]{0:T(128)S(1)} %shift.1.scalars, bf16[128,768]{1,0:T(8,128)(2,1)S(1)} %collective-permute-done.5.low, bf16[128,768]{1,0:T(8,128)(2,1)S(1)} %collective-permute-done.6.high, bf16[128,1536]{1,0:T(8,128)(2,1)S(1)} %get-tuple-element.43.refs_0_, ...), custom_call_target="tpu_custom_call" | custom-call | tf_op jit(solution)/shard_map/step/pallas_call | solution.py:273
  55.1 0.7 collective-permute-start.11
  55.8 0.7 collective-permute-start.12
  56.5 2.4 %step.5.refs_2_ = bf16[128,768]{1,0:T(8,128)(2,1)S(1)} custom-call(s32[6]{0:T(128)S(1)} %shift.1.scalars, bf16[128,768]{1,0:T(8,128)(2,1)S(1)} %collective-permute-done.11.low, bf16[128,768]{1,0:T(8,128)(2,1)S(1)} %collective-permute-done.12.high, bf16[128,1536]{1,0:T(8,128)(2,1)S(1)} %get-tuple-element.43.refs_0_, ...), custom_call_target="tpu_custom_call" | custom-call | tf_op jit(solution)/shard_map/step/pallas_call | solution.py:273
  58.9 0.7 collective-permute-start.13
  59.5 0.7 collective-permute-start.14
  60.2 2.4 %step.6.refs_3_ = bf16[128,768]{1,0:T(8,128)(2,1)S(1)} custom-call(s32[6]{0:T(128)S(1)} %shift.1.scalars, bf16[128,768]{1,0:T(8,128)(2,1)S(1)} %collective-permute-done.13.low, bf16[128,768]{1,0:T(8,128)(2,1)S(1)} %collective-permute-done.14.high, bf16[128,1536]{1,0:T(8,128)(2,1)S(1)} %get-tuple-element.43.refs_0_, ...), custom_call_target="tpu_custom_call" | custom-call | tf_op jit(solution)/shard_map/step/pallas_call | solution.py:273
  62.6 0.7 collective-permute-start.15
  63.3 0.9 collective-permute-start.16
  64.2 2.4 %step.7 = (bf16[128,768]{1,0:T(8,128)(2,1)S(1)}, bf16[64,768]{1,0:T(8,128)(2,1)S(1)}) custom-call(s32[6]{0:T(128)S(1)} %shift.1.scalars, bf16[128,768]{1,0:T(8,128)(2,1)S(1)} %collective-permute-done.15.low, bf16[128,768]{1,0:T(8,128)(2,1)S(1)} %collective-permute-done.16.high, bf16[128,1536]{1,0:T(8,128)(2,1)S(1)} %get-tuple-element.43.refs_0_, ...), custom_call_target="tpu_custom_call" | custom-call | tf_op jit(solution)/shard_map/step/pallas_call | solution.py:273
  66.6 1.3 %collective-permute-start.21 = (bf16[128,768]{1,0:T(8,128)(2,1)S(1)}, bf16[128,768]{1,0:T(8,128)(2,1)S(1)}, u32[]{:S(2)}, u32[]{:S(2)}) collective-permute-start(bf16[128,768]{1,0:T(8,128)(2,1)S(1)} %get-tuple-element.53.refs_4_), channel_id=1, source_target_pairs={{1,0},{7,6},{13,12},{19,18},{25,24},{31,30},{37,36},{43,42},{49,48... | collective-permute-start | bytes 589832 | tf_op jit(solution)/shard_map/pass_on/ppermute | solution.py:325
  67.9 1.3 %collective-permute-start.22 = (bf16[128,768]{1,0:T(8,128)(2,1)S(1)}, bf16[128,768]{1,0:T(8,128)(2,1)S(1)}, u32[]{:S(2)}, u32[]{:S(2)}) collective-permute-start(bf16[128,768]{1,0:T(8,128)(2,1)S(1)} %get-tuple-element.53.refs_4_), channel_id=1, source_target_pairs={{13,0},{19,6},{25,12},{31,18},{37,24},{43,30},{49,36},{55,42},{61,... | collective-permute-start | bytes 589832 | tf_op jit(solution)/shard_map/pass_on/ppermute | solution.py:325
  69.2 1.3 %collective-permute-start.20 = (bf16[64,768]{1,0:T(8,128)(2,1)S(1)}, bf16[64,768]{1,0:T(8,128)(2,1)S(1)}, u32[]{:S(2)}, u32[]{:S(2)}) collective-permute-start(bf16[64,768]{1,0:T(8,128)(2,1)S(1)} %get-tuple-element.57), channel_id=1, source_target_pairs={{757,0},{763,6},{1,12},{7,18},{13,24},{19,30},{25,36},{31,42},{37,... | collective-permute-start | bytes 294920 | tf_op jit(solution)/shard_map/pass_on/ppermute | solution.py:325
  70.5 0.7 split.1
  71.2 0.7 collective-permute-start.18
  71.8 0.7 collective-permute-start.19
  72.5 42.7 %collective-permute-done.20.low = bf16[64,768]{1,0:T(8,128)(2,1)S(1)} collective-permute-done((bf16[64,768]{1,0:T(8,128)(2,1)S(1)}, bf16[64,768]{1,0:T(8,128)(2,1)S(1)}, u32[]{:S(2)}, u32[]{:S(2)}) %collective-permute-start.20) | collective-permute-done | bytes 98336 | tf_op jit(solution)/shard_map/pass_on/ppermute | solution.py:325
  115.3 0.7 collective-permute-start.17
  115.9 3.3 %last_step.1 = (bf16[64,768]{1,0:T(8,128)(2,1)S(1)}, bf16[64,768]{1,0:T(8,128)(2,1)S(1)}) custom-call(s32[6]{0:T(128)S(1)} %shift.1.scalars, bf16[64,768]{1,0:T(8,128)(2,1)S(1)} %collective-permute-done.20.low, bf16[128,768]{1,0:T(8,128)(2,1)S(1)} %collective-permute-done.21.middle, bf16[128,768]{1,0:T(8,128)(2,1)S(1)} %collective-permute-done.22.high, ...), custom_call_target="tpu_custom_call" | custom-call | tf_op jit(solution)/shard_map/last_step/pallas_call | solution.py:273
  119.3 3.3 %collective-permute-start.23 = (bf16[64,768]{1,0:T(8,128)(2,1)S(1)}, bf16[64,768]{1,0:T(8,128)(2,1)S(1)}, u32[]{:S(2)}, u32[]{:S(2)}) collective-permute-start(bf16[64,768]{1,0:T(8,128)(2,1)S(1)} %get-tuple-element.64), channel_id=1, source_target_pairs={{0,6},{6,0},{12,18},{18,12},{24,30},{30,24},{36,42},{42,36},{48,54... | collective-permute-start | bytes 294920 | tf_op jit(solution)/shard_map/last_result/ppermute | solution.py:325
  122.6 0.1 fusion.5.forcing
  122.7 0.8 collective-permute-done.23.other_last
  123.5 1.4 %merge.1 = f32[2,64,768]{2,1,0:T(8,128)} custom-call(s32[5]{0:T(128)S(1)} %stack.19.scalars, bf16[64,768]{1,0:T(8,128)(2,1)S(1)} %get-tuple-element.54.own, bf16[64,768]{1,0:T(8,128)(2,1)S(1)} %collective-permute-done.17.other, bf16[64,768]{1,0:T(8,128)(2,1)S(1)} %collective-permute-done.18.near0, bf16[64,768]{1,0:T(8,128)(2,1)S(1)} %collective-permute-done.19.near1, ...), custom_call_target="tpu_custom_call" | custom-call | tf_op jit(solution)/shard_map/merge/pallas_call | solution.py:273
  (41 shorter events, 0.4 us)
Async XLA Ops:
  0.0 0.7 copy-start.8
  0.8 1.1 copy-start.4
  0.8 1.1 copy-start.6
  2.0 0.7 copy-start.5
  2.8 4.9 %copy-start.1 = (bf16[1,768,384]{2,1,0:T(8,128)(2,1)S(1)}, bf16[1,768,384]{2,1,0:T(8,128)(2,1)}, u32[]{:S(2)}) copy-start(bf16[1,768,384]{2,1,0:T(8,128)(2,1)} %param.15) | copy-start | bytes 1769476
  2.8 4.9 %copy-start.2 = (bf16[1,768,384]{2,1,0:T(8,128)(2,1)S(1)}, bf16[1,768,384]{2,1,0:T(8,128)(2,1)}, u32[]{:S(2)}) copy-start(bf16[1,768,384]{2,1,0:T(8,128)(2,1)} %param.16) | copy-start | bytes 1769476
  3.7 4.0 %copy-start = (bf16[1,768,384]{2,1,0:T(8,128)(2,1)S(1)}, bf16[1,768,384]{2,1,0:T(8,128)(2,1)}, u32[]{:S(2)}) copy-start(bf16[1,768,384]{2,1,0:T(8,128)(2,1)} %param.14) | copy-start | bytes 1769476
  3.7 3.9 %collective-permute-start = (bf16[3,64,768]{2,1,0:T(8,128)(2,1)}, bf16[3,64,768]{2,1,0:T(8,128)(2,1)S(1)}, u32[]{:S(2)}, u32[]{:S(2)}) collective-permute-start(bf16[3,64,768]{2,1,0:T(8,128)(2,1)} %get-tuple-element.67), channel_id=1, source_target_pairs={{11,17},{23,29},{35,41},{47,53},{59,65},{71,77},{83,89},{95,101},{... | collective-permute-start | bytes 884744 | tf_op jit(solution)/shard_map/first_states/ppermute | solution.py:325
  4.5 3.1 %collective-permute-start.1 = (bf16[3,64,768]{2,1,0:T(8,128)(2,1)}, bf16[3,64,768]{2,1,0:T(8,128)(2,1)S(1)}, u32[]{:S(2)}, u32[]{:S(2)}) collective-permute-start(bf16[3,64,768]{2,1,0:T(8,128)(2,1)} %get-tuple-element.66), channel_id=1, source_target_pairs={{11,23},{23,35},{35,47},{47,59},{59,71},{71,83},{83,95},{95,107},{... | collective-permute-start | bytes 884744 | tf_op jit(solution)/shard_map/first_states/ppermute | solution.py:325
  5.2 2.5 %collective-permute-start.2 = (bf16[3,64,768]{2,1,0:T(8,128)(2,1)}, bf16[3,64,768]{2,1,0:T(8,128)(2,1)S(1)}, u32[]{:S(2)}, u32[]{:S(2)}) collective-permute-start(bf16[3,64,768]{2,1,0:T(8,128)(2,1)} %get-tuple-element.65), channel_id=1, source_target_pairs={{5,11},{11,5},{17,23},{23,17},{29,35},{35,29},{41,47},{47,41},{53,... | collective-permute-start | bytes 884744 | tf_op jit(solution)/shard_map/first_states/ppermute | solution.py:325
  7.7 1.1 copy-start.3
  9.4 17.0 %collective-permute-start.3 = (bf16[2,64,768]{2,1,0:T(8,128)(2,1)S(1)}, bf16[2,64,768]{2,1,0:T(8,128)(2,1)S(1)}, u32[]{:S(2)}, u32[]{:S(2)}) collective-permute-start(bf16[2,64,768]{2,1,0:T(8,128)(2,1)S(1)} %get-tuple-element.70), channel_id=1, source_target_pairs={{0,6},{1,7},{2,8},{3,9},{4,10},{6,0},{7,1},{8,2},{9,3},{10,4},{12,... | collective-permute-start | bytes 589832 | tf_op jit(solution)/shard_map/later_states/ppermute | solution.py:325
  21.8 30.9 %collective-permute-start.5 = (bf16[128,768]{1,0:T(8,128)(2,1)S(1)}, bf16[128,768]{1,0:T(8,128)(2,1)S(1)}, u32[]{:S(2)}, u32[]{:S(2)}) collective-permute-start(bf16[128,768]{1,0:T(8,128)(2,1)S(1)} %first_step.1.refs_0_), channel_id=1, source_target_pairs={{5,4},{11,10},{17,16},{23,22},{29,28},{35,34},{41,40},{47,46},{53,... | collective-permute-start | bytes 589832 | tf_op jit(solution)/shard_map/pass_on/ppermute | solution.py:325
  22.5 30.2 %collective-permute-start.6 = (bf16[128,768]{1,0:T(8,128)(2,1)S(1)}, bf16[128,768]{1,0:T(8,128)(2,1)S(1)}, u32[]{:S(2)}, u32[]{:S(2)}) collective-permute-start(bf16[128,768]{1,0:T(8,128)(2,1)S(1)} %first_step.1.refs_0_), channel_id=1, source_target_pairs={{17,4},{23,10},{29,16},{35,22},{41,28},{47,34},{53,40},{59,46},{65... | collective-permute-start | bytes 589832 | tf_op jit(solution)/shard_map/pass_on/ppermute | solution.py:325
  23.2 4.6 %collective-permute-start.7 = (bf16[2,64,768]{2,1,0:T(8,128)(2,1)S(1)}, bf16[2,64,768]{2,1,0:T(8,128)(2,1)S(1)}, u32[]{:S(2)}, u32[]{:S(2)}) collective-permute-start(bf16[2,64,768]{2,1,0:T(8,128)(2,1)S(1)} %get-tuple-element.69), channel_id=1, source_target_pairs={{6,12},{7,13},{9,15},{18,24},{19,25},{21,27},{30,36},{31,37},{33,3... | collective-permute-start | bytes 589832 | tf_op jit(solution)/shard_map/later_states/ppermute | solution.py:325
  24.5 17.6 %collective-permute-start.8 = (bf16[2,64,768]{2,1,0:T(8,128)(2,1)S(1)}, bf16[2,64,768]{2,1,0:T(8,128)(2,1)S(1)}, u32[]{:S(2)}, u32[]{:S(2)}) collective-permute-start(bf16[2,64,768]{2,1,0:T(8,128)(2,1)S(1)} %get-tuple-element.68), channel_id=1, source_target_pairs={{6,18},{7,19},{9,21},{18,30},{19,31},{21,33},{30,42},{31,43},{33,4... | collective-permute-start | bytes 589832 | tf_op jit(solution)/shard_map/later_states/ppermute | solution.py:325
  26.5 24.0 %collective-permute-start.10 = (bf16[1,64,768]{2,1,0:T(8,128)(2,1)S(1)}, bf16[1,64,768]{2,1,0:T(8,128)(2,1)S(1)}, u32[]{:S(2)}, u32[]{:S(2)}) collective-permute-start(bf16[1,64,768]{2,1,0:T(8,128)(2,1)S(1)} %get-tuple-element.71), channel_id=1, source_target_pairs={{12,6},{24,18},{36,30},{48,42},{60,54},{72,66},{84,78},{96,90},{10... | collective-permute-start | bytes 294920 | tf_op jit(solution)/shard_map/window_above/ppermute | solution.py:325
  27.8 22.7 %collective-permute-start.9 = (bf16[1,64,768]{2,1,0:T(8,128)(2,1)S(1)}, bf16[1,64,768]{2,1,0:T(8,128)(2,1)S(1)}, u32[]{:S(2)}, u32[]{:S(2)}) collective-permute-start(bf16[1,64,768]{2,1,0:T(8,128)(2,1)S(1)} %get-tuple-element.72), channel_id=1, source_target_pairs={{12,0},{24,12},{36,24},{48,36},{60,48},{72,60},{84,72},{96,84},{10... | collective-permute-start | bytes 294920 | tf_op jit(solution)/shard_map/window_above/ppermute | solution.py:325
  42.1 6.5 %collective-permute-start.4 = (s32[1]{0:T(128)}, s32[1]{0:T(128)}, u32[]{:S(2)}, u32[]{:S(2)}) collective-permute-start(s32[1]{0:T(128)} %param.12), channel_id=1, source_target_pairs={{1,0},{2,1},{3,2},{4,3},{5,4},{7,6},{8,7},{9,8},{10,9},{11,10},{13... | collective-permute-start | bytes 20 | tf_op jit(solution)/shard_map/shifts/ppermute | solution.py:380
  55.1 1.4 %collective-permute-start.11 = (bf16[128,768]{1,0:T(8,128)(2,1)S(1)}, bf16[128,768]{1,0:T(8,128)(2,1)S(1)}, u32[]{:S(2)}, u32[]{:S(2)}) collective-permute-start(bf16[128,768]{1,0:T(8,128)(2,1)S(1)} %step.4.refs_1_), channel_id=1, source_target_pairs={{760,3},{766,9},{4,15},{10,21},{16,27},{22,33},{28,39},{34,45},{40... | collective-permute-start | bytes 589832 | tf_op jit(solution)/shard_map/pass_on/ppermute | solution.py:325
  55.8 0.7 collective-permute-start.12
  58.9 1.4 %collective-permute-start.13 = (bf16[128,768]{1,0:T(8,128)(2,1)S(1)}, bf16[128,768]{1,0:T(8,128)(2,1)S(1)}, u32[]{:S(2)}, u32[]{:S(2)}) collective-permute-start(bf16[128,768]{1,0:T(8,128)(2,1)S(1)} %step.5.refs_2_), channel_id=1, source_target_pairs={{3,2},{9,8},{15,14},{21,20},{27,26},{33,32},{39,38},{45,44},{51,50... | collective-permute-start | bytes 589832 | tf_op jit(solution)/shard_map/pass_on/ppermute | solution.py:325
  59.5 0.7 collective-permute-start.14
  62.6 1.5 %collective-permute-start.15 = (bf16[128,768]{1,0:T(8,128)(2,1)S(1)}, bf16[128,768]{1,0:T(8,128)(2,1)S(1)}, u32[]{:S(2)}, u32[]{:S(2)}) collective-permute-start(bf16[128,768]{1,0:T(8,128)(2,1)S(1)} %step.6.refs_3_), channel_id=1, source_target_pairs={{758,1},{764,7},{2,13},{8,19},{14,25},{20,31},{26,37},{32,43},{38,... | collective-permute-start | bytes 589832 | tf_op jit(solution)/shard_map/pass_on/ppermute | solution.py:325
  63.3 0.9 collective-permute-start.16
  66.6 49.3 %collective-permute-start.21 = (bf16[128,768]{1,0:T(8,128)(2,1)S(1)}, bf16[128,768]{1,0:T(8,128)(2,1)S(1)}, u32[]{:S(2)}, u32[]{:S(2)}) collective-permute-start(bf16[128,768]{1,0:T(8,128)(2,1)S(1)} %get-tuple-element.53.refs_4_), channel_id=1, source_target_pairs={{1,0},{7,6},{13,12},{19,18},{25,24},{31,30},{37,36},{43,42},{49,48... | collective-permute-start | bytes 589832 | tf_op jit(solution)/shard_map/pass_on/ppermute | solution.py:325
  67.9 48.0 %collective-permute-start.22 = (bf16[128,768]{1,0:T(8,128)(2,1)S(1)}, bf16[128,768]{1,0:T(8,128)(2,1)S(1)}, u32[]{:S(2)}, u32[]{:S(2)}) collective-permute-start(bf16[128,768]{1,0:T(8,128)(2,1)S(1)} %get-tuple-element.53.refs_4_), channel_id=1, source_target_pairs={{13,0},{19,6},{25,12},{31,18},{37,24},{43,30},{49,36},{55,42},{61,... | collective-permute-start | bytes 589832 | tf_op jit(solution)/shard_map/pass_on/ppermute | solution.py:325
  69.2 46.0 %collective-permute-start.20 = (bf16[64,768]{1,0:T(8,128)(2,1)S(1)}, bf16[64,768]{1,0:T(8,128)(2,1)S(1)}, u32[]{:S(2)}, u32[]{:S(2)}) collective-permute-start(bf16[64,768]{1,0:T(8,128)(2,1)S(1)} %get-tuple-element.57), channel_id=1, source_target_pairs={{757,0},{763,6},{1,12},{7,18},{13,24},{19,30},{25,36},{31,42},{37,... | collective-permute-start | bytes 294920 | tf_op jit(solution)/shard_map/pass_on/ppermute | solution.py:325
  71.2 51.5 %collective-permute-start.18 = (bf16[64,768]{1,0:T(8,128)(2,1)S(1)}, bf16[64,768]{1,0:T(8,128)(2,1)S(1)}, u32[]{:S(2)}, u32[]{:S(2)}) collective-permute-start(bf16[64,768]{1,0:T(8,128)(2,1)S(1)} %get-tuple-element.56), channel_id=1, source_target_pairs={{13,7},{15,9},{17,11},{25,19},{27,21},{29,23},{37,31},{39,33},{41,... | collective-permute-start | bytes 294920 | tf_op jit(solution)/shard_map/earlier_results/ppermute | solution.py:325
  71.8 50.9 %collective-permute-start.19 = (bf16[64,768]{1,0:T(8,128)(2,1)S(1)}, bf16[64,768]{1,0:T(8,128)(2,1)S(1)}, u32[]{:S(2)}, u32[]{:S(2)}) collective-permute-start(bf16[64,768]{1,0:T(8,128)(2,1)S(1)} %get-tuple-element.56), channel_id=1, source_target_pairs={{19,7},{21,9},{23,11},{31,19},{33,21},{35,23},{43,31},{45,33},{47,... | collective-permute-start | bytes 294920 | tf_op jit(solution)/shard_map/earlier_results/ppermute | solution.py:325
  115.3 7.4 %collective-permute-start.17 = (bf16[64,768]{1,0:T(8,128)(2,1)S(1)}, bf16[64,768]{1,0:T(8,128)(2,1)S(1)}, u32[]{:S(2)}, u32[]{:S(2)}) collective-permute-start(bf16[64,768]{1,0:T(8,128)(2,1)S(1)} %get-tuple-element.55), channel_id=1, source_target_pairs={{1,7},{2,8},{3,9},{4,10},{5,11},{7,1},{8,2},{9,3},{10,4},{11,5},{1... | collective-permute-start | bytes 294920 | tf_op jit(solution)/shard_map/earlier_results/ppermute | solution.py:325
  115.9 6.6 %copy-start.7 = (bf16[1,2,8,8,768]{4,3,2,1,0:T(8,128)(2,1)S(1)}, bf16[1,2,8,8,768]{4,3,2,1,0:T(8,128)(2,1)}, u32[]{:S(2)}) copy-start(bf16[1,2,8,8,768]{4,3,2,1,0:T(8,128)(2,1)} %param.10) | copy-start | bytes 589828
  119.3 4.2 %collective-permute-start.23 = (bf16[64,768]{1,0:T(8,128)(2,1)S(1)}, bf16[64,768]{1,0:T(8,128)(2,1)S(1)}, u32[]{:S(2)}, u32[]{:S(2)}) collective-permute-start(bf16[64,768]{1,0:T(8,128)(2,1)S(1)} %get-tuple-element.64), channel_id=1, source_target_pairs={{0,6},{6,0},{12,18},{18,12},{24,30},{30,24},{36,42},{42,36},{48,54... | collective-permute-start | bytes 294920 | tf_op jit(solution)/shard_map/last_result/ppermute | solution.py:325
